TPU v7x, 128 devices: a whole 4x4x4 slice. The times are simulated.
128 devices in a mesh: slab: 16 (over z, y), pair: 8 (over x, core).
Axes of the slice: x: 4, y: 4, z: 4, core: 2. Of those that a mesh axis runs over, the one named last changes fastest.
Arguments:
- amplitudes: bfloat16 [512, 8, 128, 192], P(('pair', 'slab')), may hold values from -6 to 6
- integrals: bfloat16 [128, 8, 192, 6144], P('slab', None, None, 'pair'), may hold values from -0.046875 to 0.046875
- vir_counts: int32 [8], replicated, may hold values from 1 to 192, 1200 in all
- c_orbitals: int32 [128], replicated, may hold values from 0 to 1199
- a_orbitals: int32 [32], replicated, may hold values from 0 to 1199
Outputs:
- residual: float32 [512, 8, 6144], P(('pair', 'slab'))
Inputs may be any that keep to these rules, and one draw needn't show every extreme that they name: Virtual orbitals are numbered irrep by irrep, vir_counts[g] of irrep g; the counts sum to 1200 and the largest is 192.
All inputs are finite; a program needn't handle non-finite values.
Results may differ from a plain program's by a relative error of at most 0.0003.
Values may be sent and summed in bfloat16 or wider, within the bound.
No kernel may reach another device: no remote copies, remote signals or barrier semaphores. Data moves between devices by JAX's collectives and lax.ppermute only.
A program may use at most 192 MiB of HBM per device.

v0:
```python
import jax
import jax.numpy as jnp
from jax import lax
from jax.sharding import PartitionSpec as P


def irrep_of(orbitals, vir_counts):
    ends = jnp.cumsum(vir_counts, dtype=jnp.int32)
    return jnp.sum((orbitals[:, None] >= ends[None, :]).astype(jnp.int32), axis=1, dtype=jnp.int32)


def limits(labels_of, vir_counts):
    labels = jnp.arange(vir_counts.shape[0], dtype=jnp.int32)
    blocks = jnp.bitwise_xor(labels[:, None], labels_of[None, :])
    picked = jnp.where(blocks[:, :, None] == labels[None, None, :], vir_counts[None, None, :], 0)
    return jnp.sum(picked, axis=2, dtype=jnp.int32)


def shards(amplitudes, integrals, vir_counts, c_orbitals, a_orbitals):
    irreps = vir_counts.shape[0]
    dmax = amplitudes.shape[3]
    slots = jnp.arange(dmax, dtype=jnp.int32)
    c_irrep = irrep_of(c_orbitals, vir_counts)
    a_irrep = irrep_of(a_orbitals, vir_counts)
    keep = slots[None, None, :] < limits(c_irrep, vir_counts)[:, :, None]
    kept = jnp.where(keep[None], amplitudes, jnp.zeros((), amplitudes.dtype))
    relaid = lax.all_to_all(kept, "slab", split_axis=2, concat_axis=0, tiled=True)
    n_slab = lax.axis_size("slab")
    c_dev = relaid.shape[2]
    own_irrep = lax.dynamic_slice_in_dim(c_irrep, lax.axis_index("slab") * c_dev, c_dev, 0)
    labels = jnp.arange(irreps, dtype=jnp.int32)
    blocks = jnp.bitwise_xor(labels[:, None], own_irrep[None, :])
    local = jnp.arange(c_dev, dtype=jnp.int32)
    a_columns = integrals.shape[3]
    weights = integrals[local[None, :], blocks].reshape(irreps, c_dev * dmax, a_columns)
    rows = relaid.shape[0] // n_slab
    stacked = relaid.reshape(n_slab, 1, rows, irreps, c_dev * dmax)
    gathered = lax.all_gather(stacked, "pair", axis=1, tiled=True)
    partial_sum = jnp.einsum(
        "xyrpk,pkn->xyrpn", gathered, weights, preferred_element_type=jnp.float32
    )
    summed = lax.psum_scatter(partial_sum, "slab", scatter_dimension=0, tiled=True)
    full = lax.all_to_all(summed, "pair", split_axis=1, concat_axis=4, tiled=True)
    a_win = a_orbitals.shape[0]
    allow = slots[None, None, :] < limits(a_irrep, vir_counts)[:, :, None]
    shaped = full.reshape(rows, irreps, a_win, dmax)
    result = jnp.where(allow[None], shaped, jnp.zeros((), jnp.float32))
    return result.reshape(rows, irreps, a_win * dmax)


def solution(mesh):
    in_specs = (P(("pair", "slab"), None, None, None), P("slab", None, None, "pair"), P(), P(), P())
    out_specs = P(("pair", "slab"), None, None)
    return jax.shard_map(shards, mesh=mesh, in_specs=in_specs, out_specs=out_specs, check_vma=False)
```

profile of v0, /device:TPU:0, one launch (start us, length us, event | category | flops | bytes accessed | tf_op | source)
XLA Modules:
  0.0 277.9 jit_solution(3245086138079088158)
XLA Ops:
  6.5 0.8 reduce-window.8
  7.4 0.7 convert_reduce_fusion
  8.1 0.7 select_reduce_fusion
  8.9 0.1 copy.16
  9.0 0.2 iota_compare_fusion
  9.2 3.3 %copy.17 = bf16[4,8,128,192]{3,1,0,2:T(8,128)(2,1)S(1)} copy(bf16[4,8,128,192]{2,3,1,0:T(8,128)(2,1)} %param.5) | data formatting | bytes 3145728 | tf_op args[0]
  12.5 0.2 broadcast_select_fusion
  12.7 36.3 %all_to_all.30 = bf16[4,8,128,192]{3,1,0,2:T(8,128)(2,1)S(1)} all-to-all(bf16[4,8,128,192]{3,1,0,2:T(8,128)(2,1)S(1)} %broadcast_select_fusion), channel_id=1, replica_groups=mesh['slab'=16,'pair'=8] {'slab'}, dimensions={2} | all-to-all | bytes 3145728 | tf_op jit(solution)/shard_map/all_to_all | solution.py:27
  49.0 1.2 copy.19
  50.2 2.8 reshape.130
  53.2 15.6 %gather_fusion = bf16[64,192,768]{2,1,0:T(8,128)(2,1)} fusion(bf16[8,8,192,768]{3,2,1,0:T(8,128)(2,1)} %param.6, s32[64]{0:T(128)S(1)} %reshape.132), kind=kCustom, calls=%fused_computation | custom fusion | bytes 37749248 | tf_op jit(solution)/shard_map/gather | solution.py:35
  68.8 49.1 %all-gather.2.cloned.1.call-done = bf16[16,8,4,8,1536]{4,0,2,1,3:T(8,128)(2,1)} async-done(((bf16[16,1,4,8,1536]{4,0,2,1,3:T(8,128)(2,1)}), bf16[16,8,4,8,1536]{4,0,2,1,3:T(8,128)(2,1)}) %all-gather.2.cloned.1.call-update) | async-done | bytes 12582928 | tf_op jit(solution)/shard_map/all_gather | solution.py:38
  117.9 19.5 %convolution_bitcast_fusion = f32[16,8,4,8,768]{4,0,2,1,3:T(8,128)} fusion(bf16[8,1536,768,1,1]{2,1,4,3,0:T(8,128)(2,1)} %bitcast.28, bf16[16,8,4,8,1536]{4,0,2,1,3:T(8,128)(2,1)} %all-gather.2.cloned.1.call-done), kind=kOutput, calls=%fused_computation.1 | convolution fusion | flops 9663676416 | bytes 44040192 | tf_op jit(solution)/shard_map/xyrpk,pkn->xyrpn/dot_general | solution.py:39
  137.4 16.4 %copy.20 = f32[16,8,4,8,768]{4,3,2,1,0:T(8,128)} copy(f32[16,8,4,8,768]{4,0,2,1,3:T(8,128)} %convolution_bitcast_fusion) | data formatting | bytes 25165824 | tf_op jit(solution)/shard_map/xyrpk,pkn->xyrpn/transpose | solution.py:39
  153.8 0.6 copy-done.1
  154.8 0.1 lt.61
  155.0 94.1 %reduce-scatter.4.cloned.1.call-done = f32[1,8,4,8,768]{4,3,2,1,0:T(8,128)} async-done(((f32[16,8,4,8,768]{4,3,2,1,0:T(8,128)}), f32[1,8,4,8,768]{4,3,2,1,0:T(8,128)}) %reduce-scatter.4.cloned.1.call-update) | async-done | bytes 786448
  249.1 2.8 %copy.21 = f32[1,8,4,8,768]{4,0,2,3,1:T(1,128)} copy(f32[1,8,4,8,768]{4,3,2,1,0:T(8,128)} %reduce-scatter.4.cloned.1.call-done) | data formatting | bytes 1572864 | tf_op jit(solution)/shard_map/reduce_scatter | solution.py:42
  251.9 4.2 %all-to-all-start.1 = ((f32[1,8,4,8,768]{4,0,2,3,1:T(1,128)}), f32[1,8,4,8,768]{4,0,2,3,1:T(1,128)S(1)}, u32[]{:S(2)}, u32[]{:S(2)}) async-start(f32[1,8,4,8,768]{4,0,2,3,1:T(1,128)} %copy.21), calls=%async_computation.1 | async-start | bytes 1572864 | tf_op jit(solution)/shard_map/all_to_all | solution.py:43
  256.2 13.1 %all-to-all-done.1 = f32[1,8,4,8,768]{4,0,2,3,1:T(1,128)S(1)} async-done(((f32[1,8,4,8,768]{4,0,2,3,1:T(1,128)}), f32[1,8,4,8,768]{4,0,2,3,1:T(1,128)S(1)}, u32[]{:S(2)}, u32[]{:S(2)}) %all-to-all-start.1) | async-done | bytes 786464 | tf_op jit(solution)/shard_map/all_to_all | solution.py:43
  269.3 0.2 copy.27
  269.5 0.5 copy.22
  270.0 0.1 reshape.131
  270.1 0.9 broadcast_select_fusion.1
  (22 shorter events, 0.7 us)
Async XLA Ops:
  6.5 111.3 %all-gather.2.cloned.1.call-start = ((), (), s32[]{:S(2)}) async-start(), calls=%async_computation.3 | async-start | bytes 14155776 | tf_op jit(solution)/shard_map/all_gather | solution.py:38
  7.4 0.8 copy-start.2
  53.0 196.1 %reduce-scatter.4.cloned.1.call-start = ((), (), s32[]{:S(2)}) async-start(), calls=%async_computation.4 | async-start | bytes 13369344
  153.8 0.7 copy-start.1
  153.8 0.7 copy-start.3
  153.8 0.8 copy-start
  251.9 17.4 %all-to-all-start.1 = ((f32[1,8,4,8,768]{4,0,2,3,1:T(1,128)}), f32[1,8,4,8,768]{4,0,2,3,1:T(1,128)S(1)}, u32[]{:S(2)}, u32[]{:S(2)}) async-start(f32[1,8,4,8,768]{4,0,2,3,1:T(1,128)} %copy.21), calls=%async_computation.1 | async-start | bytes 1572864 | tf_op jit(solution)/shard_map/all_to_all | solution.py:43
Sparse Core Ops, SparseCore 0:
  53.1 64.7 all-gather.1
  154.0 95.0 reduce-scatter.3
where the time goes:
time: 279 us; the launch traced here: 278 us
  waiting for transfers between devices  156 us (56%)
  local copies, waits for them, and re-layouts  44.1 us (16%)
  blocking collectives  36.3 us (13%)
  matrix products  19.5 us (7%)
  between operations  13.5 us (5%)
  starting transfers between devices  4.28 us (2%)
  other arithmetic  3.86 us (1%)
    unnamed x3, waiting for transfers between devices  94.1 us
    all_gather x1, waiting for transfers between devices, shards(): gathered = lax.all_gather(stacked, 'pair', axis=1, tiled=True)  49.1 us
    all_to_all x1, blocking collectives, shards(): lax.all_to_all(kept, 'slab', split_axis=2, concat_axis=0, tiled=True)  36.3 us
    dot_general x1, matrix products, shards(): jnp.einsum('xyrpk,pkn->xyrpn', gathered, weights, preferred_element_type=...  19.5 us
    transpose x1, local copies, waits for them, and re-layouts, shards(): jnp.einsum('xyrpk,pkn->xyrpn', gathered, weights, preferred_element_type=...  16.4 us
    gather x1, local copies, waits for them, and re-layouts, shards(): integrals[local[None, :], blocks].reshape(irreps, c_dev * dmax, a_columns)  15.6 us
    all_to_all x1, waiting for transfers between devices, shards(): lax.all_to_all(summed, 'pair', split_axis=1, concat_axis=4, tiled=True)  13.1 us
  transfers between devices with their start and end apart: 3, of which 3 were waited for; matrix products, arithmetic and copies ran while one was open for 6% of the time, Pallas kernels for 0%

commit v1 on v0

v1 whole, which is shorter than its diff:
```python
import functools

import jax
import jax.numpy as jnp
from jax import lax
from jax.experimental import pallas as pl
from jax.experimental.pallas import tpu as pltpu
from jax.sharding import PartitionSpec as P

CHUNKS = 2
TOP = 32766.0
FINE = 256.0
AXES = ("slab", "pair")


def irrep_of(orbitals, vir_counts):
    ends = jnp.cumsum(vir_counts, dtype=jnp.int32)
    return jnp.sum((orbitals[:, None] >= ends[None, :]).astype(jnp.int32), axis=1, dtype=jnp.int32)


def limits(labels_of, vir_counts):
    labels = jnp.arange(vir_counts.shape[0], dtype=jnp.int32)
    blocks = jnp.bitwise_xor(labels[:, None], labels_of[None, :])
    picked = jnp.where(blocks[:, :, None] == labels[None, None, :], vir_counts[None, None, :], 0)
    return jnp.sum(picked, axis=2, dtype=jnp.int32)


def moves(target):
    def place(z, y, x, core):
        return ((z % 4) * 4 + y % 4) * 8 + (x % 4) * 2 + core

    return [
        (place(z, y, x, core), place(*target(z, y, x, core)))
        for z in range(4) for y in range(4) for x in range(4) for core in range(2)
    ]


X_UP = moves(lambda z, y, x, core: (z, y, x + 1, core))
X_DOWN = moves(lambda z, y, x, core: (z, y, x - 1, core))
SWAP = moves(lambda z, y, x, core: (z, y, x, 1 - core))


def first(k):
    return moves(lambda z, y, x, core: (z, y + k, x, core) if core == 0 else (z + k, y, x, core))


def second(k):
    return moves(lambda z, y, x, core: (z + k, y, x, core) if core == 0 else (z, y + k, x, core))


def send(value, pairs):
    return lax.ppermute(value, AXES, pairs)


def matmul_kernel(m, irrep_ref, *refs):
    arrays, v_ref, own_ref = refs[:10], refs[10], refs[11]
    coded, (lhs, mix, codes, slots, sems) = refs[12:15], refs[15:]
    p = pl.program_id(0)
    rows = 16 * m
    c_dev, depth = slots.shape[1] // 192, 192

    def fetch(step, slot):
        return [
            pltpu.make_async_copy(
                v_ref.at[c, jnp.bitwise_xor(step, irrep_ref[c])],
                slots.at[slot, pl.ds(c * depth, depth)],
                sems.at[slot, c],
            )
            for c in range(c_dev)
        ]

    @pl.when(p == 0)
    def _():
        for copy in fetch(0, 0):
            copy.start()
        size = 128 * m
        r = lax.broadcasted_iota(jnp.int32, (size, size), 0)
        col = lax.broadcasted_iota(jnp.int32, (size, size), 1)
        pair = lax.rem(r, m)
        x_rel = lax.rem(lax.div(r, m), 4)
        other = lax.rem(lax.div(r, 4 * m), 2)
        d2 = lax.rem(lax.div(r, 8 * m), 4)
        d1 = lax.div(r, 32 * m)
        major = jnp.where(other == 0, d1, d2)
        minor = jnp.where(other == 0, d2, d1)
        source = other * (64 * m) + x_rel * (16 * m) + major * (4 * m) + minor * m + pair
        mix[...] = (source == col).astype(jnp.float32).astype(jnp.bfloat16)
        codes[...] = jnp.zeros_like(codes)

    @pl.when(p < 7)
    def _():
        for copy in fetch(p + 1, lax.rem(p + 1, 2)):
            copy.start()

    a0, a1, a3, ha, hb, o0, o1, o3, oa, ob = arrays
    low = p < 4
    for base, (r0, r1, r3, half_a, half_b) in ((0, (a0, a1, a3, ha, hb)), (4, (o0, o1, o3, oa, ob))):
        for at, ref in ((0, r0), (1, r1), (3, r3)):
            lhs[pl.ds((base + at) * rows, rows), :] = ref[...]

        @pl.when(low)
        def _():
            lhs[pl.ds((base + 2) * rows, rows), :] = half_a[...]

        @pl.when(jnp.logical_not(low))
        def _():
            lhs[pl.ds((base + 2) * rows, rows), :] = half_b[...]

    mixed = jnp.dot(mix[...], lhs[...], preferred_element_type=jnp.float32).astype(jnp.bfloat16)
    slot = lax.rem(p, 2)
    for copy in fetch(p, slot):
        copy.wait()
    product = jnp.dot(mixed, slots[slot], preferred_element_type=jnp.float32)
    piece = 32 * m
    columns = product.shape[1]
    at = pl.ds(pl.multiple_of(p * columns, 128), columns)
    own_ref[:, at] = product[:piece]
    lane = lax.broadcasted_iota(jnp.int32, (piece, 128), 1)
    for k in range(1, 4):
        part = product[k * piece:(k + 1) * piece]
        peak = jnp.maximum(jnp.max(jnp.abs(part), axis=1, keepdims=True), 2.0**-100)
        code = jnp.ceil(jnp.log2(peak) * FINE)
        coded[k - 1][:, at] = jnp.round(part * (jnp.exp2(code * (-1.0 / FINE)) * TOP)).astype(jnp.int16)
        codes[k - 1] = jnp.where(lane == p, code, codes[k - 1])

    @pl.when(p == 7)
    def _():
        for k in range(3):
            coded[k][:, pl.ds(8 * columns, 128)] = codes[k].astype(jnp.int16)


def matmul(arrays, integrals, irreps, m):
    rows, depth = 16 * m, arrays[0].shape[1]
    columns = integrals.shape[3]
    whole = pl.BlockSpec((rows, depth), lambda p, irr: (p, 0))
    low = pl.BlockSpec((rows, depth), lambda p, irr: (jnp.minimum(p, 3), 0))
    high = pl.BlockSpec((rows, depth), lambda p, irr: (jnp.maximum(p - 4, 0), 0))
    five = [whole, whole, whole, low, high]
    piece = 32 * m
    shapes = [jax.ShapeDtypeStruct((piece, 8 * columns), jnp.float32)]
    shapes += [jax.ShapeDtypeStruct((piece, 8 * columns + 128), jnp.int16)] * 3
    return pl.pallas_call(
        functools.partial(matmul_kernel, m),
        grid_spec=pltpu.PrefetchScalarGridSpec(
            num_scalar_prefetch=1,
            grid=(8,),
            in_specs=five + five + [pl.BlockSpec(memory_space=pl.ANY)],
            out_specs=[pl.BlockSpec(s.shape, lambda p, irr: (0, 0)) for s in shapes],
            scratch_shapes=[
                pltpu.VMEM((8 * rows, depth), jnp.bfloat16),
                pltpu.VMEM((8 * rows, 8 * rows), jnp.bfloat16),
                pltpu.VMEM((3, piece, 128), jnp.float32),
                pltpu.VMEM((2, depth, columns), jnp.bfloat16),
                pltpu.SemaphoreType.DMA((2, 8)),
            ],
        ),
        out_shape=shapes,
        compiler_params=pltpu.CompilerParams(vmem_limit_bytes=48 * 2**20),
        cost_estimate=pl.CostEstimate(
            flops=2 * 8 * 8 * rows * depth * columns, bytes_accessed=integrals.size * 2, transcendentals=0
        ),
    )(irreps, *arrays, integrals)


def sum_kernel(own, q1, q2, q3, s1, s2, s3, *outs):
    p = pl.program_id(0)
    total = own[...]
    lane = lax.broadcasted_iota(jnp.int32, s1.shape, 1)
    for q, s in ((q1, s1), (q2, s2), (q3, s3)):
        code = jnp.sum(jnp.where(lane == p, s[...].astype(jnp.float32), 0.0), axis=1, keepdims=True)
        total += q[...].astype(jnp.float32) * (jnp.exp2(code * (1.0 / FINE)) * (1.0 / TOP))
    each = total.shape[0] // 4
    for k in range(4):
        outs[k][...] = total[k * each:(k + 1) * each]


def sum_coded(own, parts):
    piece, width = own.shape
    columns = width // 8
    block = pl.BlockSpec((piece, columns), lambda p: (0, p))
    scale = pl.BlockSpec((piece, 128), lambda p: (0, width // 128))
    out = pl.BlockSpec((piece // 4, columns), lambda p: (0, p))
    return pl.pallas_call(
        sum_kernel,
        grid=(8,),
        in_specs=[block] * 4 + [scale] * 3,
        out_specs=[out] * 4,
        out_shape=[jax.ShapeDtypeStruct((piece // 4, width), jnp.float32)] * 4,
        cost_estimate=pl.CostEstimate(flops=8 * own.size, bytes_accessed=14 * own.size, transcendentals=0),
    )(own, *parts, *parts)


def shards(amplitudes, integrals, vir_counts, c_orbitals, a_orbitals):
    irreps = vir_counts.shape[0]
    dmax = amplitudes.shape[3]
    slots = jnp.arange(dmax, dtype=jnp.int32)
    c_irrep = irrep_of(c_orbitals, vir_counts)
    a_irrep = irrep_of(a_orbitals, vir_counts)
    keep = slots[None, None, :] < limits(c_irrep, vir_counts)[:, :, None]
    kept = jnp.where(keep[None], amplitudes, jnp.zeros((), amplitudes.dtype))
    n_slab = lax.axis_size("slab")
    c_dev = amplitudes.shape[2] // n_slab
    slab, pair = lax.axis_index("slab"), lax.axis_index("pair")
    z, y, x, core = slab // 4, slab % 4, pair // 2, pair % 2
    own_irrep = lax.dynamic_slice_in_dim(c_irrep, slab * c_dev, c_dev, 0)
    rows = amplitudes.shape[0]
    m = rows // CHUNKS
    depth = c_dev * dmax
    columns = integrals.shape[3]
    a_win = a_orbitals.shape[0]

    size = n_slab * m * irreps
    r = jnp.arange(size, dtype=jnp.int32)
    minor, d2, d1, label = r % m, r // m % 4, r // (4 * m) % 4, r // (16 * m)
    dy = jnp.where(core == 0, d1, d2)
    dz = jnp.where(core == 0, d2, d1)
    source = (((z + dz) % 4 * 4 + (y + dy) % 4) * m + minor) * irreps + label
    chooser = (source[:, None] == r[None, :]).astype(jnp.bfloat16)

    j = jnp.arange(8, dtype=jnp.int32)
    from_rel = ((j % 2) ^ core) * 4 + (j // 2 - x) % 4

    by_slab = kept.reshape(rows, irreps, n_slab, depth).transpose(2, 0, 1, 3)
    results = []
    for chunk in range(CHUNKS):
        piece = by_slab[:, chunk * m:(chunk + 1) * m]
        got = lax.all_to_all(piece, "slab", split_axis=0, concat_axis=0, tiled=True)
        a0 = jnp.dot(chooser, got.reshape(size, depth), preferred_element_type=jnp.float32).astype(jnp.bfloat16)
        a1, a3 = send(a0, X_DOWN), send(a0, X_UP)
        ha, hb = send(a1[:size // 2], X_DOWN), send(a3[size // 2:], X_UP)
        mine = [a0, a1, a3, ha, hb]
        theirs = [send(v, SWAP) for v in mine]
        own, q1, q2, q3 = matmul(mine + theirs, integrals, own_irrep, m)
        parts = [send(q, first(k)) for k, q in ((1, q1), (2, q2), (3, q3))]
        t0, t1, t2, t3 = sum_coded(own, parts)
        total = t0 + send(t1, second(1)) + send(t2, second(2)) + send(t3, second(3))
        blocks = total.reshape(8, m, irreps * columns)[from_rel]
        back = lax.all_to_all(blocks, "pair", split_axis=0, concat_axis=0, tiled=True)
        results.append(back.reshape(8, m, irreps, columns).transpose(1, 2, 0, 3).reshape(m, irreps, 8 * columns))
    full = jnp.concatenate(results, axis=0)
    allow = slots[None, None, :] < limits(a_irrep, vir_counts)[:, :, None]
    shaped = full.reshape(rows, irreps, a_win, dmax)
    result = jnp.where(allow[None], shaped, jnp.zeros((), jnp.float32))
    return result.reshape(rows, irreps, a_win * dmax)


def solution(mesh):
    in_specs = (P(("pair", "slab"), None, None, None), P("slab", None, None, "pair"), P(), P(), P())
    out_specs = P(("pair", "slab"), None, None)
    return jax.shard_map(shards, mesh=mesh, in_specs=in_specs, out_specs=out_specs, check_vma=False)
```

time: 279 us -> 223 us (0.80)
  waiting for transfers between devices: 156 us -> 78 us
  starting transfers between devices: 4.28 us -> 56.5 us
  Pallas kernels: 0 us -> 51.1 us
  blocking collectives: 36.3 us -> 0 us
  matrix products: 19.5 us -> 0.82 us
  local copies, waits for them, and re-layouts: 44.1 us -> 26.6 us
  between operations: 13.5 us -> 0.35 us
  other arithmetic: 3.86 us -> 7.85 us
    unnamed x3 -> x0, waiting for transfers between devices: 94.1 us -> none
    pallas_call x0 -> x4, Pallas kernels: none -> 51.1 us  [the longest x2 38.2 us: matmul(): pl.pallas_call(functools.partial(matmul_kernel, m), grid_spec=pltpu.Prefe...]
    all_gather x1 -> x0, waiting for transfers between devices: 49.1 us -> none  [shards(): gathered = lax.all_gather(stacked, 'pair', axis=1, tiled=True)]
    ppermute x0 -> x30, waiting for transfers between devices: none -> 41.6 us  [send(): return lax.ppermute(value, AXES, pairs)]
    ppermute x0 -> x30, starting transfers between devices: none -> 37.9 us  [send(): return lax.ppermute(value, AXES, pairs)]
    all_to_all x1 -> x0, blocking collectives: 36.3 us -> none  [shards(): lax.all_to_all(kept, 'slab', split_axis=2, concat_axis=0, tiled=True)]
    all_to_all x1 -> x4, waiting for transfers between devices: 13.1 us -> 36.4 us  [the longest x2 23.1 us: shards(): got = lax.all_to_all(piece, 'slab', split_axis=0, concat_axis=0, tiled=True)]
    dot_general x1 -> x2, matrix products: 19.5 us -> 0.82 us  [shards(): jnp.dot(chooser, got.reshape(size, depth), preferred_element_type=jnp.flo...]
  transfers between devices with their start and end apart: 3 -> 34, of which waited for: 3 -> 13; matrix products, arithmetic and copies ran while one was open for 6% -> 5% of each run, Pallas kernels for 0% -> 23%
where the time goes in v1:
time: 223 us; the launch traced here: 221 us
  waiting for transfers between devices  78 us (35%)
  starting transfers between devices  56.5 us (25%)
  Pallas kernels  51.1 us (23%)
  local copies, waits for them, and re-layouts  26.6 us (12%)
  other arithmetic  7.85 us (4%)
    ppermute x30, waiting for transfers between devices, send(): return lax.ppermute(value, AXES, pairs)  41.6 us
    pallas_call x2, Pallas kernels, matmul(): pl.pallas_call(functools.partial(matmul_kernel, m), grid_spec=pltpu.Prefe...  38.2 us
    ppermute x30, starting transfers between devices, send(): return lax.ppermute(value, AXES, pairs)  37.9 us
    all_to_all x2, waiting for transfers between devices, shards(): got = lax.all_to_all(piece, 'slab', split_axis=0, concat_axis=0, tiled=True)  23.1 us
    all_to_all x2, waiting for transfers between devices, shards(): lax.all_to_all(blocks, 'pair', split_axis=0, concat_axis=0, tiled=True)  13.3 us
    pallas_call x2, Pallas kernels, sum_coded(): pl.pallas_call(sum_kernel, grid=(8,), in_specs=[block] * 4 + [scale] * 3,...  13 us
    all_to_all x2, starting transfers between devices, shards(): got = lax.all_to_all(piece, 'slab', split_axis=0, concat_axis=0, tiled=True)  11.7 us
    unnamed x40, local copies, waits for them, and re-layouts  9.96 us
  transfers between devices with their start and end apart: 34, of which 13 were waited for; matrix products, arithmetic and copies ran while one was open for 5% of the time, Pallas kernels for 23%

profile of v1, /device:TPU:0, one launch (start us, length us, event | category | flops | bytes accessed | tf_op | source)
XLA Modules:
  0.0 221.3 jit_solution(3317893080330829286)
XLA Ops:
  2.4 2.8 %broadcast_select_fusion = bf16[4,8,128,192]{2,3,1,0:T(8,128)(2,1)} fusion(bf16[4,8,128,192]{2,3,1,0:T(8,128)(2,1)} %param.5, pred[8,128,192]{1,2,0:T(8,128)(4,1)S(1)} %iota_compare_fusion), kind=kLoop, calls=%fused_computation.4 | loop fusion | flops 786432 | bytes 3342336 | tf_op jit(solution)/shard_map/jit(_where)/select_n | solution.py:200
  13.6 8.1 %all-to-all-start = ((bf16[16,2,8,1536]{3,2,1,0:T(8,128)(2,1)}), bf16[16,2,8,1536]{3,2,1,0:T(8,128)(2,1)S(1)}, u32[]{:S(2)}, u32[]{:S(2)}) async-start(bf16[16,2,8,1536]{3,2,1,0:T(8,128)(2,1)} %copy.19), calls=%async_computation | async-start | bytes 1572864 | tf_op jit(solution)/shard_map/all_to_all | solution.py:227
  23.1 13.2 %all-to-all-done = bf16[16,2,8,1536]{3,2,1,0:T(8,128)(2,1)S(1)} async-done(((bf16[16,2,8,1536]{3,2,1,0:T(8,128)(2,1)}), bf16[16,2,8,1536]{3,2,1,0:T(8,128)(2,1)S(1)}, u32[]{:S(2)}, u32[]{:S(2)}) %all-to-all-start) | async-done | bytes 786464 | tf_op jit(solution)/shard_map/all_to_all | solution.py:227
  36.3 3.6 %all-to-all-start.2 = ((bf16[16,2,8,1536]{3,2,1,0:T(8,128)(2,1)}), bf16[16,2,8,1536]{3,2,1,0:T(8,128)(2,1)S(1)}, u32[]{:S(2)}, u32[]{:S(2)}) async-start(bf16[16,2,8,1536]{3,2,1,0:T(8,128)(2,1)} %copy.21), calls=%async_computation.2 | async-start | bytes 1572864 | tf_op jit(solution)/shard_map/all_to_all | solution.py:227
  43.2 10.0 %all-to-all-done.2 = bf16[16,2,8,1536]{3,2,1,0:T(8,128)(2,1)S(1)} async-done(((bf16[16,2,8,1536]{3,2,1,0:T(8,128)(2,1)}), bf16[16,2,8,1536]{3,2,1,0:T(8,128)(2,1)S(1)}, u32[]{:S(2)}, u32[]{:S(2)}) %all-to-all-start.2) | async-done | bytes 786464 | tf_op jit(solution)/shard_map/all_to_all | solution.py:227
  56.4 4.8 %collective-permute-done.refs_1_ = bf16[256,1536]{1,0:T(8,128)(2,1)} collective-permute-done((bf16[256,1536]{1,0:T(8,128)(2,1)S(1)}, bf16[256,1536]{1,0:T(8,128)(2,1)}, u32[]{:S(2)}, u32[]{:S(2)}) %collective-permute-start) | collective-permute-done | bytes 786464 | tf_op jit(solution)/shard_map/ppermute | solution.py:52
  62.2 3.9 %collective-permute-start.2 = (bf16[128,1536]{1,0:T(8,128)(2,1)S(1)}, bf16[128,1536]{1,0:T(8,128)(2,1)S(1)}, u32[]{:S(2)}, u32[]{:S(2)}) collective-permute-start(bf16[128,1536]{1,0:T(8,128)(2,1)S(1)} %slice.29), channel_id=1, source_target_pairs={{0,6},{1,7},{2,0},{3,1},{4,2},{5,3},{6,4},{7,5},{8,14},{9,15},{10,... | collective-permute-start | bytes 1179656 | tf_op jit(solution)/shard_map/ppermute | solution.py:52
  67.2 10.9 %collective-permute-done.15.refs_1_ = bf16[256,1536]{1,0:T(8,128)(2,1)S(1)} collective-permute-done((bf16[256,1536]{1,0:T(8,128)(2,1)S(1)}, bf16[256,1536]{1,0:T(8,128)(2,1)S(1)}, u32[]{:S(2)}, u32[]{:S(2)}) %collective-permute-start.15) | collective-permute-done | bytes 786464 | tf_op jit(solution)/shard_map/ppermute | solution.py:52
  78.1 3.8 %collective-permute-start.17 = (bf16[128,1536]{1,0:T(8,128)(2,1)S(1)}, bf16[128,1536]{1,0:T(8,128)(2,1)S(1)}, u32[]{:S(2)}, u32[]{:S(2)}) collective-permute-start(bf16[128,1536]{1,0:T(8,128)(2,1)S(1)} %slice.32), channel_id=1, source_target_pairs={{0,6},{1,7},{2,0},{3,1},{4,2},{5,3},{6,4},{7,5},{8,14},{9,15},{10,... | collective-permute-start | bytes 1179656 | tf_op jit(solution)/shard_map/ppermute | solution.py:52
  82.4 4.1 %collective-permute-done.2.refs_3_ = bf16[128,1536]{1,0:T(8,128)(2,1)S(1)} collective-permute-done((bf16[128,1536]{1,0:T(8,128)(2,1)S(1)}, bf16[128,1536]{1,0:T(8,128)(2,1)S(1)}, u32[]{:S(2)}, u32[]{:S(2)}) %collective-permute-start.2) | collective-permute-done | bytes 393248 | tf_op jit(solution)/shard_map/ppermute | solution.py:52
  88.9 3.4 %collective-permute-done.17.refs_3_ = bf16[128,1536]{1,0:T(8,128)(2,1)S(1)} collective-permute-done((bf16[128,1536]{1,0:T(8,128)(2,1)S(1)}, bf16[128,1536]{1,0:T(8,128)(2,1)S(1)}, u32[]{:S(2)}, u32[]{:S(2)}) %collective-permute-start.17) | collective-permute-done | bytes 393248 | tf_op jit(solution)/shard_map/ppermute | solution.py:52
  93.0 2.9 %collective-permute-done.18.refs_4_ = bf16[128,1536]{1,0:T(8,128)(2,1)S(1)} collective-permute-done((bf16[128,1536]{1,0:T(8,128)(2,1)S(1)}, bf16[128,1536]{1,0:T(8,128)(2,1)S(1)}, u32[]{:S(2)}, u32[]{:S(2)}) %collective-permute-start.18) | collective-permute-done | bytes 393248 | tf_op jit(solution)/shard_map/ppermute | solution.py:52
  103.8 19.1 %shard_map.55 = (f32[64,6144]{1,0:T(8,128)}, s16[64,6272]{1,0:T(8,128)(2,1)}, s16[64,6272]{1,0:T(8,128)(2,1)}, s16[64,6272]{1,0:T(8,128)(2,1)}) custom-call(s32[8]{0:T(128)S(1)} %dynamic_slice.3.irrep_ref, bf16[256,1536]{1,0:T(8,128)(2,1)S(1)} %convolution_convert_fusion.1.refs_0_, bf16[256,1536]{1,0:T(8,128)(2,1)} %collective-permute-done.refs_1_, ...), custom_call_target="tpu_custom_call" | custom-call | flops 4831838208 | bytes 18874368 | tf_op jit(solution)/shard_map/pallas_call | solution.py:142
  122.9 3.4 %collective-permute-start.10 = (s16[64,6272]{1,0:T(8,128)(2,1)}, s16[64,6272]{1,0:T(8,128)(2,1)S(1)}, u32[]{:S(2)}, u32[]{:S(2)}) collective-permute-start(s16[64,6272]{1,0:T(8,128)(2,1)} %get-tuple-element.23), channel_id=1, source_target_pairs={{0,16},{1,65},{2,18},{3,67},{4,20},{5,69},{6,22},{7,71},{8,24},{9,... | collective-permute-start | bytes 2408456 | tf_op jit(solution)/shard_map/ppermute | solution.py:52
  128.3 19.1 %shard_map.57 = (f32[64,6144]{1,0:T(8,128)}, s16[64,6272]{1,0:T(8,128)(2,1)}, s16[64,6272]{1,0:T(8,128)(2,1)}, s16[64,6272]{1,0:T(8,128)(2,1)}) custom-call(s32[8]{0:T(128)S(1)} %dynamic_slice.3.irrep_ref, bf16[256,1536]{1,0:T(8,128)(2,1)S(1)} %convolution_convert_fusion.refs_0_, bf16[256,1536]{1,0:T(8,128)(2,1)S(1)} %collective-permute-done.15.refs_1_, ...), custom_call_target="tpu_custom_call" | custom-call | flops 4831838208 | bytes 18874368 | tf_op jit(solution)/shard_map/pallas_call | solution.py:142
  148.1 3.3 %collective-permute-start.25 = (s16[64,6272]{1,0:T(8,128)(2,1)}, s16[64,6272]{1,0:T(8,128)(2,1)S(1)}, u32[]{:S(2)}, u32[]{:S(2)}) collective-permute-start(s16[64,6272]{1,0:T(8,128)(2,1)} %get-tuple-element.31), channel_id=1, source_target_pairs={{0,16},{1,65},{2,18},{3,67},{4,20},{5,69},{6,22},{7,71},{8,24},{9,... | collective-permute-start | bytes 2408456 | tf_op jit(solution)/shard_map/ppermute | solution.py:52
  152.3 6.5 %shard_map.56 = (f32[16,6144]{1,0:T(8,128)}, f32[16,6144]{1,0:T(8,128)}, f32[16,6144]{1,0:T(8,128)}, f32[16,6144]{1,0:T(8,128)}) custom-call(f32[64,6144]{1,0:T(8,128)} %get-tuple-element.21.own, s16[64,6272]{1,0:T(8,128)(2,1)} %collective-permute-done.9.q1.s1, s16[64,6272]{1,0:T(8,128)(2,1)} %copy-done.15, s16[64,6272]{1,0:T(8,128)(2,1)} %collective-permute-done.11.q3.s3, ...), custom_call_target="tpu_custom_call" | custom-call | flops 3145728 | bytes 5505024 | tf_op jit(solution)/shard_map/pallas_call | solution.py:183
  165.5 12.1 %collective-permute-done.25.q2.s2 = s16[64,6272]{1,0:T(8,128)(2,1)S(1)} collective-permute-done((s16[64,6272]{1,0:T(8,128)(2,1)}, s16[64,6272]{1,0:T(8,128)(2,1)S(1)}, u32[]{:S(2)}, u32[]{:S(2)}) %collective-permute-start.25) | collective-permute-done | bytes 802848 | tf_op jit(solution)/shard_map/ppermute | solution.py:52
  179.5 6.5 %shard_map.58 = (f32[16,6144]{1,0:T(8,128)}, f32[16,6144]{1,0:T(8,128)}, f32[16,6144]{1,0:T(8,128)}, f32[16,6144]{1,0:T(8,128)}) custom-call(f32[64,6144]{1,0:T(8,128)} %get-tuple-element.29.own, s16[64,6272]{1,0:T(8,128)(2,1)} %copy-done.12, s16[64,6272]{1,0:T(8,128)(2,1)} %copy-done.13, s16[64,6272]{1,0:T(8,128)(2,1)} %copy-done.14, ...), custom_call_target="tpu_custom_call" | custom-call | flops 3145728 | bytes 5505024 | tf_op jit(solution)/shard_map/pallas_call | solution.py:183
  187.2 3.4 %collective-permute-start.28 = (f32[16,6144]{1,0:T(8,128)}, f32[16,6144]{1,0:T(8,128)S(1)}, u32[]{:S(2)}, u32[]{:S(2)}) collective-permute-start(f32[16,6144]{1,0:T(8,128)} %get-tuple-element.35), channel_id=1, source_target_pairs={{0,64},{1,17},{2,66},{3,19},{4,68},{5,21},{6,70},{7,23},{8,72},{9,... | collective-permute-start | bytes 1179656 | tf_op jit(solution)/shard_map/ppermute | solution.py:52
  195.3 3.5 %all-to-all-start.1 = ((f32[8,2,6144]{2,1,0:T(2,128)}), f32[8,2,6144]{2,1,0:T(2,128)S(1)}, u32[]{:S(2)}, u32[]{:S(2)}) async-start(f32[8,2,6144]{2,1,0:T(2,128)} %gather_fusion), calls=%async_computation.1 | async-start | bytes 786432 | tf_op jit(solution)/shard_map/all_to_all | solution.py:238
  202.8 4.8 %all-to-all-done.1 = f32[8,2,6144]{2,1,0:T(2,128)S(1)} async-done(((f32[8,2,6144]{2,1,0:T(2,128)}), f32[8,2,6144]{2,1,0:T(2,128)S(1)}, u32[]{:S(2)}, u32[]{:S(2)}) %all-to-all-start.1) | async-done | bytes 393248 | tf_op jit(solution)/shard_map/all_to_all | solution.py:238
  207.6 3.5 %all-to-all-start.3 = ((f32[8,2,6144]{2,1,0:T(2,128)}), f32[8,2,6144]{2,1,0:T(2,128)S(1)}, u32[]{:S(2)}, u32[]{:S(2)}) async-start(f32[8,2,6144]{2,1,0:T(2,128)} %gather_fusion.1), calls=%async_computation.3 | async-start | bytes 786432 | tf_op jit(solution)/shard_map/all_to_all | solution.py:238
  211.5 8.5 %all-to-all-done.3 = f32[8,2,6144]{2,1,0:T(2,128)S(1)} async-done(((f32[8,2,6144]{2,1,0:T(2,128)}), f32[8,2,6144]{2,1,0:T(2,128)S(1)}, u32[]{:S(2)}, u32[]{:S(2)}) %all-to-all-start.3) | async-done | bytes 393248 | tf_op jit(solution)/shard_map/all_to_all | solution.py:238
  (128 shorter events, 56.1 us)
Async XLA Ops:
  13.6 22.6 %all-to-all-start = ((bf16[16,2,8,1536]{3,2,1,0:T(8,128)(2,1)}), bf16[16,2,8,1536]{3,2,1,0:T(8,128)(2,1)S(1)}, u32[]{:S(2)}, u32[]{:S(2)}) async-start(bf16[16,2,8,1536]{3,2,1,0:T(8,128)(2,1)} %copy.19), calls=%async_computation | async-start | bytes 1572864 | tf_op jit(solution)/shard_map/all_to_all | solution.py:227
  36.3 16.9 %all-to-all-start.2 = ((bf16[16,2,8,1536]{3,2,1,0:T(8,128)(2,1)}), bf16[16,2,8,1536]{3,2,1,0:T(8,128)(2,1)S(1)}, u32[]{:S(2)}, u32[]{:S(2)}) async-start(bf16[16,2,8,1536]{3,2,1,0:T(8,128)(2,1)} %copy.21), calls=%async_computation.2 | async-start | bytes 1572864 | tf_op jit(solution)/shard_map/all_to_all | solution.py:227
  40.4 20.8 %collective-permute-start = (bf16[256,1536]{1,0:T(8,128)(2,1)S(1)}, bf16[256,1536]{1,0:T(8,128)(2,1)}, u32[]{:S(2)}, u32[]{:S(2)}) collective-permute-start(bf16[256,1536]{1,0:T(8,128)(2,1)S(1)} %convolution_convert_fusion.1.refs_0_), channel_id=1, source_target_pairs={{0,6},{1,7},{2,0},{3,1},{4,2},{5,3},{6,4},{7,5},{8,14},{9,15},{10,... | collective-permute-start | bytes 2359304 | tf_op jit(solution)/shard_map/ppermute | solution.py:52
  43.2 22.9 %collective-permute-start.1 = (bf16[256,1536]{1,0:T(8,128)(2,1)S(1)}, bf16[256,1536]{1,0:T(8,128)(2,1)}, u32[]{:S(2)}, u32[]{:S(2)}) collective-permute-start(bf16[256,1536]{1,0:T(8,128)(2,1)S(1)} %convolution_convert_fusion.1.refs_0_), channel_id=1, source_target_pairs={{0,2},{1,3},{2,4},{3,5},{4,6},{5,7},{6,0},{7,1},{8,10},{9,11},{10,... | collective-permute-start | bytes 2359304 | tf_op jit(solution)/shard_map/ppermute | solution.py:52
  53.6 24.5 %collective-permute-start.15 = (bf16[256,1536]{1,0:T(8,128)(2,1)S(1)}, bf16[256,1536]{1,0:T(8,128)(2,1)S(1)}, u32[]{:S(2)}, u32[]{:S(2)}) collective-permute-start(bf16[256,1536]{1,0:T(8,128)(2,1)S(1)} %convolution_convert_fusion.refs_0_), channel_id=1, source_target_pairs={{0,6},{1,7},{2,0},{3,1},{4,2},{5,3},{6,4},{7,5},{8,14},{9,15},{10,... | collective-permute-start | bytes 2359304 | tf_op jit(solution)/shard_map/ppermute | solution.py:52
  56.4 25.4 %collective-permute-start.4 = (bf16[256,1536]{1,0:T(8,128)(2,1)S(1)}, bf16[256,1536]{1,0:T(8,128)(2,1)S(1)}, u32[]{:S(2)}, u32[]{:S(2)}) collective-permute-start(bf16[256,1536]{1,0:T(8,128)(2,1)S(1)} %convolution_convert_fusion.1.refs_0_), channel_id=1, source_target_pairs={{0,1},{1,0},{2,3},{3,2},{4,5},{5,4},{6,7},{7,6},{8,9},{9,8},{10,11... | collective-permute-start | bytes 2359304 | tf_op jit(solution)/shard_map/ppermute | solution.py:52
  56.4 25.5 %collective-permute-start.16 = (bf16[256,1536]{1,0:T(8,128)(2,1)S(1)}, bf16[256,1536]{1,0:T(8,128)(2,1)S(1)}, u32[]{:S(2)}, u32[]{:S(2)}) collective-permute-start(bf16[256,1536]{1,0:T(8,128)(2,1)S(1)} %convolution_convert_fusion.refs_0_), channel_id=1, source_target_pairs={{0,2},{1,3},{2,4},{3,5},{4,6},{5,7},{6,0},{7,1},{8,10},{9,11},{10,... | collective-permute-start | bytes 2359304 | tf_op jit(solution)/shard_map/ppermute | solution.py:52
  62.2 24.3 %collective-permute-start.2 = (bf16[128,1536]{1,0:T(8,128)(2,1)S(1)}, bf16[128,1536]{1,0:T(8,128)(2,1)S(1)}, u32[]{:S(2)}, u32[]{:S(2)}) collective-permute-start(bf16[128,1536]{1,0:T(8,128)(2,1)S(1)} %slice.29), channel_id=1, source_target_pairs={{0,6},{1,7},{2,0},{3,1},{4,2},{5,3},{6,4},{7,5},{8,14},{9,15},{10,... | collective-permute-start | bytes 1179656 | tf_op jit(solution)/shard_map/ppermute | solution.py:52
  67.1 21.0 %collective-permute-start.3 = (bf16[128,1536]{1,0:T(8,128)(2,1)S(1)}, bf16[128,1536]{1,0:T(8,128)(2,1)S(1)}, u32[]{:S(2)}, u32[]{:S(2)}) collective-permute-start(bf16[128,1536]{1,0:T(8,128)(2,1)S(1)} %slice.30), channel_id=1, source_target_pairs={{0,2},{1,3},{2,4},{3,5},{4,6},{5,7},{6,0},{7,1},{8,10},{9,11},{10,... | collective-permute-start | bytes 1179656 | tf_op jit(solution)/shard_map/ppermute | solution.py:52
  81.8 16.3 %collective-permute-start.5 = (bf16[256,1536]{1,0:T(8,128)(2,1)}, bf16[256,1536]{1,0:T(8,128)(2,1)}, u32[]{:S(2)}, u32[]{:S(2)}) collective-permute-start(bf16[256,1536]{1,0:T(8,128)(2,1)} %collective-permute-done.refs_1_), channel_id=1, source_target_pairs={{0,1},{1,0},{2,3},{3,2},{4,5},{5,4},{6,7},{7,6},{8,9},{9,8},{10,11... | collective-permute-start | bytes 2359304 | tf_op jit(solution)/shard_map/ppermute | solution.py:52
  81.9 16.7 %collective-permute-start.6 = (bf16[256,1536]{1,0:T(8,128)(2,1)}, bf16[256,1536]{1,0:T(8,128)(2,1)}, u32[]{:S(2)}, u32[]{:S(2)}) collective-permute-start(bf16[256,1536]{1,0:T(8,128)(2,1)} %collective-permute-done.1.refs_2_), channel_id=1, source_target_pairs={{0,1},{1,0},{2,3},{3,2},{4,5},{5,4},{6,7},{7,6},{8,9},{9,8},{10,11... | collective-permute-start | bytes 2359304 | tf_op jit(solution)/shard_map/ppermute | solution.py:52
  95.9 27.0 %collective-permute-start.19 = (bf16[256,1536]{1,0:T(8,128)(2,1)S(1)}, bf16[256,1536]{1,0:T(8,128)(2,1)}, u32[]{:S(2)}, u32[]{:S(2)}) collective-permute-start(bf16[256,1536]{1,0:T(8,128)(2,1)S(1)} %convolution_convert_fusion.refs_0_), channel_id=1, source_target_pairs={{0,1},{1,0},{2,3},{3,2},{4,5},{5,4},{6,7},{7,6},{8,9},{9,8},{10,11... | collective-permute-start | bytes 2359304 | tf_op jit(solution)/shard_map/ppermute | solution.py:52
  96.7 31.6 %collective-permute-start.20 = (bf16[256,1536]{1,0:T(8,128)(2,1)S(1)}, bf16[256,1536]{1,0:T(8,128)(2,1)}, u32[]{:S(2)}, u32[]{:S(2)}) collective-permute-start(bf16[256,1536]{1,0:T(8,128)(2,1)S(1)} %collective-permute-done.15.refs_1_), channel_id=1, source_target_pairs={{0,1},{1,0},{2,3},{3,2},{4,5},{5,4},{6,7},{7,6},{8,9},{9,8},{10,11... | collective-permute-start | bytes 2359304 | tf_op jit(solution)/shard_map/ppermute | solution.py:52
  98.0 30.3 %collective-permute-start.21 = (bf16[256,1536]{1,0:T(8,128)(2,1)S(1)}, bf16[256,1536]{1,0:T(8,128)(2,1)}, u32[]{:S(2)}, u32[]{:S(2)}) collective-permute-start(bf16[256,1536]{1,0:T(8,128)(2,1)S(1)} %collective-permute-done.16.refs_2_), channel_id=1, source_target_pairs={{0,1},{1,0},{2,3},{3,2},{4,5},{5,4},{6,7},{7,6},{8,9},{9,8},{10,11... | collective-permute-start | bytes 2359304 | tf_op jit(solution)/shard_map/ppermute | solution.py:52
  98.1 28.1 %collective-permute-start.22 = (bf16[128,1536]{1,0:T(8,128)(2,1)S(1)}, bf16[128,1536]{1,0:T(8,128)(2,1)S(1)}, u32[]{:S(2)}, u32[]{:S(2)}) collective-permute-start(bf16[128,1536]{1,0:T(8,128)(2,1)S(1)} %collective-permute-done.17.refs_3_), channel_id=1, source_target_pairs={{0,1},{1,0},{2,3},{3,2},{4,5},{5,4},{6,7},{7,6},{8,9},{9,8},{10,11... | collective-permute-start | bytes 1179656 | tf_op jit(solution)/shard_map/ppermute | solution.py:52
  98.6 28.9 %collective-permute-start.23 = (bf16[128,1536]{1,0:T(8,128)(2,1)}, bf16[128,1536]{1,0:T(8,128)(2,1)S(1)}, u32[]{:S(2)}, u32[]{:S(2)}) collective-permute-start(bf16[128,1536]{1,0:T(8,128)(2,1)} %copy-done.2), channel_id=1, source_target_pairs={{0,1},{1,0},{2,3},{3,2},{4,5},{5,4},{6,7},{7,6},{8,9},{9,8},{10,11... | collective-permute-start | bytes 1179656 | tf_op jit(solution)/shard_map/ppermute | solution.py:52
  122.9 28.4 %collective-permute-start.10 = (s16[64,6272]{1,0:T(8,128)(2,1)}, s16[64,6272]{1,0:T(8,128)(2,1)S(1)}, u32[]{:S(2)}, u32[]{:S(2)}) collective-permute-start(s16[64,6272]{1,0:T(8,128)(2,1)} %get-tuple-element.23), channel_id=1, source_target_pairs={{0,16},{1,65},{2,18},{3,67},{4,20},{5,69},{6,22},{7,71},{8,24},{9,... | collective-permute-start | bytes 2408456 | tf_op jit(solution)/shard_map/ppermute | solution.py:52
  126.3 26.0 %collective-permute-start.11 = (s16[64,6272]{1,0:T(8,128)(2,1)}, s16[64,6272]{1,0:T(8,128)(2,1)}, u32[]{:S(2)}, u32[]{:S(2)}) collective-permute-start(s16[64,6272]{1,0:T(8,128)(2,1)} %get-tuple-element.24), channel_id=1, source_target_pairs={{0,24},{1,97},{2,26},{3,99},{4,28},{5,101},{6,30},{7,103},{8,0},{9... | collective-permute-start | bytes 2408456 | tf_op jit(solution)/shard_map/ppermute | solution.py:52
  127.4 24.9 %collective-permute-start.9 = (s16[64,6272]{1,0:T(8,128)(2,1)}, s16[64,6272]{1,0:T(8,128)(2,1)}, u32[]{:S(2)}, u32[]{:S(2)}) collective-permute-start(s16[64,6272]{1,0:T(8,128)(2,1)} %get-tuple-element.22), channel_id=1, source_target_pairs={{0,8},{1,33},{2,10},{3,35},{4,12},{5,37},{6,14},{7,39},{8,16},{9,4... | collective-permute-start | bytes 2408456 | tf_op jit(solution)/shard_map/ppermute | solution.py:52
  148.1 29.6 %collective-permute-start.25 = (s16[64,6272]{1,0:T(8,128)(2,1)}, s16[64,6272]{1,0:T(8,128)(2,1)S(1)}, u32[]{:S(2)}, u32[]{:S(2)}) collective-permute-start(s16[64,6272]{1,0:T(8,128)(2,1)} %get-tuple-element.31), channel_id=1, source_target_pairs={{0,16},{1,65},{2,18},{3,67},{4,20},{5,69},{6,22},{7,71},{8,24},{9,... | collective-permute-start | bytes 2408456 | tf_op jit(solution)/shard_map/ppermute | solution.py:52
  152.2 26.4 %collective-permute-start.26 = (s16[64,6272]{1,0:T(8,128)(2,1)}, s16[64,6272]{1,0:T(8,128)(2,1)S(1)}, u32[]{:S(2)}, u32[]{:S(2)}) collective-permute-start(s16[64,6272]{1,0:T(8,128)(2,1)} %get-tuple-element.32), channel_id=1, source_target_pairs={{0,24},{1,97},{2,26},{3,99},{4,28},{5,101},{6,30},{7,103},{8,0},{9... | collective-permute-start | bytes 2408456 | tf_op jit(solution)/shard_map/ppermute | solution.py:52
  158.8 31.8 %collective-permute-start.12 = (f32[16,6144]{1,0:T(8,128)}, f32[16,6144]{1,0:T(8,128)}, u32[]{:S(2)}, u32[]{:S(2)}) collective-permute-start(f32[16,6144]{1,0:T(8,128)} %get-tuple-element.26), channel_id=1, source_target_pairs={{0,32},{1,9},{2,34},{3,11},{4,36},{5,13},{6,38},{7,15},{8,40},{9,1... | collective-permute-start | bytes 1179656 | tf_op jit(solution)/shard_map/ppermute | solution.py:52
  160.4 31.7 %collective-permute-start.13 = (f32[16,6144]{1,0:T(8,128)}, f32[16,6144]{1,0:T(8,128)}, u32[]{:S(2)}, u32[]{:S(2)}) collective-permute-start(f32[16,6144]{1,0:T(8,128)} %get-tuple-element.27), channel_id=1, source_target_pairs={{0,64},{1,17},{2,66},{3,19},{4,68},{5,21},{6,70},{7,23},{8,72},{9,... | collective-permute-start | bytes 1179656 | tf_op jit(solution)/shard_map/ppermute | solution.py:52
  163.1 29.0 %collective-permute-start.14 = (f32[16,6144]{1,0:T(8,128)}, f32[16,6144]{1,0:T(8,128)}, u32[]{:S(2)}, u32[]{:S(2)}) collective-permute-start(f32[16,6144]{1,0:T(8,128)} %get-tuple-element.28), channel_id=1, source_target_pairs={{0,96},{1,25},{2,98},{3,27},{4,100},{5,29},{6,102},{7,31},{8,104},... | collective-permute-start | bytes 1179656 | tf_op jit(solution)/shard_map/ppermute | solution.py:52
  (30 other events, 238.4 us)

commit v2 on v0

v2 whole, which is shorter than its diff:
```python
import functools

import jax
import jax.numpy as jnp
from jax import lax
from jax.experimental import pallas as pl
from jax.experimental.pallas import tpu as pltpu
from jax.sharding import PartitionSpec as P

SPLIT = (4, 4)
TOP = 32766.0
FINE = 256.0
AXES = ("slab", "pair")
MIB = 2**20
LIMIT = 58
HBM = pl.BlockSpec(memory_space=pl.ANY)
VMEM = pl.BlockSpec(memory_space=pltpu.VMEM)
SMEM = pl.BlockSpec(memory_space=pltpu.SMEM)


def place(z, y, x, core):
    return ((z % 4) * 4 + y % 4) * 8 + (x % 4) * 2 + core


def moves(target):
    return [
        (place(z, y, x, core), place(*target(z, y, x, core)))
        for z in range(4) for y in range(4) for x in range(4) for core in range(2)
    ]


X_UP = moves(lambda z, y, x, core: (z, y, x + 1, core))
X_DOWN = moves(lambda z, y, x, core: (z, y, x - 1, core))
SWAP = moves(lambda z, y, x, core: (z, y, x, 1 - core))
GROUPS = [[place(z, y, x, 0) for x in range(4) for z in range(4)] for y in range(4)]
GROUPS += [[place(z, y, x, 1) for x in range(4) for y in range(4)] for z in range(4)]


def first(k):
    return moves(lambda z, y, x, core: (z, y + k, x, core) if core == 0 else (z + k, y, x, core))


def send(value, pairs):
    return lax.ppermute(value, AXES, pairs)


def cost(flops, size):
    return pl.CostEstimate(flops=flops, bytes_accessed=size, transcendentals=0)


def params(size):
    return pltpu.CompilerParams(vmem_limit_bytes=size * MIB)


def one_hot(rows, source):
    r = lax.broadcasted_iota(jnp.int32, (rows, rows), 0)
    col = lax.broadcasted_iota(jnp.int32, (rows, rows), 1)
    return (source(r) == col).astype(jnp.float32).astype(jnp.bfloat16)


def pick(matrix, value):
    return jnp.dot(matrix, value, preferred_element_type=jnp.float32)


def code_of(part):
    peak = jnp.maximum(jnp.max(jnp.abs(part), axis=1, keepdims=True), 2.0**-100)
    code = jnp.ceil(jnp.log2(peak) * FINE)
    return code, jnp.round(part * (jnp.exp2(code * (-1.0 / FINE)) * TOP))


def ends_of(counts):
    ends, total = [], 0
    for g in range(8):
        total = total + counts[g]
        ends.append(total)
    return ends


def arrange_kernel(start, counts, c_ref, t_ref, out, sorted_ref):
    pairs, count, dmax, c_tot = t_ref.shape
    n_slab = c_tot // 8
    rows = pairs * count
    ends = ends_of(counts)
    orbital = c_ref[...]
    irrep = sum((orbital >= ends[g]).astype(jnp.int32) for g in range(8))
    slot = lax.broadcasted_iota(jnp.int32, (dmax, c_tot), 0)
    by_c = one_hot(c_tot, lambda r: lax.rem(r, n_slab) * 8 + lax.div(r, n_slab))
    for p in range(count):
        block = jnp.bitwise_xor(irrep, start + p)
        limit = sum(jnp.where(block == g, counts[g], 0) for g in range(8))
        keep = slot < limit
        for pair in range(pairs):
            kept = jnp.where(keep, t_ref[pair, p].astype(jnp.float32), 0.0).astype(jnp.bfloat16)
            split = lax.dot_general(by_c, kept, (((1,), (1,)), ((), ())), preferred_element_type=jnp.float32)
            split = split.astype(jnp.bfloat16)
            q = pair * count + p
            for c in range(8):
                sorted_ref[c, q * n_slab:(q + 1) * n_slab] = split[c * n_slab:(c + 1) * n_slab]
    by_slab = one_hot(n_slab * rows, lambda r: lax.rem(r, rows) * n_slab + lax.div(r, rows))
    for i in range(4):
        both = [pick(by_slab, sorted_ref[2 * i + h]) for h in range(2)]
        out[:, i * 2 * dmax:(i + 1) * 2 * dmax] = jnp.concatenate(both, axis=1).astype(jnp.bfloat16)


def arrange(amplitudes, vir_counts, c_orbitals, start, count):
    rows, _, dmax, c_tot = amplitudes.shape
    size = c_tot // 8 * rows * count
    return pl.pallas_call(
        functools.partial(arrange_kernel, start),
        grid=(1,),
        in_specs=[
            SMEM,
            pl.BlockSpec((1, c_tot), lambda i: (0, 0)),
            pl.BlockSpec((rows, count, dmax, c_tot), lambda i: (0, start // count, 0, 0)),
        ],
        out_specs=pl.BlockSpec((size, 8 * dmax), lambda i: (0, 0)),
        out_shape=jax.ShapeDtypeStruct((size, 8 * dmax), jnp.bfloat16),
        scratch_shapes=[pltpu.VMEM((8, size, dmax), jnp.bfloat16)],
        compiler_params=params(LIMIT),
        cost_estimate=cost(2 * 10**9, 4 * 10**6),
    )(vir_counts, c_orbitals.reshape(1, c_tot), amplitudes)


def matmul_kernel(m, start, counts, c_orbitals, *refs):
    lows, highs, (v_own, v_other) = refs[:4], refs[4:8], refs[8:10]
    outs = refs[10:14]
    lhs, slots, even, odd, own, coded, codes, sems, v_sems, o_sems = refs[14:]
    number, _, rows, depth = lhs.shape
    c_dev, _, dmax, half = v_own.shape
    width = 2 * half
    split = lows[0].shape[0]
    slab, pair = lax.axis_index("slab"), lax.axis_index("pair")
    x, core = lax.div(pair, 2), lax.rem(pair, 2)
    me = jnp.where(core == 0, lax.rem(slab, 4), lax.div(slab, 4))
    ends = ends_of(counts)
    irreps = []
    for c in range(c_dev):
        orbital = c_orbitals[slab * c_dev + c]
        irreps.append(sum((orbital >= ends[g]).astype(jnp.int32) for g in range(8)))

    def fetch(p):
        return [
            pltpu.make_async_copy(
                ref.at[c, jnp.bitwise_xor(irreps[c], start + p)],
                slots.at[p % 3, side, pl.ds(c * dmax, dmax)],
                v_sems.at[p % 3, side, c],
            )
            for side, ref in ((0, v_own), (1, v_other)) for c in range(c_dev)
        ]

    def arrivals(refs, first_p, at):
        return [
            pltpu.make_async_copy(ref, lhs.at[pl.ds(first_p, ref.shape[0]), lax.rem(x + r, 4)], sems.at[at + r])
            for r, ref in enumerate(refs)
        ]

    low, high = arrivals(lows, 0, 0), arrivals(highs, split, 4)
    for copy in low + fetch(0) + high + fetch(1):
        copy.start()
    codes[...] = jnp.zeros_like(codes)
    lane = lax.broadcasted_iota(jnp.int32, (rows, 128), 1)
    started = []

    def finish(p, ref):
        at = slice(p * width, (p + 1) * width)
        for k in range(4):
            d1 = lax.rem(me + k, 4)
            part = jnp.concatenate([ref[4 * r + d1] for r in range(4)], axis=0)
            if k == 0:
                own[:, at] = part
                source = own.at[:, at]
            else:
                code, value = code_of(part)
                coded[k - 1, :, at] = value.astype(jnp.int16)
                codes[k - 1] = jnp.where(lane == p, code, codes[k - 1])
                source = coded.at[k - 1, :, at]
            started.append(pltpu.make_async_copy(source, outs[k].at[:, at], o_sems.at[p, k]))
            started[-1].start()

    products = (even, odd)
    for p in range(number):
        if p in (0, split):
            for copy in (high if p else low):
                copy.wait()
        if p + 2 < number:
            for copy in fetch(p + 2):
                copy.start()
        for copy in fetch(p):
            copy.wait()
        left = lhs[p].reshape(4 * rows, depth)
        for side, at in ((0, core), (1, 1 - core)):
            at = pl.ds(pl.multiple_of(at * half, 128), half)
            products[p % 2][:, :, at] = pick(left, slots[p % 3, side]).reshape(16, 4 * m, half)
        if p > 0:
            finish(p - 1, products[(p - 1) % 2])
    finish(number - 1, products[(number - 1) % 2])
    at = slice(number * width, number * width + 128)
    for k in range(1, 4):
        coded[k - 1, :, at] = codes[k - 1].astype(jnp.int16)
        started.append(pltpu.make_async_copy(coded.at[k - 1, :, at], outs[k].at[:, at], o_sems.at[number, k]))
        started[-1].start()
    for copy in started:
        copy.wait()


def matmul(lows, highs, v_own, v_other, vir_counts, c_orbitals, m, start):
    c_dev, _, dmax, half = v_own.shape
    rows, depth, width = 16 * m, c_dev * dmax, 2 * half
    arrays = [a.reshape(-1, rows, depth) for a in lows + highs]
    number = arrays[0].shape[0] + arrays[-1].shape[0]
    shapes = [jax.ShapeDtypeStruct((rows, number * width), jnp.float32)]
    shapes += [jax.ShapeDtypeStruct((rows, number * width + 128), jnp.int16)] * 3
    return pl.pallas_call(
        functools.partial(matmul_kernel, m, start),
        in_specs=[SMEM] * 2 + [HBM] * 10,
        out_specs=[HBM] * 4,
        out_shape=shapes,
        scratch_shapes=[
            pltpu.VMEM((number, 4, rows, depth), jnp.bfloat16),
            pltpu.VMEM((3, 2, depth, half), jnp.bfloat16),
            pltpu.VMEM((16, 4 * m, width), jnp.float32),
            pltpu.VMEM((16, 4 * m, width), jnp.float32),
            pltpu.VMEM((rows, number * width), jnp.float32),
            pltpu.VMEM((3, rows, number * width + 128), jnp.int16),
            pltpu.VMEM((3, rows, 128), jnp.float32),
            pltpu.SemaphoreType.DMA((8,)),
            pltpu.SemaphoreType.DMA((3, 2, 8)),
            pltpu.SemaphoreType.DMA((number + 1, 4)),
        ],
        compiler_params=params(LIMIT),
        cost_estimate=cost(2 * number * 4 * rows * depth * width, number * v_own.size // 2),
    )(vir_counts, c_orbitals, *arrays, v_own, v_other)


def sum_kernel(number, own, q1, q2, q3, out, high, low):
    rows = own.shape[0]
    width = own.shape[1] // number
    lane = lax.broadcasted_iota(jnp.int32, (rows, 128), 1)
    scales = []
    for q in (q1, q2, q3):
        scales.append(jnp.exp2(q[:, number * width:].astype(jnp.float32) * (1.0 / FINE)) * (1.0 / TOP))
    for p in range(number):
        at = slice(p * width, (p + 1) * width)
        total = own[:, at]
        for q, scale in zip((q1, q2, q3), scales):
            one = jnp.sum(jnp.where(lane == p, scale, 0.0), axis=1, keepdims=True)
            total += q[:, at].astype(jnp.float32) * one
        code, value = code_of(total)
        value = jnp.concatenate([value, jnp.broadcast_to(code, (rows, 128))], axis=1)
        upper = jnp.round(value * (1.0 / 256.0))
        high[p * rows:(p + 1) * rows] = upper.astype(jnp.bfloat16)
        low[p * rows:(p + 1) * rows] = (value - 256.0 * upper).astype(jnp.bfloat16)
    order = one_hot(number * rows, lambda r: lax.rem(r, number) * rows + lax.div(r, number))
    out[...] = (pick(order, high[...]) * 256.0 + pick(order, low[...])).astype(jnp.int16)


def sum_coded(own, parts, number):
    rows, total = own.shape
    width = total // number + 128
    return pl.pallas_call(
        functools.partial(sum_kernel, number),
        in_specs=[VMEM] * 4,
        out_specs=VMEM,
        out_shape=jax.ShapeDtypeStruct((number * rows, width), jnp.int16),
        scratch_shapes=[pltpu.VMEM((number * rows, width), jnp.bfloat16)] * 2,
        compiler_params=params(LIMIT),
        cost_estimate=cost(8 * own.size, 12 * own.size),
    )(own, *parts)


def final_kernel(allow, *refs):
    got, out = refs[:-1], refs[-1]
    width = out.shape[1]
    pairs = out.shape[0] // 8
    start = 0
    for ref in got:
        number = ref.shape[0] // (4 * pairs)
        value = ref[...].astype(jnp.float32)
        scale = jnp.exp2(value[:, width:] * (1.0 / FINE)) * (1.0 / TOP)
        value = value[:, :width] * jnp.concatenate([scale] * (width // 128), axis=1)
        total = jnp.sum(value.reshape(4, pairs * number, width), axis=0)
        keep = allow[start:start + number] > 0.5
        for pair in range(pairs):
            part = total[pair * number:(pair + 1) * number]
            out[pair * 8 + start:pair * 8 + start + number] = jnp.where(keep, part, 0.0)
        start += number


def final(got, allow, pairs):
    width = got[0].shape[1] - 128
    return pl.pallas_call(
        final_kernel,
        grid=(4,),
        in_specs=[pl.BlockSpec((8, width), lambda i: (0, i))]
        + [pl.BlockSpec((g.shape[0] // 4, width + 128), lambda i: (i, 0)) for g in got],
        out_specs=pl.BlockSpec((8 * pairs, width), lambda i: (0, i)),
        out_shape=jax.ShapeDtypeStruct((8 * pairs, 4 * width), jnp.float32),
        compiler_params=params(LIMIT),
        cost_estimate=cost(10**7, 4 * 10**6),
    )(allow, *got)


def allowed(vir_counts, a_orbitals, dmax):
    labels = jnp.arange(8, dtype=jnp.int32)
    ends = jnp.sum(jnp.where(labels[:, None] <= labels[None, :], vir_counts[:, None], 0), axis=0)
    irrep = jnp.sum((a_orbitals[:, None] >= ends[None, :]).astype(jnp.int32), axis=1)
    block = jnp.bitwise_xor(labels[:, None], irrep[None, :])
    limit = jnp.sum(jnp.where(block[:, :, None] == labels, vir_counts, 0), axis=2)
    keep = jnp.arange(dmax, dtype=jnp.int32)[None, None, :] < limit[:, :, None]
    return keep.astype(jnp.float32).reshape(8, -1)


def shards(amplitudes, integrals, vir_counts, c_orbitals, a_orbitals):
    m, irreps, c_tot, dmax = amplitudes.shape
    depth = c_tot // 16 * dmax
    other = send(integrals, SWAP)
    core = lax.axis_index("pair") % 2
    by_s = jnp.swapaxes(amplitudes, 2, 3)
    starts = [sum(SPLIT[:i]) for i in range(len(SPLIT))]
    pieces = [arrange(by_s, vir_counts, c_orbitals, s, n) for s, n in zip(starts, SPLIT)]

    relaid = []
    for chunk, number in enumerate(SPLIT):
        size = 16 * m * number
        r = jnp.arange(size, dtype=jnp.int32)
        minor, d2, d1, label = r % m, r // m % 4, r // (4 * m) % 4, r // (16 * m)
        dy = jnp.where(core == 0, d1, d2)
        dz = jnp.where(core == 0, d2, d1)
        source = ((dz * 4 + dy) * m + minor) * number + label
        chooser = (source[:, None] == r[None, :]).astype(jnp.bfloat16)
        piece = pieces[chunk].reshape(16, m * number, depth)
        got = lax.all_to_all(piece, "slab", split_axis=0, concat_axis=0, tiled=True).reshape(size, depth)
        if chunk == 0:
            got, *pieces[1:] = lax.optimization_barrier((got, *pieces[1:]))
        cut = size // 2
        relaid.append([pick(part, got).astype(jnp.bfloat16) for part in (chooser[:cut], chooser[cut:])])

    products, before = [], None
    for chunk, (low, high) in enumerate(relaid):
        if before is not None:
            low, high, *_ = lax.optimization_barrier((low, high, *before))
        low1, high3 = send(low, X_DOWN), send(high, X_UP)
        high1, low3 = send(high, X_DOWN), send(low, X_UP)
        if products:
            low1, high3, _ = lax.optimization_barrier((low1, high3, products[-1][0]))
        low2, high2 = send(low1, X_DOWN), send(high3, X_UP)
        before = (low2, high2)
        arrays = [low, low1, low2, low3, high, high1, high2, high3]
        if chunk + 1 < len(SPLIT):
            arrays = lax.optimization_barrier((*arrays, *relaid[chunk + 1]))
            relaid[chunk + 1] = arrays[8:]
        products.append(matmul(
            list(arrays[:4]), list(arrays[4:8]), integrals, other, vir_counts, c_orbitals, m, starts[chunk]
        ))

    sent = [[send(q, first(k)) for k, q in enumerate(product) if k] for product in products]
    results = []
    for chunk, number in enumerate(SPLIT):
        own, parts = products[chunk][0], sent[chunk]
        if chunk + 1 < len(SPLIT):
            own, *parts = lax.optimization_barrier((own, *parts, products[chunk + 1][0]))[:4]
        coded = sum_coded(own, parts, number)
        coded = coded.reshape(16, m * number, coded.shape[1])
        got = lax.all_to_all(coded, AXES, split_axis=0, concat_axis=0, tiled=True, axis_index_groups=GROUPS)
        results.append(got.reshape(16 * m * number, got.shape[2]))
    full = final(results, allowed(vir_counts, a_orbitals, dmax), m)
    return full.reshape(m, irreps, full.shape[1])


def solution(mesh):
    in_specs = (P(("pair", "slab"), None, None, None), P("slab", None, None, "pair"), P(), P(), P())
    out_specs = P(("pair", "slab"), None, None)
    return jax.shard_map(shards, mesh=mesh, in_specs=in_specs, out_specs=out_specs, check_vma=False)
```

time: 279 us -> 160 us (0.57)
  waiting for transfers between devices: 156 us -> 54.5 us
  starting transfers between devices: 4.28 us -> 50.3 us
  Pallas kernels: 0 us -> 45.1 us
  local copies, waits for them, and re-layouts: 44.1 us -> 6.39 us
  blocking collectives: 36.3 us -> 0 us
  matrix products: 19.5 us -> 1.13 us
  between operations: 13.5 us -> 0.32 us
    unnamed x3 -> x0, waiting for transfers between devices: 94.1 us -> none
    all_gather x1 -> x0, waiting for transfers between devices: 49.1 us -> none  [shards(): gathered = lax.all_gather(stacked, 'pair', axis=1, tiled=True)]
    pallas_call x0 -> x7, Pallas kernels: none -> 45.1 us  [the longest x2 25.1 us: matmul(): pl.pallas_call(functools.partial(matmul_kernel, m, start), in_specs=[SMEM...]
    all_to_all x1 -> x0, blocking collectives: 36.3 us -> none  [shards(): lax.all_to_all(kept, 'slab', split_axis=2, concat_axis=0, tiled=True)]
    ppermute x0 -> x19, waiting for transfers between devices: none -> 31.7 us  [send(): return lax.ppermute(value, AXES, pairs)]
    ppermute x0 -> x19, starting transfers between devices: none -> 28.3 us  [send(): return lax.ppermute(value, AXES, pairs)]
    dot_general x1 -> x4, matrix products: 19.5 us -> 1.13 us  [pick(): return jnp.dot(matrix, value, preferred_element_type=jnp.float32)]
    all_to_all x1 -> x4, starting transfers between devices: 4.24 us -> 22 us  [the longest x2 11.7 us: shards(): lax.all_to_all(piece, 'slab', split_axis=0, concat_axis=0, tiled=True)]
  transfers between devices with their start and end apart: 3 -> 23, of which waited for: 3 -> 10; matrix products, arithmetic and copies ran while one was open for 6% -> 2% of each run, Pallas kernels for 0% -> 26%
where the time goes in v2:
time: 160 us; the launch traced here: 159 us
  waiting for transfers between devices  54.5 us (34%)
  starting transfers between devices  50.3 us (31%)
  Pallas kernels  45.1 us (28%)
  local copies, waits for them, and re-layouts  6.39 us (4%)
    ppermute x19, waiting for transfers between devices, send(): return lax.ppermute(value, AXES, pairs)  31.7 us
    ppermute x19, starting transfers between devices, send(): return lax.ppermute(value, AXES, pairs)  28.3 us
    pallas_call x2, Pallas kernels, matmul(): pl.pallas_call(functools.partial(matmul_kernel, m, start), in_specs=[SMEM...  25.1 us
    all_to_all x2, starting transfers between devices, shards(): lax.all_to_all(piece, 'slab', split_axis=0, concat_axis=0, tiled=True)  11.7 us
    all_to_all x2, waiting for transfers between devices, shards(): lax.all_to_all(piece, 'slab', split_axis=0, concat_axis=0, tiled=True)  11.7 us
    all_to_all x2, waiting for transfers between devices, shards(): lax.all_to_all(coded, AXES, split_axis=0, concat_axis=0, tiled=True, axis...  11.1 us
    all_to_all x2, starting transfers between devices, shards(): lax.all_to_all(coded, AXES, split_axis=0, concat_axis=0, tiled=True, axis...  10.3 us
    pallas_call x2, Pallas kernels, sum_coded(): pl.pallas_call(functools.partial(sum_kernel, number), in_specs=[VMEM] * 4...  9.81 us
  transfers between devices with their start and end apart: 23, of which 10 were waited for; matrix products, arithmetic and copies ran while one was open for 2% of the time, Pallas kernels for 26%

profile of v2, /device:TPU:0, one launch (start us, length us, event | category | flops | bytes accessed | tf_op | source)
XLA Modules:
  0.0 158.9 jit_solution(4946806801212909111)
XLA Ops:
  0.0 3.2 %shard_map.55 = bf16[256,1536]{1,0:T(8,128)(2,1)} custom-call(s32[8]{0:T(128)} %counts.7, s32[1,128]{1,0:T(1,128)} %bitcast.55, bf16[4,8,192,128]{3,2,1,0:T(8,128)(2,1)} %bitcast.57), custom_call_target="tpu_custom_call" | custom-call | flops 2000000000 | bytes 4000000 | tf_op jit(solution)/shard_map/pallas_call | solution.py:108
  3.2 8.1 %all-to-all-start = ((bf16[16,16,1536]{2,1,0:T(8,128)(2,1)}), bf16[16,16,1536]{2,1,0:T(8,128)(2,1)S(1)}, u32[]{:S(2)}, u32[]{:S(2)}) async-start(bf16[16,16,1536]{2,1,0:T(8,128)(2,1)} %bitcast.44), calls=%async_computation | async-start | bytes 1572864 | tf_op jit(solution)/shard_map/all_to_all | solution.py:332
  11.4 3.2 %shard_map.56 = bf16[256,1536]{1,0:T(8,128)(2,1)} custom-call(s32[8]{0:T(128)} %counts.7, s32[1,128]{1,0:T(1,128)} %bitcast.56, bf16[4,8,192,128]{3,2,1,0:T(8,128)(2,1)} %bitcast.58), custom_call_target="tpu_custom_call" | custom-call | flops 2000000000 | bytes 4000000 | tf_op jit(solution)/shard_map/pallas_call | solution.py:108
  14.7 11.7 %all-to-all-done = bf16[16,16,1536]{2,1,0:T(8,128)(2,1)S(1)} async-done(((bf16[16,16,1536]{2,1,0:T(8,128)(2,1)}), bf16[16,16,1536]{2,1,0:T(8,128)(2,1)S(1)}, u32[]{:S(2)}, u32[]{:S(2)}) %all-to-all-start) | async-done | bytes 786464 | tf_op jit(solution)/shard_map/all_to_all | solution.py:332
  26.4 3.6 %all-to-all-start.1 = ((bf16[16,16,1536]{2,1,0:T(8,128)(2,1)}), bf16[16,16,1536]{2,1,0:T(8,128)(2,1)S(1)}, u32[]{:S(2)}, u32[]{:S(2)}) async-start(bf16[16,16,1536]{2,1,0:T(8,128)(2,1)} %bitcast.43), calls=%async_computation.1 | async-start | bytes 1572864 | tf_op jit(solution)/shard_map/all_to_all | solution.py:332
  30.3 2.8 %collective-permute-start = (bf16[128,1536]{1,0:T(8,128)(2,1)S(1)}, bf16[128,1536]{1,0:T(8,128)(2,1)S(1)}, u32[]{:S(2)}, u32[]{:S(2)}) collective-permute-start(bf16[128,1536]{1,0:T(8,128)(2,1)S(1)} %convolution_convert_fusion.3), channel_id=1, source_target_pairs={{0,6},{1,7},{2,0},{3,1},{4,2},{5,3},{6,4},{7,5},{8,14},{9,15},{10,... | collective-permute-start | bytes 1179656 | tf_op jit(solution)/shard_map/ppermute | solution.py:44
  34.3 2.6 %collective-permute-start.3 = (bf16[128,1536]{1,0:T(8,128)(2,1)S(1)}, bf16[128,1536]{1,0:T(8,128)(2,1)S(1)}, u32[]{:S(2)}, u32[]{:S(2)}) collective-permute-start(bf16[128,1536]{1,0:T(8,128)(2,1)S(1)} %convolution_convert_fusion.2), channel_id=1, source_target_pairs={{0,6},{1,7},{2,0},{3,1},{4,2},{5,3},{6,4},{7,5},{8,14},{9,15},{10,... | collective-permute-start | bytes 1179656 | tf_op jit(solution)/shard_map/ppermute | solution.py:44
  36.9 5.9 %collective-permute-done = bf16[128,1536]{1,0:T(8,128)(2,1)S(1)} collective-permute-done((bf16[128,1536]{1,0:T(8,128)(2,1)S(1)}, bf16[128,1536]{1,0:T(8,128)(2,1)S(1)}, u32[]{:S(2)}, u32[]{:S(2)}) %collective-permute-start) | collective-permute-done | bytes 393248 | tf_op jit(solution)/shard_map/ppermute | solution.py:44
  42.7 3.7 %collective-permute-start.1 = (bf16[128,1536]{1,0:T(8,128)(2,1)S(1)}, bf16[128,1536]{1,0:T(8,128)(2,1)}, u32[]{:S(2)}, u32[]{:S(2)}) collective-permute-start(bf16[128,1536]{1,0:T(8,128)(2,1)S(1)} %collective-permute-done), channel_id=1, source_target_pairs={{0,6},{1,7},{2,0},{3,1},{4,2},{5,3},{6,4},{7,5},{8,14},{9,15},{10,... | collective-permute-start | bytes 1179656 | tf_op jit(solution)/shard_map/ppermute | solution.py:44
  47.4 7.8 %collective-permute-done.2 = bf16[128,1536]{1,0:T(8,128)(2,1)S(1)} collective-permute-done((bf16[128,1536]{1,0:T(8,128)(2,1)S(1)}, bf16[128,1536]{1,0:T(8,128)(2,1)S(1)}, u32[]{:S(2)}, u32[]{:S(2)}) %collective-permute-start.2) | collective-permute-done | bytes 393248 | tf_op jit(solution)/shard_map/ppermute | solution.py:44
  55.2 2.4 %collective-permute-done.1 = bf16[128,1536]{1,0:T(8,128)(2,1)} collective-permute-done((bf16[128,1536]{1,0:T(8,128)(2,1)S(1)}, bf16[128,1536]{1,0:T(8,128)(2,1)}, u32[]{:S(2)}, u32[]{:S(2)}) %collective-permute-start.1) | collective-permute-done | bytes 393248 | tf_op jit(solution)/shard_map/ppermute | solution.py:44
  57.7 3.9 %collective-permute-done.5 = bf16[128,1536]{1,0:T(8,128)(2,1)} collective-permute-done((bf16[128,1536]{1,0:T(8,128)(2,1)S(1)}, bf16[128,1536]{1,0:T(8,128)(2,1)}, u32[]{:S(2)}, u32[]{:S(2)}) %collective-permute-start.5) | collective-permute-done | bytes 393248 | tf_op jit(solution)/shard_map/ppermute | solution.py:44
  63.6 3.2 %collective-permute-start.14 = (bf16[128,1536]{1,0:T(8,128)(2,1)S(1)}, bf16[128,1536]{1,0:T(8,128)(2,1)S(1)}, u32[]{:S(2)}, u32[]{:S(2)}) collective-permute-start(bf16[128,1536]{1,0:T(8,128)(2,1)S(1)} %convolution_convert_fusion), channel_id=1, source_target_pairs={{0,6},{1,7},{2,0},{3,1},{4,2},{5,3},{6,4},{7,5},{8,14},{9,15},{10,... | collective-permute-start | bytes 1179656 | tf_op jit(solution)/shard_map/ppermute | solution.py:44
  66.9 12.5 %shard_map.57 = (f32[64,6144]{1,0:T(8,128)}, s16[64,6272]{1,0:T(8,128)(2,1)}, s16[64,6272]{1,0:T(8,128)(2,1)}, s16[64,6272]{1,0:T(8,128)(2,1)}) custom-call(s32[8]{0:T(128)} %counts.7, s32[128]{0:T(128)} %c_orbitals.3, bf16[2,64,1536]{2,1,0:T(8,128)(2,1)} %bitcast.41, bf16[2,64,1536]{2,1,0:T(8,128)(2,1)} %bitcast.46, bf16[2,64,1536]{2,1,0:T(8,128)(2,1)} %bitcast.8.refs_2_, ...), custom_call_target="tpu_custom_call" | custom-call | flops 4831838208 | bytes 18874368 | tf_op jit(solution)/shard_map/pallas_call | solution.py:213
  83.6 2.7 %collective-permute-start.8 = (s16[64,6272]{1,0:T(8,128)(2,1)}, s16[64,6272]{1,0:T(8,128)(2,1)S(1)}, u32[]{:S(2)}, u32[]{:S(2)}) collective-permute-start(s16[64,6272]{1,0:T(8,128)(2,1)} %get-tuple-element.45), channel_id=1, source_target_pairs={{0,16},{1,65},{2,18},{3,67},{4,20},{5,69},{6,22},{7,71},{8,24},{9,... | collective-permute-start | bytes 2408456 | tf_op jit(solution)/shard_map/ppermute | solution.py:44
  90.1 12.6 %shard_map.58 = (f32[64,6144]{1,0:T(8,128)}, s16[64,6272]{1,0:T(8,128)(2,1)}, s16[64,6272]{1,0:T(8,128)(2,1)}, s16[64,6272]{1,0:T(8,128)(2,1)}) custom-call(s32[8]{0:T(128)} %counts.7, s32[128]{0:T(128)} %c_orbitals.3, bf16[2,64,1536]{2,1,0:T(8,128)(2,1)} %bitcast.40, bf16[2,64,1536]{2,1,0:T(8,128)(2,1)} %bitcast.45, bf16[2,64,1536]{2,1,0:T(8,128)(2,1)} %bitcast.53, ...), custom_call_target="tpu_custom_call" | custom-call | flops 4831838208 | bytes 18874368 | tf_op jit(solution)/shard_map/pallas_call | solution.py:213
  104.1 2.7 %collective-permute-start.17 = (s16[64,6272]{1,0:T(8,128)(2,1)}, s16[64,6272]{1,0:T(8,128)(2,1)S(1)}, u32[]{:S(2)}, u32[]{:S(2)}) collective-permute-start(s16[64,6272]{1,0:T(8,128)(2,1)} %get-tuple-element.59), channel_id=1, source_target_pairs={{0,16},{1,65},{2,18},{3,67},{4,20},{5,69},{6,22},{7,71},{8,24},{9,... | collective-permute-start | bytes 2408456 | tf_op jit(solution)/shard_map/ppermute | solution.py:44
  109.4 4.9 %shard_map.59 = s16[256,1664]{1,0:T(8,128)(2,1)} custom-call(f32[64,6144]{1,0:T(8,128)} %get-tuple-element.54.own, s16[64,6272]{1,0:T(8,128)(2,1)} %copy-done.6, s16[64,6272]{1,0:T(8,128)(2,1)} %copy-done.8, s16[64,6272]{1,0:T(8,128)(2,1)} %copy-done.10), custom_call_target="tpu_custom_call" | custom-call | flops 3145728 | bytes 4718592 | tf_op jit(solution)/shard_map/pallas_call | solution.py:260
  114.3 5.2 %all-to-all-start.2 = ((s16[16,16,1664]{2,1,0:T(8,128)(2,1)}), s16[16,16,1664]{2,1,0:T(8,128)(2,1)S(1)}, u32[]{:S(2)}, u32[]{:S(2)}) async-start(s16[16,16,1664]{2,1,0:T(8,128)(2,1)} %bitcast.35), calls=%async_computation.2 | async-start | bytes 1703936 | tf_op jit(solution)/shard_map/all_to_all | solution.py:364
  120.8 9.8 %collective-permute-done.17.q2 = s16[64,6272]{1,0:T(8,128)(2,1)S(1)} collective-permute-done((s16[64,6272]{1,0:T(8,128)(2,1)}, s16[64,6272]{1,0:T(8,128)(2,1)S(1)}, u32[]{:S(2)}, u32[]{:S(2)}) %collective-permute-start.17) | collective-permute-done | bytes 802848 | tf_op jit(solution)/shard_map/ppermute | solution.py:44
  132.4 4.9 %shard_map.60 = s16[256,1664]{1,0:T(8,128)(2,1)} custom-call(f32[64,6144]{1,0:T(8,128)} %get-tuple-element.53.own, s16[64,6272]{1,0:T(8,128)(2,1)} %copy-done.7, s16[64,6272]{1,0:T(8,128)(2,1)} %copy-done.9, s16[64,6272]{1,0:T(8,128)(2,1)} %copy-done.11), custom_call_target="tpu_custom_call" | custom-call | flops 3145728 | bytes 4718592 | tf_op jit(solution)/shard_map/pallas_call | solution.py:260
  137.3 5.1 %all-to-all-start.3 = ((s16[16,16,1664]{2,1,0:T(8,128)(2,1)}), s16[16,16,1664]{2,1,0:T(8,128)(2,1)S(1)}, u32[]{:S(2)}, u32[]{:S(2)}) async-start(s16[16,16,1664]{2,1,0:T(8,128)(2,1)} %bitcast.36), calls=%async_computation.3 | async-start | bytes 1703936 | tf_op jit(solution)/shard_map/all_to_all | solution.py:364
  143.1 11.1 %all-to-all-done.3 = s16[16,16,1664]{2,1,0:T(8,128)(2,1)S(1)} async-done(((s16[16,16,1664]{2,1,0:T(8,128)(2,1)}), s16[16,16,1664]{2,1,0:T(8,128)(2,1)S(1)}, u32[]{:S(2)}, u32[]{:S(2)}) %all-to-all-start.3) | async-done | bytes 852000 | tf_op jit(solution)/shard_map/all_to_all | solution.py:364
  155.1 3.8 %shard_map.61 = f32[32,6144]{1,0:T(8,128)} custom-call(f32[8,6144]{1,0:T(8,128)} %compare_convert_fusion.allow, s16[256,1664]{1,0:T(8,128)(2,1)} %bitcast.37, s16[256,1664]{1,0:T(8,128)(2,1)} %bitcast.38), custom_call_target="tpu_custom_call" | custom-call | flops 10000000 | bytes 4000000 | tf_op jit(solution)/shard_map/pallas_call | solution.py:291
  (94 shorter events, 21.2 us)
Async XLA Ops:
  0.0 66.8 %collective-permute-start.6 = (bf16[8,8,192,768]{3,2,1,0:T(8,128)(2,1)}, bf16[8,8,192,768]{3,2,1,0:T(8,128)(2,1)}, u32[]{:S(2)}, u32[]{:S(2)}) collective-permute-start(bf16[8,8,192,768]{3,2,1,0:T(8,128)(2,1)} %refs_8_.3), channel_id=1, source_target_pairs={{0,1},{1,0},{2,3},{3,2},{4,5},{5,4},{6,7},{7,6},{8,9},{9,8},{10,11... | collective-permute-start | bytes 56623112 | tf_op jit(solution)/shard_map/ppermute | solution.py:44
  3.2 23.2 %all-to-all-start = ((bf16[16,16,1536]{2,1,0:T(8,128)(2,1)}), bf16[16,16,1536]{2,1,0:T(8,128)(2,1)S(1)}, u32[]{:S(2)}, u32[]{:S(2)}) async-start(bf16[16,16,1536]{2,1,0:T(8,128)(2,1)} %bitcast.44), calls=%async_computation | async-start | bytes 1572864 | tf_op jit(solution)/shard_map/all_to_all | solution.py:332
  26.4 20.4 %all-to-all-start.1 = ((bf16[16,16,1536]{2,1,0:T(8,128)(2,1)}), bf16[16,16,1536]{2,1,0:T(8,128)(2,1)S(1)}, u32[]{:S(2)}, u32[]{:S(2)}) async-start(bf16[16,16,1536]{2,1,0:T(8,128)(2,1)} %bitcast.43), calls=%async_computation.1 | async-start | bytes 1572864 | tf_op jit(solution)/shard_map/all_to_all | solution.py:332
  30.3 12.4 %collective-permute-start = (bf16[128,1536]{1,0:T(8,128)(2,1)S(1)}, bf16[128,1536]{1,0:T(8,128)(2,1)S(1)}, u32[]{:S(2)}, u32[]{:S(2)}) collective-permute-start(bf16[128,1536]{1,0:T(8,128)(2,1)S(1)} %convolution_convert_fusion.3), channel_id=1, source_target_pairs={{0,6},{1,7},{2,0},{3,1},{4,2},{5,3},{6,4},{7,5},{8,14},{9,15},{10,... | collective-permute-start | bytes 1179656 | tf_op jit(solution)/shard_map/ppermute | solution.py:44
  33.5 33.4 %copy-start.5 = (bf16[128,1536]{1,0:T(8,128)(2,1)}, bf16[128,1536]{1,0:T(8,128)(2,1)S(1)}, u32[]{:S(2)}) copy-start(bf16[128,1536]{1,0:T(8,128)(2,1)S(1)} %convolution_convert_fusion.2) | copy-start | bytes 1179652
  33.5 13.3 %collective-permute-start.4 = (bf16[128,1536]{1,0:T(8,128)(2,1)S(1)}, bf16[128,1536]{1,0:T(8,128)(2,1)S(1)}, u32[]{:S(2)}, u32[]{:S(2)}) collective-permute-start(bf16[128,1536]{1,0:T(8,128)(2,1)S(1)} %convolution_convert_fusion.2), channel_id=1, source_target_pairs={{0,2},{1,3},{2,4},{3,5},{4,6},{5,7},{6,0},{7,1},{8,10},{9,11},{10,... | collective-permute-start | bytes 1179656 | tf_op jit(solution)/shard_map/ppermute | solution.py:44
  33.5 21.7 %collective-permute-start.2 = (bf16[128,1536]{1,0:T(8,128)(2,1)S(1)}, bf16[128,1536]{1,0:T(8,128)(2,1)S(1)}, u32[]{:S(2)}, u32[]{:S(2)}) collective-permute-start(bf16[128,1536]{1,0:T(8,128)(2,1)S(1)} %convolution_convert_fusion.3), channel_id=1, source_target_pairs={{0,2},{1,3},{2,4},{3,5},{4,6},{5,7},{6,0},{7,1},{8,10},{9,11},{10,... | collective-permute-start | bytes 1179656 | tf_op jit(solution)/shard_map/ppermute | solution.py:44
  34.3 21.0 %collective-permute-start.3 = (bf16[128,1536]{1,0:T(8,128)(2,1)S(1)}, bf16[128,1536]{1,0:T(8,128)(2,1)S(1)}, u32[]{:S(2)}, u32[]{:S(2)}) collective-permute-start(bf16[128,1536]{1,0:T(8,128)(2,1)S(1)} %convolution_convert_fusion.2), channel_id=1, source_target_pairs={{0,6},{1,7},{2,0},{3,1},{4,2},{5,3},{6,4},{7,5},{8,14},{9,15},{10,... | collective-permute-start | bytes 1179656 | tf_op jit(solution)/shard_map/ppermute | solution.py:44
  42.7 14.9 %collective-permute-start.1 = (bf16[128,1536]{1,0:T(8,128)(2,1)S(1)}, bf16[128,1536]{1,0:T(8,128)(2,1)}, u32[]{:S(2)}, u32[]{:S(2)}) collective-permute-start(bf16[128,1536]{1,0:T(8,128)(2,1)S(1)} %collective-permute-done), channel_id=1, source_target_pairs={{0,6},{1,7},{2,0},{3,1},{4,2},{5,3},{6,4},{7,5},{8,14},{9,15},{10,... | collective-permute-start | bytes 1179656 | tf_op jit(solution)/shard_map/ppermute | solution.py:44
  46.8 14.8 %collective-permute-start.5 = (bf16[128,1536]{1,0:T(8,128)(2,1)S(1)}, bf16[128,1536]{1,0:T(8,128)(2,1)}, u32[]{:S(2)}, u32[]{:S(2)}) collective-permute-start(bf16[128,1536]{1,0:T(8,128)(2,1)S(1)} %collective-permute-done.4), channel_id=1, source_target_pairs={{0,2},{1,3},{2,4},{3,5},{4,6},{5,7},{6,0},{7,1},{8,10},{9,11},{10,... | collective-permute-start | bytes 1179656 | tf_op jit(solution)/shard_map/ppermute | solution.py:44
  61.6 17.8 %collective-permute-start.10 = (bf16[128,1536]{1,0:T(8,128)(2,1)S(1)}, bf16[128,1536]{1,0:T(8,128)(2,1)S(1)}, u32[]{:S(2)}, u32[]{:S(2)}) collective-permute-start(bf16[128,1536]{1,0:T(8,128)(2,1)S(1)} %convolution_convert_fusion.1), channel_id=1, source_target_pairs={{0,6},{1,7},{2,0},{3,1},{4,2},{5,3},{6,4},{7,5},{8,14},{9,15},{10,... | collective-permute-start | bytes 1179656 | tf_op jit(solution)/shard_map/ppermute | solution.py:44
  61.6 22.1 %collective-permute-start.13 = (bf16[128,1536]{1,0:T(8,128)(2,1)S(1)}, bf16[128,1536]{1,0:T(8,128)(2,1)S(1)}, u32[]{:S(2)}, u32[]{:S(2)}) collective-permute-start(bf16[128,1536]{1,0:T(8,128)(2,1)S(1)} %convolution_convert_fusion.1), channel_id=1, source_target_pairs={{0,2},{1,3},{2,4},{3,5},{4,6},{5,7},{6,0},{7,1},{8,10},{9,11},{10,... | collective-permute-start | bytes 1179656 | tf_op jit(solution)/shard_map/ppermute | solution.py:44
  63.6 16.5 %collective-permute-start.11 = (bf16[128,1536]{1,0:T(8,128)(2,1)S(1)}, bf16[128,1536]{1,0:T(8,128)(2,1)S(1)}, u32[]{:S(2)}, u32[]{:S(2)}) collective-permute-start(bf16[128,1536]{1,0:T(8,128)(2,1)S(1)} %convolution_convert_fusion), channel_id=1, source_target_pairs={{0,2},{1,3},{2,4},{3,5},{4,6},{5,7},{6,0},{7,1},{8,10},{9,11},{10,... | collective-permute-start | bytes 1179656 | tf_op jit(solution)/shard_map/ppermute | solution.py:44
  63.6 22.7 %collective-permute-start.14 = (bf16[128,1536]{1,0:T(8,128)(2,1)S(1)}, bf16[128,1536]{1,0:T(8,128)(2,1)S(1)}, u32[]{:S(2)}, u32[]{:S(2)}) collective-permute-start(bf16[128,1536]{1,0:T(8,128)(2,1)S(1)} %convolution_convert_fusion), channel_id=1, source_target_pairs={{0,6},{1,7},{2,0},{3,1},{4,2},{5,3},{6,4},{7,5},{8,14},{9,15},{10,... | collective-permute-start | bytes 1179656 | tf_op jit(solution)/shard_map/ppermute | solution.py:44
  80.1 8.4 %collective-permute-start.12 = (bf16[128,1536]{1,0:T(8,128)(2,1)S(1)}, bf16[128,1536]{1,0:T(8,128)(2,1)S(1)}, u32[]{:S(2)}, u32[]{:S(2)}) collective-permute-start(bf16[128,1536]{1,0:T(8,128)(2,1)S(1)} %collective-permute-done.10), channel_id=1, source_target_pairs={{0,6},{1,7},{2,0},{3,1},{4,2},{5,3},{6,4},{7,5},{8,14},{9,15},{10,... | collective-permute-start | bytes 1179656 | tf_op jit(solution)/shard_map/ppermute | solution.py:44
  80.1 9.2 %collective-permute-start.15 = (bf16[128,1536]{1,0:T(8,128)(2,1)S(1)}, bf16[128,1536]{1,0:T(8,128)(2,1)S(1)}, u32[]{:S(2)}, u32[]{:S(2)}) collective-permute-start(bf16[128,1536]{1,0:T(8,128)(2,1)S(1)} %collective-permute-done.11), channel_id=1, source_target_pairs={{0,2},{1,3},{2,4},{3,5},{4,6},{5,7},{6,0},{7,1},{8,10},{9,11},{10,... | collective-permute-start | bytes 1179656 | tf_op jit(solution)/shard_map/ppermute | solution.py:44
  82.2 24.6 %collective-permute-start.7 = (s16[64,6272]{1,0:T(8,128)(2,1)}, s16[64,6272]{1,0:T(8,128)(2,1)S(1)}, u32[]{:S(2)}, u32[]{:S(2)}) collective-permute-start(s16[64,6272]{1,0:T(8,128)(2,1)} %get-tuple-element.44), channel_id=1, source_target_pairs={{0,8},{1,33},{2,10},{3,35},{4,12},{5,37},{6,14},{7,39},{8,16},{9,4... | collective-permute-start | bytes 2408456 | tf_op jit(solution)/shard_map/ppermute | solution.py:44
  83.6 24.6 %collective-permute-start.8 = (s16[64,6272]{1,0:T(8,128)(2,1)}, s16[64,6272]{1,0:T(8,128)(2,1)S(1)}, u32[]{:S(2)}, u32[]{:S(2)}) collective-permute-start(s16[64,6272]{1,0:T(8,128)(2,1)} %get-tuple-element.45), channel_id=1, source_target_pairs={{0,16},{1,65},{2,18},{3,67},{4,20},{5,69},{6,22},{7,71},{8,24},{9,... | collective-permute-start | bytes 2408456 | tf_op jit(solution)/shard_map/ppermute | solution.py:44
  87.1 21.2 %collective-permute-start.9 = (s16[64,6272]{1,0:T(8,128)(2,1)}, s16[64,6272]{1,0:T(8,128)(2,1)S(1)}, u32[]{:S(2)}, u32[]{:S(2)}) collective-permute-start(s16[64,6272]{1,0:T(8,128)(2,1)} %get-tuple-element.46), channel_id=1, source_target_pairs={{0,24},{1,97},{2,26},{3,99},{4,28},{5,101},{6,30},{7,103},{8,0},{9... | collective-permute-start | bytes 2408456 | tf_op jit(solution)/shard_map/ppermute | solution.py:44
  102.7 18.1 %collective-permute-start.16 = (s16[64,6272]{1,0:T(8,128)(2,1)}, s16[64,6272]{1,0:T(8,128)(2,1)S(1)}, u32[]{:S(2)}, u32[]{:S(2)}) collective-permute-start(s16[64,6272]{1,0:T(8,128)(2,1)} %get-tuple-element.58), channel_id=1, source_target_pairs={{0,8},{1,33},{2,10},{3,35},{4,12},{5,37},{6,14},{7,39},{8,16},{9,4... | collective-permute-start | bytes 2408456 | tf_op jit(solution)/shard_map/ppermute | solution.py:44
  104.1 26.5 %collective-permute-start.17 = (s16[64,6272]{1,0:T(8,128)(2,1)}, s16[64,6272]{1,0:T(8,128)(2,1)S(1)}, u32[]{:S(2)}, u32[]{:S(2)}) collective-permute-start(s16[64,6272]{1,0:T(8,128)(2,1)} %get-tuple-element.59), channel_id=1, source_target_pairs={{0,16},{1,65},{2,18},{3,67},{4,20},{5,69},{6,22},{7,71},{8,24},{9,... | collective-permute-start | bytes 2408456 | tf_op jit(solution)/shard_map/ppermute | solution.py:44
  106.8 23.8 %collective-permute-start.18 = (s16[64,6272]{1,0:T(8,128)(2,1)}, s16[64,6272]{1,0:T(8,128)(2,1)S(1)}, u32[]{:S(2)}, u32[]{:S(2)}) collective-permute-start(s16[64,6272]{1,0:T(8,128)(2,1)} %get-tuple-element.60), channel_id=1, source_target_pairs={{0,24},{1,97},{2,26},{3,99},{4,28},{5,101},{6,30},{7,103},{8,0},{9... | collective-permute-start | bytes 2408456 | tf_op jit(solution)/shard_map/ppermute | solution.py:44
  114.3 23.0 %all-to-all-start.2 = ((s16[16,16,1664]{2,1,0:T(8,128)(2,1)}), s16[16,16,1664]{2,1,0:T(8,128)(2,1)S(1)}, u32[]{:S(2)}, u32[]{:S(2)}) async-start(s16[16,16,1664]{2,1,0:T(8,128)(2,1)} %bitcast.35), calls=%async_computation.2 | async-start | bytes 1703936 | tf_op jit(solution)/shard_map/all_to_all | solution.py:364
  137.3 16.9 %all-to-all-start.3 = ((s16[16,16,1664]{2,1,0:T(8,128)(2,1)}), s16[16,16,1664]{2,1,0:T(8,128)(2,1)S(1)}, u32[]{:S(2)}, u32[]{:S(2)}) async-start(s16[16,16,1664]{2,1,0:T(8,128)(2,1)} %bitcast.36), calls=%async_computation.3 | async-start | bytes 1703936 | tf_op jit(solution)/shard_map/all_to_all | solution.py:364
  (24 other events, 219.2 us)

commit v3 on v2

--- a/solution.py
+++ b/solution.py
@@ -12,7 +12,7 @@
 FINE = 256.0
 AXES = ("slab", "pair")
 MIB = 2**20
-LIMIT = 58
+LIMIT = 52
 HBM = pl.BlockSpec(memory_space=pl.ANY)
 VMEM = pl.BlockSpec(memory_space=pltpu.VMEM)
 SMEM = pl.BlockSpec(memory_space=pltpu.SMEM)
@@ -42,6 +42,10 @@
 
 def send(value, pairs):
     return lax.ppermute(value, AXES, pairs)
+
+
+def in_vmem(values):
+    return [pltpu.with_memory_space_constraint(v, pltpu.VMEM) for v in values]
 
 
 def cost(flops, size):
@@ -76,8 +80,8 @@
     return ends
 
 
-def arrange_kernel(start, counts, c_ref, t_ref, out, sorted_ref):
-    pairs, count, dmax, c_tot = t_ref.shape
+def arrange_kernel(start, count, counts, c_ref, t_ref, out, sorted_ref):
+    pairs, _, dmax, c_tot = t_ref.shape
     n_slab = c_tot // 8
     rows = pairs * count
     ends = ends_of(counts)
@@ -90,7 +94,7 @@
         limit = sum(jnp.where(block == g, counts[g], 0) for g in range(8))
         keep = slot < limit
         for pair in range(pairs):
-            kept = jnp.where(keep, t_ref[pair, p].astype(jnp.float32), 0.0).astype(jnp.bfloat16)
+            kept = jnp.where(keep, t_ref[pair, start + p].astype(jnp.float32), 0.0).astype(jnp.bfloat16)
             split = lax.dot_general(by_c, kept, (((1,), (1,)), ((), ())), preferred_element_type=jnp.float32)
             split = split.astype(jnp.bfloat16)
             q = pair * count + p
@@ -106,47 +110,75 @@
     rows, _, dmax, c_tot = amplitudes.shape
     size = c_tot // 8 * rows * count
     return pl.pallas_call(
-        functools.partial(arrange_kernel, start),
+        functools.partial(arrange_kernel, start, count),
         grid=(1,),
         in_specs=[
             SMEM,
             pl.BlockSpec((1, c_tot), lambda i: (0, 0)),
-            pl.BlockSpec((rows, count, dmax, c_tot), lambda i: (0, start // count, 0, 0)),
+            pl.BlockSpec((rows, 8, dmax, c_tot), lambda i: (0, 0, 0, 0)),
         ],
         out_specs=pl.BlockSpec((size, 8 * dmax), lambda i: (0, 0)),
         out_shape=jax.ShapeDtypeStruct((size, 8 * dmax), jnp.bfloat16),
         scratch_shapes=[pltpu.VMEM((8, size, dmax), jnp.bfloat16)],
-        compiler_params=params(LIMIT),
+        compiler_params=params(58),
         cost_estimate=cost(2 * 10**9, 4 * 10**6),
     )(vir_counts, c_orbitals.reshape(1, c_tot), amplitudes)
 
 
+def copies_of(sides, counts, c_orbitals, label, target, sems):
+    c_dev, _, dmax, _ = sides[0].shape
+    ends = ends_of(counts)
+    slab = lax.axis_index("slab")
+    copies = []
+    for c in range(c_dev):
+        orbital = c_orbitals[slab * c_dev + c]
+        irrep = sum((orbital >= ends[g]).astype(jnp.int32) for g in range(8))
+        for side, ref in enumerate(sides):
+            copies.append(pltpu.make_async_copy(
+                ref.at[c, jnp.bitwise_xor(irrep, label)], target.at[side, pl.ds(c * dmax, dmax)], sems.at[side, c]
+            ))
+    return copies
+
+
+def load_kernel(label, counts, c_orbitals, v_own, v_other, after, out, sems):
+    del after
+    copies = copies_of((v_own, v_other), counts, c_orbitals, label, out, sems)
+    for copy in copies:
+        copy.start()
+    for copy in copies:
+        copy.wait()
+
+
+def load(v_own, v_other, vir_counts, c_orbitals, label, after):
+    c_dev, _, dmax, half = v_own.shape
+    return pl.pallas_call(
+        functools.partial(load_kernel, label),
+        in_specs=[SMEM, SMEM, HBM, HBM, HBM],
+        out_specs=VMEM,
+        out_shape=pltpu.VMEM((2, c_dev * dmax, half), jnp.bfloat16),
+        scratch_shapes=[pltpu.SemaphoreType.DMA((2, c_dev))],
+        compiler_params=params(LIMIT),
+        cost_estimate=cost(0, v_own.size),
+    )(vir_counts, c_orbitals, v_own, v_other, after)
+
+
 def matmul_kernel(m, start, counts, c_orbitals, *refs):
-    lows, highs, (v_own, v_other) = refs[:4], refs[4:8], refs[8:10]
-    outs = refs[10:14]
-    lhs, slots, even, odd, own, coded, codes, sems, v_sems, o_sems = refs[14:]
+    lows, highs, sides = refs[:4], refs[4:8], refs[8:10]
+    ready = refs[10]
+    outs = refs[-14:-10]
+    lhs, slots, even, odd, own, coded, codes, sems, v_sems, o_sems = refs[-10:]
     number, _, rows, depth = lhs.shape
-    c_dev, _, dmax, half = v_own.shape
+    half = sides[0].shape[3]
     width = 2 * half
     split = lows[0].shape[0]
     slab, pair = lax.axis_index("slab"), lax.axis_index("pair")
     x, core = lax.div(pair, 2), lax.rem(pair, 2)
     me = jnp.where(core == 0, lax.rem(slab, 4), lax.div(slab, 4))
-    ends = ends_of(counts)
-    irreps = []
-    for c in range(c_dev):
-        orbital = c_orbitals[slab * c_dev + c]
-        irreps.append(sum((orbital >= ends[g]).astype(jnp.int32) for g in range(8)))
 
     def fetch(p):
-        return [
-            pltpu.make_async_copy(
-                ref.at[c, jnp.bitwise_xor(irreps[c], start + p)],
-                slots.at[p % 3, side, pl.ds(c * dmax, dmax)],
-                v_sems.at[p % 3, side, c],
-            )
-            for side, ref in ((0, v_own), (1, v_other)) for c in range(c_dev)
-        ]
+        if p == 0:
+            return []
+        return copies_of(sides, counts, c_orbitals, start + p, slots.at[p % 3], v_sems.at[p % 3])
 
     def arrivals(refs, first_p, at):
         return [
@@ -190,7 +222,8 @@
         left = lhs[p].reshape(4 * rows, depth)
         for side, at in ((0, core), (1, 1 - core)):
             at = pl.ds(pl.multiple_of(at * half, 128), half)
-            products[p % 2][:, :, at] = pick(left, slots[p % 3, side]).reshape(16, 4 * m, half)
+            right = slots[p % 3, side] if p else ready[side]
+            products[p % 2][:, :, at] = pick(left, right).reshape(16, 4 * m, half)
         if p > 0:
             finish(p - 1, products[(p - 1) % 2])
     finish(number - 1, products[(number - 1) % 2])
@@ -203,16 +236,18 @@
         copy.wait()
 
 
-def matmul(lows, highs, v_own, v_other, vir_counts, c_orbitals, m, start):
+def matmul(lows, highs, v_own, v_other, vir_counts, c_orbitals, m, start, ready, near):
     c_dev, _, dmax, half = v_own.shape
     rows, depth, width = 16 * m, c_dev * dmax, 2 * half
     arrays = [a.reshape(-1, rows, depth) for a in lows + highs]
     number = arrays[0].shape[0] + arrays[-1].shape[0]
     shapes = [jax.ShapeDtypeStruct((rows, number * width), jnp.float32)]
     shapes += [jax.ShapeDtypeStruct((rows, number * width + 128), jnp.int16)] * 3
+    if near:
+        arrays = in_vmem(arrays)
     return pl.pallas_call(
         functools.partial(matmul_kernel, m, start),
-        in_specs=[SMEM] * 2 + [HBM] * 10,
+        in_specs=[SMEM] * 2 + [VMEM if near else HBM] * 8 + [HBM] * 2 + [VMEM],
         out_specs=[HBM] * 4,
         out_shape=shapes,
         scratch_shapes=[
@@ -229,22 +264,35 @@
         ],
         compiler_params=params(LIMIT),
         cost_estimate=cost(2 * number * 4 * rows * depth * width, number * v_own.size // 2),
-    )(vir_counts, c_orbitals, *arrays, v_own, v_other)
-
-
-def sum_kernel(number, own, q1, q2, q3, out, high, low):
+    )(vir_counts, c_orbitals, *arrays, v_own, v_other, *in_vmem([ready]))
+
+
+def sum_kernel(number, own_ref, q1, q2, q3, out, own, q, high, low, sems):
     rows = own.shape[0]
     width = own.shape[1] // number
-    lane = lax.broadcasted_iota(jnp.int32, (rows, 128), 1)
-    scales = []
-    for q in (q1, q2, q3):
-        scales.append(jnp.exp2(q[:, number * width:].astype(jnp.float32) * (1.0 / FINE)) * (1.0 / TOP))
+    tail = slice(number * width, number * width + 128)
+    codes = [pltpu.make_async_copy(ref.at[:, tail], q.at[k, :, tail], sems.at[number, k]) for k, ref in enumerate((q1, q2, q3))]
+    copies = []
     for p in range(number):
         at = slice(p * width, (p + 1) * width)
+        copies.append([pltpu.make_async_copy(own_ref.at[:, at], own.at[:, at], sems.at[p, 3])])
+        for k, ref in enumerate((q1, q2, q3)):
+            copies[p].append(pltpu.make_async_copy(ref.at[:, at], q.at[k, :, at], sems.at[p, k]))
+    for group in [codes] + copies:
+        for copy in group:
+            copy.start()
+    lane = lax.broadcasted_iota(jnp.int32, (rows, 128), 1)
+    for copy in codes:
+        copy.wait()
+    scales = [jnp.exp2(q[k, :, tail].astype(jnp.float32) * (1.0 / FINE)) * (1.0 / TOP) for k in range(3)]
+    for p in range(number):
+        for copy in copies[p]:
+            copy.wait()
+        at = slice(p * width, (p + 1) * width)
         total = own[:, at]
-        for q, scale in zip((q1, q2, q3), scales):
-            one = jnp.sum(jnp.where(lane == p, scale, 0.0), axis=1, keepdims=True)
-            total += q[:, at].astype(jnp.float32) * one
+        for k in range(3):
+            one = jnp.sum(jnp.where(lane == p, scales[k], 0.0), axis=1, keepdims=True)
+            total += q[k, :, at].astype(jnp.float32) * one
         code, value = code_of(total)
         value = jnp.concatenate([value, jnp.broadcast_to(code, (rows, 128))], axis=1)
         upper = jnp.round(value * (1.0 / 256.0))
@@ -259,10 +307,16 @@
     width = total // number + 128
     return pl.pallas_call(
         functools.partial(sum_kernel, number),
-        in_specs=[VMEM] * 4,
+        in_specs=[HBM] * 4,
         out_specs=VMEM,
         out_shape=jax.ShapeDtypeStruct((number * rows, width), jnp.int16),
-        scratch_shapes=[pltpu.VMEM((number * rows, width), jnp.bfloat16)] * 2,
+        scratch_shapes=[
+            pltpu.VMEM(own.shape, jnp.float32),
+            pltpu.VMEM((3,) + parts[0].shape, jnp.int16),
+            pltpu.VMEM((number * rows, width), jnp.bfloat16),
+            pltpu.VMEM((number * rows, width), jnp.bfloat16),
+            pltpu.SemaphoreType.DMA((number + 1, 4)),
+        ],
         compiler_params=params(LIMIT),
         cost_estimate=cost(8 * own.size, 12 * own.size),
     )(own, *parts)
@@ -270,34 +324,37 @@
 
 def final_kernel(allow, *refs):
     got, out = refs[:-1], refs[-1]
-    width = out.shape[1]
+    width = out.shape[1] // 4
     pairs = out.shape[0] // 8
-    start = 0
-    for ref in got:
-        number = ref.shape[0] // (4 * pairs)
-        value = ref[...].astype(jnp.float32)
-        scale = jnp.exp2(value[:, width:] * (1.0 / FINE)) * (1.0 / TOP)
-        value = value[:, :width] * jnp.concatenate([scale] * (width // 128), axis=1)
-        total = jnp.sum(value.reshape(4, pairs * number, width), axis=0)
-        keep = allow[start:start + number] > 0.5
-        for pair in range(pairs):
-            part = total[pair * number:(pair + 1) * number]
-            out[pair * 8 + start:pair * 8 + start + number] = jnp.where(keep, part, 0.0)
-        start += number
+    for x in range(4):
+        start = 0
+        for ref in got:
+            number = ref.shape[0] // (16 * pairs)
+            total = 0.0
+            size = pairs * number
+            for d2 in range(4):
+                value = ref[(4 * x + d2) * size:(4 * x + d2 + 1) * size].astype(jnp.float32)
+                scale = jnp.exp2(value[:, width:] * (1.0 / FINE)) * (1.0 / TOP)
+                total += value[:, :width] * jnp.concatenate([scale] * (width // 128), axis=1)
+            at = slice(x * width, (x + 1) * width)
+            keep = allow[start:start + number, at] > 0.5
+            for pair in range(pairs):
+                part = total[pair * number:(pair + 1) * number]
+                out[pair * 8 + start:pair * 8 + start + number, at] = jnp.where(keep, part, 0.0)
+            start += number
 
 
 def final(got, allow, pairs):
     width = got[0].shape[1] - 128
+    last = pltpu.with_memory_space_constraint(got[-1], pltpu.VMEM)
     return pl.pallas_call(
         final_kernel,
-        grid=(4,),
-        in_specs=[pl.BlockSpec((8, width), lambda i: (0, i))]
-        + [pl.BlockSpec((g.shape[0] // 4, width + 128), lambda i: (i, 0)) for g in got],
-        out_specs=pl.BlockSpec((8 * pairs, width), lambda i: (0, i)),
+        in_specs=[VMEM] * (1 + len(got)),
+        out_specs=VMEM,
         out_shape=jax.ShapeDtypeStruct((8 * pairs, 4 * width), jnp.float32),
-        compiler_params=params(LIMIT),
+        compiler_params=params(24),
         cost_estimate=cost(10**7, 4 * 10**6),
-    )(allow, *got)
+    )(allow, *got[:-1], last)
 
 
 def allowed(vir_counts, a_orbitals, dmax):
@@ -332,26 +389,23 @@
         got = lax.all_to_all(piece, "slab", split_axis=0, concat_axis=0, tiled=True).reshape(size, depth)
         if chunk == 0:
             got, *pieces[1:] = lax.optimization_barrier((got, *pieces[1:]))
-        cut = size // 2
+        cut = 16 * m * (number // 2)
         relaid.append([pick(part, got).astype(jnp.bfloat16) for part in (chooser[:cut], chooser[cut:])])
 
     products, before = [], None
     for chunk, (low, high) in enumerate(relaid):
         if before is not None:
-            low, high, *_ = lax.optimization_barrier((low, high, *before))
+            low, high, other, *_ = lax.optimization_barrier((low, high, other, *before))
         low1, high3 = send(low, X_DOWN), send(high, X_UP)
         high1, low3 = send(high, X_DOWN), send(low, X_UP)
+        before = (high1, low3)
         if products:
             low1, high3, _ = lax.optimization_barrier((low1, high3, products[-1][0]))
         low2, high2 = send(low1, X_DOWN), send(high3, X_UP)
-        before = (low2, high2)
         arrays = [low, low1, low2, low3, high, high1, high2, high3]
-        if chunk + 1 < len(SPLIT):
-            arrays = lax.optimization_barrier((*arrays, *relaid[chunk + 1]))
-            relaid[chunk + 1] = arrays[8:]
-        products.append(matmul(
-            list(arrays[:4]), list(arrays[4:8]), integrals, other, vir_counts, c_orbitals, m, starts[chunk]
-        ))
+        operands = (integrals, other, vir_counts, c_orbitals)
+        ready = load(*operands, starts[chunk], products[-1][1] if chunk else relaid[-1][0])
+        products.append(matmul(arrays[:4], arrays[4:], *operands, m, starts[chunk], ready, chunk > 0))
 
     sent = [[send(q, first(k)) for k, q in enumerate(product) if k] for product in products]
     results = []

time: 160 us -> 151 us (0.944)
  waiting for transfers between devices: 54.5 us -> 49.5 us
  local copies, waits for them, and re-layouts: 6.39 us -> 2.83 us
    ppermute x19, waiting for transfers between devices: 31.7 us -> 26.2 us  [send(): return lax.ppermute(value, AXES, pairs)]
    unnamed x50 -> x26, local copies, waits for them, and re-layouts: 5.41 us -> 1.84 us
    pallas_call x5 -> x7, Pallas kernels: 20 us -> 23.3 us  [the longest x2 8.59 us: sum_coded(): pl.pallas_call(functools.partial(sum_kernel, number), in_specs=[HBM] * 4,...]
    pallas_call x2, Pallas kernels: 25.1 us -> 22.5 us  [matmul(): pl.pallas_call(functools.partial(matmul_kernel, m, start), in_specs=[SMEM...]
  transfers between devices with their start and end apart: 23 -> 23, of which waited for: 10 -> 10; matrix products, arithmetic and copies ran while one was open for 2% -> 2% of each run, Pallas kernels for 26% -> 30%
where the time goes in v3:
time: 151 us; the launch traced here: 150 us
  starting transfers between devices  50.3 us (33%)
  waiting for transfers between devices  49.5 us (33%)
  Pallas kernels  45.8 us (30%)
  local copies, waits for them, and re-layouts  2.83 us (2%)
    ppermute x19, starting transfers between devices, send(): return lax.ppermute(value, AXES, pairs)  28.7 us
    ppermute x19, waiting for transfers between devices, send(): return lax.ppermute(value, AXES, pairs)  26.2 us
    pallas_call x2, Pallas kernels, matmul(): pl.pallas_call(functools.partial(matmul_kernel, m, start), in_specs=[SMEM...  22.5 us
    all_to_all x2, waiting for transfers between devices, shards(): lax.all_to_all(coded, AXES, split_axis=0, concat_axis=0, tiled=True, axis...  11.8 us
    all_to_all x2, starting transfers between devices, shards(): lax.all_to_all(piece, 'slab', split_axis=0, concat_axis=0, tiled=True)  11.7 us
    all_to_all x2, waiting for transfers between devices, shards(): lax.all_to_all(piece, 'slab', split_axis=0, concat_axis=0, tiled=True)  11.4 us
    all_to_all x2, starting transfers between devices, shards(): lax.all_to_all(coded, AXES, split_axis=0, concat_axis=0, tiled=True, axis...  9.9 us
    pallas_call x2, Pallas kernels, sum_coded(): pl.pallas_call(functools.partial(sum_kernel, number), in_specs=[HBM] * 4,...  8.59 us
  transfers between devices with their start and end apart: 23, of which 10 were waited for; matrix products, arithmetic and copies ran while one was open for 2% of the time, Pallas kernels for 30%

profile of v3, /device:TPU:0, one launch (start us, length us, event | category | flops | bytes accessed | tf_op | source)
XLA Modules:
  0.0 150.2 jit_solution(7064584068700795019)
XLA Ops:
  0.0 3.5 %shard_map.55 = bf16[256,1536]{1,0:T(8,128)(2,1)} custom-call(s32[8]{0:T(128)} %counts.11, s32[1,128]{1,0:T(1,128)} %bitcast.55, bf16[4,8,192,128]{3,2,1,0:T(8,128)(2,1)} %bitcast.57), custom_call_target="tpu_custom_call" | custom-call | flops 2000000000 | bytes 4000000 | tf_op jit(solution)/shard_map/pallas_call | solution.py:112
  3.5 8.1 %all-to-all-start = ((bf16[16,16,1536]{2,1,0:T(8,128)(2,1)}), bf16[16,16,1536]{2,1,0:T(8,128)(2,1)S(1)}, u32[]{:S(2)}, u32[]{:S(2)}) async-start(bf16[16,16,1536]{2,1,0:T(8,128)(2,1)} %bitcast.50), calls=%async_computation | async-start | bytes 1572864 | tf_op jit(solution)/shard_map/all_to_all | solution.py:389
  11.7 3.5 %shard_map.56 = bf16[256,1536]{1,0:T(8,128)(2,1)} custom-call(s32[8]{0:T(128)} %counts.11, s32[1,128]{1,0:T(1,128)} %bitcast.56, bf16[4,8,192,128]{3,2,1,0:T(8,128)(2,1)} %bitcast.58), custom_call_target="tpu_custom_call" | custom-call | flops 2000000000 | bytes 4000000 | tf_op jit(solution)/shard_map/pallas_call | solution.py:112
  15.3 11.4 %all-to-all-done = bf16[16,16,1536]{2,1,0:T(8,128)(2,1)S(1)} async-done(((bf16[16,16,1536]{2,1,0:T(8,128)(2,1)}), bf16[16,16,1536]{2,1,0:T(8,128)(2,1)S(1)}, u32[]{:S(2)}, u32[]{:S(2)}) %all-to-all-start) | async-done | bytes 786464 | tf_op jit(solution)/shard_map/all_to_all | solution.py:389
  26.7 3.6 %all-to-all-start.1 = ((bf16[16,16,1536]{2,1,0:T(8,128)(2,1)}), bf16[16,16,1536]{2,1,0:T(8,128)(2,1)S(1)}, u32[]{:S(2)}, u32[]{:S(2)}) async-start(bf16[16,16,1536]{2,1,0:T(8,128)(2,1)} %bitcast.49), calls=%async_computation.1 | async-start | bytes 1572864 | tf_op jit(solution)/shard_map/all_to_all | solution.py:389
  32.5 1.8 %collective-permute-start = (bf16[128,1536]{1,0:T(8,128)(2,1)S(1)}, bf16[128,1536]{1,0:T(8,128)(2,1)S(1)}, u32[]{:S(2)}, u32[]{:S(2)}) collective-permute-start(bf16[128,1536]{1,0:T(8,128)(2,1)S(1)} %convolution_convert_fusion.3), channel_id=1, source_target_pairs={{0,6},{1,7},{2,0},{3,1},{4,2},{5,3},{6,4},{7,5},{8,14},{9,15},{10,... | collective-permute-start | bytes 1179656 | tf_op jit(solution)/shard_map/ppermute | solution.py:44
  34.6 2.9 %collective-permute-start.3 = (bf16[128,1536]{1,0:T(8,128)(2,1)S(1)}, bf16[128,1536]{1,0:T(8,128)(2,1)S(1)}, u32[]{:S(2)}, u32[]{:S(2)}) collective-permute-start(bf16[128,1536]{1,0:T(8,128)(2,1)S(1)} %convolution_convert_fusion.2), channel_id=1, source_target_pairs={{0,6},{1,7},{2,0},{3,1},{4,2},{5,3},{6,4},{7,5},{8,14},{9,15},{10,... | collective-permute-start | bytes 1179656 | tf_op jit(solution)/shard_map/ppermute | solution.py:44
  37.5 6.4 %collective-permute-done.4 = bf16[128,1536]{1,0:T(8,128)(2,1)S(1)} collective-permute-done((bf16[128,1536]{1,0:T(8,128)(2,1)S(1)}, bf16[128,1536]{1,0:T(8,128)(2,1)S(1)}, u32[]{:S(2)}, u32[]{:S(2)}) %collective-permute-start.4) | collective-permute-done | bytes 393248 | tf_op jit(solution)/shard_map/ppermute | solution.py:44
  44.6 2.9 %collective-permute-start.1 = (bf16[128,1536]{1,0:T(8,128)(2,1)S(1)}, bf16[128,1536]{1,0:T(8,128)(2,1)}, u32[]{:S(2)}, u32[]{:S(2)}) collective-permute-start(bf16[128,1536]{1,0:T(8,128)(2,1)S(1)} %collective-permute-done), channel_id=1, source_target_pairs={{0,6},{1,7},{2,0},{3,1},{4,2},{5,3},{6,4},{7,5},{8,14},{9,15},{10,... | collective-permute-start | bytes 1179656 | tf_op jit(solution)/shard_map/ppermute | solution.py:44
  48.1 4.2 %collective-permute-done.2 = bf16[128,1536]{1,0:T(8,128)(2,1)S(1)} collective-permute-done((bf16[128,1536]{1,0:T(8,128)(2,1)S(1)}, bf16[128,1536]{1,0:T(8,128)(2,1)S(1)}, u32[]{:S(2)}, u32[]{:S(2)}) %collective-permute-start.2) | collective-permute-done | bytes 393248 | tf_op jit(solution)/shard_map/ppermute | solution.py:44
  53.0 2.9 %collective-permute-start.10 = (bf16[128,1536]{1,0:T(8,128)(2,1)S(1)}, bf16[128,1536]{1,0:T(8,128)(2,1)S(1)}, u32[]{:S(2)}, u32[]{:S(2)}) collective-permute-start(bf16[128,1536]{1,0:T(8,128)(2,1)S(1)} %convolution_convert_fusion.1.after), channel_id=1, source_target_pairs={{0,6},{1,7},{2,0},{3,1},{4,2},{5,3},{6,4},{7,5},{8,14},{9,15},{10,... | collective-permute-start | bytes 1179656 | tf_op jit(solution)/shard_map/ppermute | solution.py:44
  56.5 3.2 %shard_map.57.refs_10_ = bf16[2,1536,768]{2,1,0:T(8,128)(2,1)S(1)} custom-call(s32[8]{0:T(128)} %counts.11, s32[128]{0:T(128)} %c_orbitals.7, bf16[8,8,192,768]{3,2,1,0:T(8,128)(2,1)} %refs_8_.3, bf16[8,8,192,768]{3,2,1,0:T(8,128)(2,1)} %collective-permute-done.6.v_other.refs_9_, bf16[128,1536]{1,0:T(8,128)(2,1)} %copy-done), custom_call_target="tpu_custom_call" | custom-call | bytes 9437184 | tf_op jit(solution)/shard_map/pallas_call | solution.py:154
  60.9 1.8 %collective-permute-start.14 = (bf16[128,1536]{1,0:T(8,128)(2,1)S(1)}, bf16[128,1536]{1,0:T(8,128)(2,1)S(1)}, u32[]{:S(2)}, u32[]{:S(2)}) collective-permute-start(bf16[128,1536]{1,0:T(8,128)(2,1)S(1)} %convolution_convert_fusion), channel_id=1, source_target_pairs={{0,6},{1,7},{2,0},{3,1},{4,2},{5,3},{6,4},{7,5},{8,14},{9,15},{10,... | collective-permute-start | bytes 1179656 | tf_op jit(solution)/shard_map/ppermute | solution.py:44
  62.7 11.8 %shard_map.58 = (f32[64,6144]{1,0:T(8,128)}, s16[64,6272]{1,0:T(8,128)(2,1)}, s16[64,6272]{1,0:T(8,128)(2,1)}, s16[64,6272]{1,0:T(8,128)(2,1)}) custom-call(s32[8]{0:T(128)} %counts.11, s32[128]{0:T(128)} %c_orbitals.7, bf16[2,64,1536]{2,1,0:T(8,128)(2,1)} %bitcast.48, bf16[2,64,1536]{2,1,0:T(8,128)(2,1)} %bitcast.52, bf16[2,64,1536]{2,1,0:T(8,128)(2,1)} %bitcast.6.refs_2_, ...), custom_call_target="tpu_custom_call" | custom-call | flops 4831838208 | bytes 18874368 | tf_op jit(solution)/shard_map/pallas_call | solution.py:248
  79.4 2.7 %collective-permute-start.8 = (s16[64,6272]{1,0:T(8,128)(2,1)}, s16[64,6272]{1,0:T(8,128)(2,1)S(1)}, u32[]{:S(2)}, u32[]{:S(2)}) collective-permute-start(s16[64,6272]{1,0:T(8,128)(2,1)} %get-tuple-element.28), channel_id=1, source_target_pairs={{0,16},{1,65},{2,18},{3,67},{4,20},{5,69},{6,22},{7,71},{8,24},{9,... | collective-permute-start | bytes 2408456 | tf_op jit(solution)/shard_map/ppermute | solution.py:44
  83.5 3.1 %shard_map.59.refs_10_ = bf16[2,1536,768]{2,1,0:T(8,128)(2,1)S(1)} custom-call(s32[8]{0:T(128)} %counts.11, s32[128]{0:T(128)} %c_orbitals.7, bf16[8,8,192,768]{3,2,1,0:T(8,128)(2,1)} %refs_8_.3, bf16[8,8,192,768]{3,2,1,0:T(8,128)(2,1)} %collective-permute-done.6.v_other.refs_9_, s16[64,6272]{1,0:T(8,128)(2,1)} %get-tuple-element.27.after), custom_call_target="tpu_custom_call" | custom-call | bytes 9437184 | tf_op jit(solution)/shard_map/pallas_call | solution.py:154
  87.4 10.7 %shard_map.60 = (f32[64,6144]{1,0:T(8,128)}, s16[64,6272]{1,0:T(8,128)(2,1)}, s16[64,6272]{1,0:T(8,128)(2,1)}, s16[64,6272]{1,0:T(8,128)(2,1)}) custom-call(s32[8]{0:T(128)} %counts.11, s32[128]{0:T(128)} %c_orbitals.7, bf16[2,64,1536]{2,1,0:T(8,128)(2,1)S(1)} %bitcast.31, bf16[2,64,1536]{2,1,0:T(8,128)(2,1)S(1)} %bitcast.35, ...), custom_call_target="tpu_custom_call" | custom-call | flops 4831838208 | bytes 18874368 | tf_op jit(solution)/shard_map/pallas_call | solution.py:248
  99.7 2.7 %collective-permute-start.17 = (s16[64,6272]{1,0:T(8,128)(2,1)}, s16[64,6272]{1,0:T(8,128)(2,1)S(1)}, u32[]{:S(2)}, u32[]{:S(2)}) collective-permute-start(s16[64,6272]{1,0:T(8,128)(2,1)} %get-tuple-element.41), channel_id=1, source_target_pairs={{0,16},{1,65},{2,18},{3,67},{4,20},{5,69},{6,22},{7,71},{8,24},{9,... | collective-permute-start | bytes 2408456 | tf_op jit(solution)/shard_map/ppermute | solution.py:44
  104.8 4.3 %shard_map.61 = s16[256,1664]{1,0:T(8,128)(2,1)} custom-call(f32[64,6144]{1,0:T(8,128)} %get-tuple-element.36.own_ref, s16[64,6272]{1,0:T(8,128)(2,1)S(1)} %collective-permute-done.7.q1, s16[64,6272]{1,0:T(8,128)(2,1)S(1)} %collective-permute-done.8.q2, s16[64,6272]{1,0:T(8,128)(2,1)} %copy-done.4), custom_call_target="tpu_custom_call" | custom-call | flops 3145728 | bytes 4718592 | tf_op jit(solution)/shard_map/pallas_call | solution.py:308
  109.1 4.3 %all-to-all-start.2 = ((s16[16,16,1664]{2,1,0:T(8,128)(2,1)}), s16[16,16,1664]{2,1,0:T(8,128)(2,1)S(1)}, u32[]{:S(2)}, u32[]{:S(2)}) async-start(s16[16,16,1664]{2,1,0:T(8,128)(2,1)} %bitcast.45), calls=%async_computation.2 | async-start | bytes 1703936 | tf_op jit(solution)/shard_map/all_to_all | solution.py:418
  114.7 11.5 %collective-permute-done.17.q2 = s16[64,6272]{1,0:T(8,128)(2,1)S(1)} collective-permute-done((s16[64,6272]{1,0:T(8,128)(2,1)}, s16[64,6272]{1,0:T(8,128)(2,1)S(1)}, u32[]{:S(2)}, u32[]{:S(2)}) %collective-permute-start.17) | collective-permute-done | bytes 802848 | tf_op jit(solution)/shard_map/ppermute | solution.py:44
  127.1 4.3 %shard_map.62 = s16[256,1664]{1,0:T(8,128)(2,1)} custom-call(f32[64,6144]{1,0:T(8,128)} %get-tuple-element.35.own_ref, s16[64,6272]{1,0:T(8,128)(2,1)S(1)} %collective-permute-done.16.q1, s16[64,6272]{1,0:T(8,128)(2,1)S(1)} %collective-permute-done.17.q2, s16[64,6272]{1,0:T(8,128)(2,1)} %copy-done.5), custom_call_target="tpu_custom_call" | custom-call | flops 3145728 | bytes 4718592 | tf_op jit(solution)/shard_map/pallas_call | solution.py:308
  131.4 5.6 %all-to-all-start.3 = ((s16[16,16,1664]{2,1,0:T(8,128)(2,1)}), s16[16,16,1664]{2,1,0:T(8,128)(2,1)S(1)}, u32[]{:S(2)}, u32[]{:S(2)}) async-start(s16[16,16,1664]{2,1,0:T(8,128)(2,1)} %bitcast.46), calls=%async_computation.3 | async-start | bytes 1703936 | tf_op jit(solution)/shard_map/all_to_all | solution.py:418
  137.0 11.8 %all-to-all-done.3 = s16[16,16,1664]{2,1,0:T(8,128)(2,1)S(1)} async-done(((s16[16,16,1664]{2,1,0:T(8,128)(2,1)}), s16[16,16,1664]{2,1,0:T(8,128)(2,1)S(1)}, u32[]{:S(2)}, u32[]{:S(2)}) %all-to-all-start.3) | async-done | bytes 852000 | tf_op jit(solution)/shard_map/all_to_all | solution.py:418
  (72 shorter events, 20.7 us)
Async XLA Ops:
  0.0 53.0 %collective-permute-start.6 = (bf16[8,8,192,768]{3,2,1,0:T(8,128)(2,1)}, bf16[8,8,192,768]{3,2,1,0:T(8,128)(2,1)}, u32[]{:S(2)}, u32[]{:S(2)}) collective-permute-start(bf16[8,8,192,768]{3,2,1,0:T(8,128)(2,1)} %refs_8_.3), channel_id=1, source_target_pairs={{0,1},{1,0},{2,3},{3,2},{4,5},{5,4},{6,7},{7,6},{8,9},{9,8},{10,11... | collective-permute-start | bytes 56623112 | tf_op jit(solution)/shard_map/ppermute | solution.py:44
  3.5 23.2 %all-to-all-start = ((bf16[16,16,1536]{2,1,0:T(8,128)(2,1)}), bf16[16,16,1536]{2,1,0:T(8,128)(2,1)S(1)}, u32[]{:S(2)}, u32[]{:S(2)}) async-start(bf16[16,16,1536]{2,1,0:T(8,128)(2,1)} %bitcast.50), calls=%async_computation | async-start | bytes 1572864 | tf_op jit(solution)/shard_map/all_to_all | solution.py:389
  26.7 20.9 %all-to-all-start.1 = ((bf16[16,16,1536]{2,1,0:T(8,128)(2,1)}), bf16[16,16,1536]{2,1,0:T(8,128)(2,1)S(1)}, u32[]{:S(2)}, u32[]{:S(2)}) async-start(bf16[16,16,1536]{2,1,0:T(8,128)(2,1)} %bitcast.49), calls=%async_computation.1 | async-start | bytes 1572864 | tf_op jit(solution)/shard_map/all_to_all | solution.py:389
  30.6 29.1 %copy-start.2 = (bf16[128,1536]{1,0:T(8,128)(2,1)}, bf16[128,1536]{1,0:T(8,128)(2,1)S(1)}, u32[]{:S(2)}) copy-start(bf16[128,1536]{1,0:T(8,128)(2,1)S(1)} %convolution_convert_fusion.2) | copy-start | bytes 1179652
  30.6 13.3 %collective-permute-start.4 = (bf16[128,1536]{1,0:T(8,128)(2,1)S(1)}, bf16[128,1536]{1,0:T(8,128)(2,1)S(1)}, u32[]{:S(2)}, u32[]{:S(2)}) collective-permute-start(bf16[128,1536]{1,0:T(8,128)(2,1)S(1)} %convolution_convert_fusion.2), channel_id=1, source_target_pairs={{0,2},{1,3},{2,4},{3,5},{4,6},{5,7},{6,0},{7,1},{8,10},{9,11},{10,... | collective-permute-start | bytes 1179656 | tf_op jit(solution)/shard_map/ppermute | solution.py:44
  32.5 12.1 %collective-permute-start = (bf16[128,1536]{1,0:T(8,128)(2,1)S(1)}, bf16[128,1536]{1,0:T(8,128)(2,1)S(1)}, u32[]{:S(2)}, u32[]{:S(2)}) collective-permute-start(bf16[128,1536]{1,0:T(8,128)(2,1)S(1)} %convolution_convert_fusion.3), channel_id=1, source_target_pairs={{0,6},{1,7},{2,0},{3,1},{4,2},{5,3},{6,4},{7,5},{8,14},{9,15},{10,... | collective-permute-start | bytes 1179656 | tf_op jit(solution)/shard_map/ppermute | solution.py:44
  34.3 18.1 %collective-permute-start.2 = (bf16[128,1536]{1,0:T(8,128)(2,1)S(1)}, bf16[128,1536]{1,0:T(8,128)(2,1)S(1)}, u32[]{:S(2)}, u32[]{:S(2)}) collective-permute-start(bf16[128,1536]{1,0:T(8,128)(2,1)S(1)} %convolution_convert_fusion.3), channel_id=1, source_target_pairs={{0,2},{1,3},{2,4},{3,5},{4,6},{5,7},{6,0},{7,1},{8,10},{9,11},{10,... | collective-permute-start | bytes 1179656 | tf_op jit(solution)/shard_map/ppermute | solution.py:44
  34.6 18.5 %collective-permute-start.3 = (bf16[128,1536]{1,0:T(8,128)(2,1)S(1)}, bf16[128,1536]{1,0:T(8,128)(2,1)S(1)}, u32[]{:S(2)}, u32[]{:S(2)}) collective-permute-start(bf16[128,1536]{1,0:T(8,128)(2,1)S(1)} %convolution_convert_fusion.2), channel_id=1, source_target_pairs={{0,6},{1,7},{2,0},{3,1},{4,2},{5,3},{6,4},{7,5},{8,14},{9,15},{10,... | collective-permute-start | bytes 1179656 | tf_op jit(solution)/shard_map/ppermute | solution.py:44
  43.9 17.0 %collective-permute-start.5 = (bf16[128,1536]{1,0:T(8,128)(2,1)S(1)}, bf16[128,1536]{1,0:T(8,128)(2,1)}, u32[]{:S(2)}, u32[]{:S(2)}) collective-permute-start(bf16[128,1536]{1,0:T(8,128)(2,1)S(1)} %collective-permute-done.4), channel_id=1, source_target_pairs={{0,2},{1,3},{2,4},{3,5},{4,6},{5,7},{6,0},{7,1},{8,10},{9,11},{10,... | collective-permute-start | bytes 1179656 | tf_op jit(solution)/shard_map/ppermute | solution.py:44
  44.6 18.1 %collective-permute-start.1 = (bf16[128,1536]{1,0:T(8,128)(2,1)S(1)}, bf16[128,1536]{1,0:T(8,128)(2,1)}, u32[]{:S(2)}, u32[]{:S(2)}) collective-permute-start(bf16[128,1536]{1,0:T(8,128)(2,1)S(1)} %collective-permute-done), channel_id=1, source_target_pairs={{0,6},{1,7},{2,0},{3,1},{4,2},{5,3},{6,4},{7,5},{8,14},{9,15},{10,... | collective-permute-start | bytes 1179656 | tf_op jit(solution)/shard_map/ppermute | solution.py:44
  53.0 21.5 %collective-permute-start.10 = (bf16[128,1536]{1,0:T(8,128)(2,1)S(1)}, bf16[128,1536]{1,0:T(8,128)(2,1)S(1)}, u32[]{:S(2)}, u32[]{:S(2)}) collective-permute-start(bf16[128,1536]{1,0:T(8,128)(2,1)S(1)} %convolution_convert_fusion.1.after), channel_id=1, source_target_pairs={{0,6},{1,7},{2,0},{3,1},{4,2},{5,3},{6,4},{7,5},{8,14},{9,15},{10,... | collective-permute-start | bytes 1179656 | tf_op jit(solution)/shard_map/ppermute | solution.py:44
  56.0 23.4 %collective-permute-start.13 = (bf16[128,1536]{1,0:T(8,128)(2,1)S(1)}, bf16[128,1536]{1,0:T(8,128)(2,1)S(1)}, u32[]{:S(2)}, u32[]{:S(2)}) collective-permute-start(bf16[128,1536]{1,0:T(8,128)(2,1)S(1)} %convolution_convert_fusion.1.after), channel_id=1, source_target_pairs={{0,2},{1,3},{2,4},{3,5},{4,6},{5,7},{6,0},{7,1},{8,10},{9,11},{10,... | collective-permute-start | bytes 1179656 | tf_op jit(solution)/shard_map/ppermute | solution.py:44
  56.0 19.7 %collective-permute-start.11 = (bf16[128,1536]{1,0:T(8,128)(2,1)S(1)}, bf16[128,1536]{1,0:T(8,128)(2,1)S(1)}, u32[]{:S(2)}, u32[]{:S(2)}) collective-permute-start(bf16[128,1536]{1,0:T(8,128)(2,1)S(1)} %convolution_convert_fusion), channel_id=1, source_target_pairs={{0,2},{1,3},{2,4},{3,5},{4,6},{5,7},{6,0},{7,1},{8,10},{9,11},{10,... | collective-permute-start | bytes 1179656 | tf_op jit(solution)/shard_map/ppermute | solution.py:44
  60.9 21.2 %collective-permute-start.14 = (bf16[128,1536]{1,0:T(8,128)(2,1)S(1)}, bf16[128,1536]{1,0:T(8,128)(2,1)S(1)}, u32[]{:S(2)}, u32[]{:S(2)}) collective-permute-start(bf16[128,1536]{1,0:T(8,128)(2,1)S(1)} %convolution_convert_fusion), channel_id=1, source_target_pairs={{0,6},{1,7},{2,0},{3,1},{4,2},{5,3},{6,4},{7,5},{8,14},{9,15},{10,... | collective-permute-start | bytes 1179656 | tf_op jit(solution)/shard_map/ppermute | solution.py:44
  75.7 11.0 %collective-permute-start.12 = (bf16[128,1536]{1,0:T(8,128)(2,1)S(1)}, bf16[128,1536]{1,0:T(8,128)(2,1)S(1)}, u32[]{:S(2)}, u32[]{:S(2)}) collective-permute-start(bf16[128,1536]{1,0:T(8,128)(2,1)S(1)} %collective-permute-done.10), channel_id=1, source_target_pairs={{0,6},{1,7},{2,0},{3,1},{4,2},{5,3},{6,4},{7,5},{8,14},{9,15},{10,... | collective-permute-start | bytes 1179656 | tf_op jit(solution)/shard_map/ppermute | solution.py:44
  77.3 10.1 %collective-permute-start.15 = (bf16[128,1536]{1,0:T(8,128)(2,1)S(1)}, bf16[128,1536]{1,0:T(8,128)(2,1)S(1)}, u32[]{:S(2)}, u32[]{:S(2)}) collective-permute-start(bf16[128,1536]{1,0:T(8,128)(2,1)S(1)} %collective-permute-done.11), channel_id=1, source_target_pairs={{0,2},{1,3},{2,4},{3,5},{4,6},{5,7},{6,0},{7,1},{8,10},{9,11},{10,... | collective-permute-start | bytes 1179656 | tf_op jit(solution)/shard_map/ppermute | solution.py:44
  77.7 24.6 %collective-permute-start.7 = (s16[64,6272]{1,0:T(8,128)(2,1)}, s16[64,6272]{1,0:T(8,128)(2,1)S(1)}, u32[]{:S(2)}, u32[]{:S(2)}) collective-permute-start(s16[64,6272]{1,0:T(8,128)(2,1)} %get-tuple-element.27.after), channel_id=1, source_target_pairs={{0,8},{1,33},{2,10},{3,35},{4,12},{5,37},{6,14},{7,39},{8,16},{9,4... | collective-permute-start | bytes 2408456 | tf_op jit(solution)/shard_map/ppermute | solution.py:44
  79.4 24.5 %collective-permute-start.8 = (s16[64,6272]{1,0:T(8,128)(2,1)}, s16[64,6272]{1,0:T(8,128)(2,1)S(1)}, u32[]{:S(2)}, u32[]{:S(2)}) collective-permute-start(s16[64,6272]{1,0:T(8,128)(2,1)} %get-tuple-element.28), channel_id=1, source_target_pairs={{0,16},{1,65},{2,18},{3,67},{4,20},{5,69},{6,22},{7,71},{8,24},{9,... | collective-permute-start | bytes 2408456 | tf_op jit(solution)/shard_map/ppermute | solution.py:44
  82.1 21.8 %collective-permute-start.9 = (s16[64,6272]{1,0:T(8,128)(2,1)}, s16[64,6272]{1,0:T(8,128)(2,1)S(1)}, u32[]{:S(2)}, u32[]{:S(2)}) collective-permute-start(s16[64,6272]{1,0:T(8,128)(2,1)} %get-tuple-element.29), channel_id=1, source_target_pairs={{0,24},{1,97},{2,26},{3,99},{4,28},{5,101},{6,30},{7,103},{8,0},{9... | collective-permute-start | bytes 2408456 | tf_op jit(solution)/shard_map/ppermute | solution.py:44
  98.2 16.5 %collective-permute-start.16 = (s16[64,6272]{1,0:T(8,128)(2,1)}, s16[64,6272]{1,0:T(8,128)(2,1)S(1)}, u32[]{:S(2)}, u32[]{:S(2)}) collective-permute-start(s16[64,6272]{1,0:T(8,128)(2,1)} %get-tuple-element.40), channel_id=1, source_target_pairs={{0,8},{1,33},{2,10},{3,35},{4,12},{5,37},{6,14},{7,39},{8,16},{9,4... | collective-permute-start | bytes 2408456 | tf_op jit(solution)/shard_map/ppermute | solution.py:44
  99.7 26.5 %collective-permute-start.17 = (s16[64,6272]{1,0:T(8,128)(2,1)}, s16[64,6272]{1,0:T(8,128)(2,1)S(1)}, u32[]{:S(2)}, u32[]{:S(2)}) collective-permute-start(s16[64,6272]{1,0:T(8,128)(2,1)} %get-tuple-element.41), channel_id=1, source_target_pairs={{0,16},{1,65},{2,18},{3,67},{4,20},{5,69},{6,22},{7,71},{8,24},{9,... | collective-permute-start | bytes 2408456 | tf_op jit(solution)/shard_map/ppermute | solution.py:44
  102.4 23.8 %collective-permute-start.18 = (s16[64,6272]{1,0:T(8,128)(2,1)}, s16[64,6272]{1,0:T(8,128)(2,1)S(1)}, u32[]{:S(2)}, u32[]{:S(2)}) collective-permute-start(s16[64,6272]{1,0:T(8,128)(2,1)} %get-tuple-element.42), channel_id=1, source_target_pairs={{0,24},{1,97},{2,26},{3,99},{4,28},{5,101},{6,30},{7,103},{8,0},{9... | collective-permute-start | bytes 2408456 | tf_op jit(solution)/shard_map/ppermute | solution.py:44
  109.1 22.3 %all-to-all-start.2 = ((s16[16,16,1664]{2,1,0:T(8,128)(2,1)}), s16[16,16,1664]{2,1,0:T(8,128)(2,1)S(1)}, u32[]{:S(2)}, u32[]{:S(2)}) async-start(s16[16,16,1664]{2,1,0:T(8,128)(2,1)} %bitcast.45), calls=%async_computation.2 | async-start | bytes 1703936 | tf_op jit(solution)/shard_map/all_to_all | solution.py:418
  131.4 17.4 %all-to-all-start.3 = ((s16[16,16,1664]{2,1,0:T(8,128)(2,1)}), s16[16,16,1664]{2,1,0:T(8,128)(2,1)S(1)}, u32[]{:S(2)}, u32[]{:S(2)}) async-start(s16[16,16,1664]{2,1,0:T(8,128)(2,1)} %bitcast.46), calls=%async_computation.3 | async-start | bytes 1703936 | tf_op jit(solution)/shard_map/all_to_all | solution.py:418
  (12 other events, 141.2 us)

commit v4 on v3

--- a/solution.py
+++ b/solution.py
@@ -94,7 +94,7 @@
         limit = sum(jnp.where(block == g, counts[g], 0) for g in range(8))
         keep = slot < limit
         for pair in range(pairs):
-            kept = jnp.where(keep, t_ref[pair, start + p].astype(jnp.float32), 0.0).astype(jnp.bfloat16)
+            kept = jnp.where(keep, t_ref[pair, p].astype(jnp.float32), 0.0).astype(jnp.bfloat16)
             split = lax.dot_general(by_c, kept, (((1,), (1,)), ((), ())), preferred_element_type=jnp.float32)
             split = split.astype(jnp.bfloat16)
             q = pair * count + p
@@ -115,7 +115,7 @@
         in_specs=[
             SMEM,
             pl.BlockSpec((1, c_tot), lambda i: (0, 0)),
-            pl.BlockSpec((rows, 8, dmax, c_tot), lambda i: (0, 0, 0, 0)),
+            pl.BlockSpec((rows, count, dmax, c_tot), lambda i: (0, start // count, 0, 0)),
         ],
         out_specs=pl.BlockSpec((size, 8 * dmax), lambda i: (0, 0)),
         out_shape=jax.ShapeDtypeStruct((size, 8 * dmax), jnp.bfloat16),
@@ -267,7 +267,7 @@
     )(vir_counts, c_orbitals, *arrays, v_own, v_other, *in_vmem([ready]))
 
 
-def sum_kernel(number, own_ref, q1, q2, q3, out, own, q, high, low, sems):
+def sum_kernel(number, own_ref, q1, q2, q3, out, own, q, mixed, sems):
     rows = own.shape[0]
     width = own.shape[1] // number
     tail = slice(number * width, number * width + 128)
@@ -295,11 +295,10 @@
             total += q[k, :, at].astype(jnp.float32) * one
         code, value = code_of(total)
         value = jnp.concatenate([value, jnp.broadcast_to(code, (rows, 128))], axis=1)
-        upper = jnp.round(value * (1.0 / 256.0))
-        high[p * rows:(p + 1) * rows] = upper.astype(jnp.bfloat16)
-        low[p * rows:(p + 1) * rows] = (value - 256.0 * upper).astype(jnp.bfloat16)
-    order = one_hot(number * rows, lambda r: lax.rem(r, number) * rows + lax.div(r, number))
-    out[...] = (pick(order, high[...]) * 256.0 + pick(order, low[...])).astype(jnp.int16)
+        for j in range(mixed.shape[0]):
+            mixed[j, pl.ds(p, rows, number), :] = value[:, j * 128:(j + 1) * 128]
+    for j in range(mixed.shape[0]):
+        out[:, j * 128:(j + 1) * 128] = mixed[j].astype(jnp.int16)
 
 
 def sum_coded(own, parts, number):
@@ -313,8 +312,7 @@
         scratch_shapes=[
             pltpu.VMEM(own.shape, jnp.float32),
             pltpu.VMEM((3,) + parts[0].shape, jnp.int16),
-            pltpu.VMEM((number * rows, width), jnp.bfloat16),
-            pltpu.VMEM((number * rows, width), jnp.bfloat16),
+            pltpu.VMEM((width // 128, number * rows, 128), jnp.float32),
             pltpu.SemaphoreType.DMA((number + 1, 4)),
         ],
         compiler_params=params(LIMIT),
@@ -407,7 +405,7 @@
         ready = load(*operands, starts[chunk], products[-1][1] if chunk else relaid[-1][0])
         products.append(matmul(arrays[:4], arrays[4:], *operands, m, starts[chunk], ready, chunk > 0))
 
-    sent = [[send(q, first(k)) for k, q in enumerate(product) if k] for product in products]
+    sent = [[send(product[k], first(k)) for k in (1, 3, 2)] for product in products]
     results = []
     for chunk, number in enumerate(SPLIT):
         own, parts = products[chunk][0], sent[chunk]

time: 151 us -> 149 us (0.987)
  starting transfers between devices: 50.3 us -> 47.8 us
  waiting for transfers between devices: 49.5 us -> 51.5 us
  Pallas kernels: 45.8 us -> 44.1 us
    ppermute x19, waiting for transfers between devices: 26.2 us -> 28 us  [send(): return lax.ppermute(value, AXES, pairs)]
  transfers between devices with their start and end apart: 23 -> 23, of which waited for: 10 -> 11; matrix products, arithmetic and copies ran while one was open for 2% -> 2% of each run, Pallas kernels for 30% -> 29%
where the time goes in v4:
time: 149 us; the launch traced here: 148 us
  waiting for transfers between devices  51.5 us (35%)
  starting transfers between devices  47.8 us (32%)
  Pallas kernels  44.1 us (30%)
  local copies, waits for them, and re-layouts  2.83 us (2%)
    ppermute x19, waiting for transfers between devices, send(): return lax.ppermute(value, AXES, pairs)  28 us
    ppermute x19, starting transfers between devices, send(): return lax.ppermute(value, AXES, pairs)  27.5 us
    pallas_call x2, Pallas kernels, matmul(): pl.pallas_call(functools.partial(matmul_kernel, m, start), in_specs=[SMEM...  22.5 us
    all_to_all x2, waiting for transfers between devices, shards(): lax.all_to_all(coded, AXES, split_axis=0, concat_axis=0, tiled=True, axis...  11.8 us
    all_to_all x2, starting transfers between devices, shards(): lax.all_to_all(piece, 'slab', split_axis=0, concat_axis=0, tiled=True)  11.7 us
    all_to_all x2, waiting for transfers between devices, shards(): lax.all_to_all(piece, 'slab', split_axis=0, concat_axis=0, tiled=True)  11.7 us
    all_to_all x2, starting transfers between devices, shards(): lax.all_to_all(coded, AXES, split_axis=0, concat_axis=0, tiled=True, axis...  8.61 us
    pallas_call x2, Pallas kernels, sum_coded(): pl.pallas_call(functools.partial(sum_kernel, number), in_specs=[HBM] * 4,...  7.47 us
  transfers between devices with their start and end apart: 23, of which 11 were waited for; matrix products, arithmetic and copies ran while one was open for 2% of the time, Pallas kernels for 29%

profile of v4, /device:TPU:0, one launch (start us, length us, event | category | flops | bytes accessed | tf_op | source)
XLA Modules:
  0.0 148.1 jit_solution(11235760627606790904)
XLA Ops:
  0.0 3.2 %shard_map.55 = bf16[256,1536]{1,0:T(8,128)(2,1)} custom-call(s32[8]{0:T(128)} %counts.11, s32[1,128]{1,0:T(1,128)} %bitcast.55, bf16[4,8,192,128]{3,2,1,0:T(8,128)(2,1)} %bitcast.57), custom_call_target="tpu_custom_call" | custom-call | flops 2000000000 | bytes 4000000 | tf_op jit(solution)/shard_map/pallas_call | solution.py:112
  3.2 8.1 %all-to-all-start = ((bf16[16,16,1536]{2,1,0:T(8,128)(2,1)}), bf16[16,16,1536]{2,1,0:T(8,128)(2,1)S(1)}, u32[]{:S(2)}, u32[]{:S(2)}) async-start(bf16[16,16,1536]{2,1,0:T(8,128)(2,1)} %bitcast.50), calls=%async_computation | async-start | bytes 1572864 | tf_op jit(solution)/shard_map/all_to_all | solution.py:387
  11.4 3.2 %shard_map.56 = bf16[256,1536]{1,0:T(8,128)(2,1)} custom-call(s32[8]{0:T(128)} %counts.11, s32[1,128]{1,0:T(1,128)} %bitcast.56, bf16[4,8,192,128]{3,2,1,0:T(8,128)(2,1)} %bitcast.58), custom_call_target="tpu_custom_call" | custom-call | flops 2000000000 | bytes 4000000 | tf_op jit(solution)/shard_map/pallas_call | solution.py:112
  14.7 11.7 %all-to-all-done = bf16[16,16,1536]{2,1,0:T(8,128)(2,1)S(1)} async-done(((bf16[16,16,1536]{2,1,0:T(8,128)(2,1)}), bf16[16,16,1536]{2,1,0:T(8,128)(2,1)S(1)}, u32[]{:S(2)}, u32[]{:S(2)}) %all-to-all-start) | async-done | bytes 786464 | tf_op jit(solution)/shard_map/all_to_all | solution.py:387
  26.4 3.6 %all-to-all-start.1 = ((bf16[16,16,1536]{2,1,0:T(8,128)(2,1)}), bf16[16,16,1536]{2,1,0:T(8,128)(2,1)S(1)}, u32[]{:S(2)}, u32[]{:S(2)}) async-start(bf16[16,16,1536]{2,1,0:T(8,128)(2,1)} %bitcast.49), calls=%async_computation.1 | async-start | bytes 1572864 | tf_op jit(solution)/shard_map/all_to_all | solution.py:387
  32.2 1.8 %collective-permute-start = (bf16[128,1536]{1,0:T(8,128)(2,1)S(1)}, bf16[128,1536]{1,0:T(8,128)(2,1)S(1)}, u32[]{:S(2)}, u32[]{:S(2)}) collective-permute-start(bf16[128,1536]{1,0:T(8,128)(2,1)S(1)} %convolution_convert_fusion.3), channel_id=1, source_target_pairs={{0,6},{1,7},{2,0},{3,1},{4,2},{5,3},{6,4},{7,5},{8,14},{9,15},{10,... | collective-permute-start | bytes 1179656 | tf_op jit(solution)/shard_map/ppermute | solution.py:44
  34.3 3.0 %collective-permute-start.3 = (bf16[128,1536]{1,0:T(8,128)(2,1)S(1)}, bf16[128,1536]{1,0:T(8,128)(2,1)S(1)}, u32[]{:S(2)}, u32[]{:S(2)}) collective-permute-start(bf16[128,1536]{1,0:T(8,128)(2,1)S(1)} %convolution_convert_fusion.2), channel_id=1, source_target_pairs={{0,6},{1,7},{2,0},{3,1},{4,2},{5,3},{6,4},{7,5},{8,14},{9,15},{10,... | collective-permute-start | bytes 1179656 | tf_op jit(solution)/shard_map/ppermute | solution.py:44
  37.2 6.4 %collective-permute-done.4 = bf16[128,1536]{1,0:T(8,128)(2,1)S(1)} collective-permute-done((bf16[128,1536]{1,0:T(8,128)(2,1)S(1)}, bf16[128,1536]{1,0:T(8,128)(2,1)S(1)}, u32[]{:S(2)}, u32[]{:S(2)}) %collective-permute-start.4) | collective-permute-done | bytes 393248 | tf_op jit(solution)/shard_map/ppermute | solution.py:44
  44.3 3.0 %collective-permute-start.1 = (bf16[128,1536]{1,0:T(8,128)(2,1)S(1)}, bf16[128,1536]{1,0:T(8,128)(2,1)}, u32[]{:S(2)}, u32[]{:S(2)}) collective-permute-start(bf16[128,1536]{1,0:T(8,128)(2,1)S(1)} %collective-permute-done), channel_id=1, source_target_pairs={{0,6},{1,7},{2,0},{3,1},{4,2},{5,3},{6,4},{7,5},{8,14},{9,15},{10,... | collective-permute-start | bytes 1179656 | tf_op jit(solution)/shard_map/ppermute | solution.py:44
  47.9 4.2 %collective-permute-done.2 = bf16[128,1536]{1,0:T(8,128)(2,1)S(1)} collective-permute-done((bf16[128,1536]{1,0:T(8,128)(2,1)S(1)}, bf16[128,1536]{1,0:T(8,128)(2,1)S(1)}, u32[]{:S(2)}, u32[]{:S(2)}) %collective-permute-start.2) | collective-permute-done | bytes 393248 | tf_op jit(solution)/shard_map/ppermute | solution.py:44
  52.7 3.0 %collective-permute-start.10 = (bf16[128,1536]{1,0:T(8,128)(2,1)S(1)}, bf16[128,1536]{1,0:T(8,128)(2,1)S(1)}, u32[]{:S(2)}, u32[]{:S(2)}) collective-permute-start(bf16[128,1536]{1,0:T(8,128)(2,1)S(1)} %convolution_convert_fusion.1.after), channel_id=1, source_target_pairs={{0,6},{1,7},{2,0},{3,1},{4,2},{5,3},{6,4},{7,5},{8,14},{9,15},{10,... | collective-permute-start | bytes 1179656 | tf_op jit(solution)/shard_map/ppermute | solution.py:44
  56.2 3.2 %shard_map.57.refs_10_ = bf16[2,1536,768]{2,1,0:T(8,128)(2,1)S(1)} custom-call(s32[8]{0:T(128)} %counts.11, s32[128]{0:T(128)} %c_orbitals.7, bf16[8,8,192,768]{3,2,1,0:T(8,128)(2,1)} %refs_8_.3, bf16[8,8,192,768]{3,2,1,0:T(8,128)(2,1)} %collective-permute-done.6.v_other.refs_9_, bf16[128,1536]{1,0:T(8,128)(2,1)} %copy-done), custom_call_target="tpu_custom_call" | custom-call | bytes 9437184 | tf_op jit(solution)/shard_map/pallas_call | solution.py:154
  60.6 1.8 %collective-permute-start.14 = (bf16[128,1536]{1,0:T(8,128)(2,1)S(1)}, bf16[128,1536]{1,0:T(8,128)(2,1)S(1)}, u32[]{:S(2)}, u32[]{:S(2)}) collective-permute-start(bf16[128,1536]{1,0:T(8,128)(2,1)S(1)} %convolution_convert_fusion), channel_id=1, source_target_pairs={{0,6},{1,7},{2,0},{3,1},{4,2},{5,3},{6,4},{7,5},{8,14},{9,15},{10,... | collective-permute-start | bytes 1179656 | tf_op jit(solution)/shard_map/ppermute | solution.py:44
  62.5 11.8 %shard_map.58 = (f32[64,6144]{1,0:T(8,128)}, s16[64,6272]{1,0:T(8,128)(2,1)}, s16[64,6272]{1,0:T(8,128)(2,1)}, s16[64,6272]{1,0:T(8,128)(2,1)}) custom-call(s32[8]{0:T(128)} %counts.11, s32[128]{0:T(128)} %c_orbitals.7, bf16[2,64,1536]{2,1,0:T(8,128)(2,1)} %bitcast.48, bf16[2,64,1536]{2,1,0:T(8,128)(2,1)} %bitcast.52, bf16[2,64,1536]{2,1,0:T(8,128)(2,1)} %bitcast.6.refs_2_, ...), custom_call_target="tpu_custom_call" | custom-call | flops 4831838208 | bytes 18874368 | tf_op jit(solution)/shard_map/pallas_call | solution.py:248
  80.7 1.9 %collective-permute-start.9 = (s16[64,6272]{1,0:T(8,128)(2,1)}, s16[64,6272]{1,0:T(8,128)(2,1)S(1)}, u32[]{:S(2)}, u32[]{:S(2)}) collective-permute-start(s16[64,6272]{1,0:T(8,128)(2,1)} %get-tuple-element.29), channel_id=1, source_target_pairs={{0,16},{1,65},{2,18},{3,67},{4,20},{5,69},{6,22},{7,71},{8,24},{9,... | collective-permute-start | bytes 2408456 | tf_op jit(solution)/shard_map/ppermute | solution.py:44
  82.7 3.1 %shard_map.59.refs_10_ = bf16[2,1536,768]{2,1,0:T(8,128)(2,1)S(1)} custom-call(s32[8]{0:T(128)} %counts.11, s32[128]{0:T(128)} %c_orbitals.7, bf16[8,8,192,768]{3,2,1,0:T(8,128)(2,1)} %refs_8_.3, bf16[8,8,192,768]{3,2,1,0:T(8,128)(2,1)} %collective-permute-done.6.v_other.refs_9_, s16[64,6272]{1,0:T(8,128)(2,1)} %get-tuple-element.27.after), custom_call_target="tpu_custom_call" | custom-call | bytes 9437184 | tf_op jit(solution)/shard_map/pallas_call | solution.py:154
  87.1 10.7 %shard_map.60 = (f32[64,6144]{1,0:T(8,128)}, s16[64,6272]{1,0:T(8,128)(2,1)}, s16[64,6272]{1,0:T(8,128)(2,1)}, s16[64,6272]{1,0:T(8,128)(2,1)}) custom-call(s32[8]{0:T(128)} %counts.11, s32[128]{0:T(128)} %c_orbitals.7, bf16[2,64,1536]{2,1,0:T(8,128)(2,1)S(1)} %bitcast.31, bf16[2,64,1536]{2,1,0:T(8,128)(2,1)S(1)} %bitcast.35, ...), custom_call_target="tpu_custom_call" | custom-call | flops 4831838208 | bytes 18874368 | tf_op jit(solution)/shard_map/pallas_call | solution.py:248
  101.2 1.8 %collective-permute-start.18 = (s16[64,6272]{1,0:T(8,128)(2,1)}, s16[64,6272]{1,0:T(8,128)(2,1)S(1)}, u32[]{:S(2)}, u32[]{:S(2)}) collective-permute-start(s16[64,6272]{1,0:T(8,128)(2,1)} %get-tuple-element.42), channel_id=1, source_target_pairs={{0,16},{1,65},{2,18},{3,67},{4,20},{5,69},{6,22},{7,71},{8,24},{9,... | collective-permute-start | bytes 2408456 | tf_op jit(solution)/shard_map/ppermute | solution.py:44
  103.9 3.7 %shard_map.61 = s16[256,1664]{1,0:T(8,128)(2,1)} custom-call(f32[64,6144]{1,0:T(8,128)} %get-tuple-element.36.own_ref, s16[64,6272]{1,0:T(8,128)(2,1)S(1)} %collective-permute-done.7.q1, s16[64,6272]{1,0:T(8,128)(2,1)S(1)} %collective-permute-done.8.q2, s16[64,6272]{1,0:T(8,128)(2,1)} %copy-done.4), custom_call_target="tpu_custom_call" | custom-call | flops 3145728 | bytes 4718592 | tf_op jit(solution)/shard_map/pallas_call | solution.py:307
  107.6 4.3 %all-to-all-start.2 = ((s16[16,16,1664]{2,1,0:T(8,128)(2,1)}), s16[16,16,1664]{2,1,0:T(8,128)(2,1)S(1)}, u32[]{:S(2)}, u32[]{:S(2)}) async-start(s16[16,16,1664]{2,1,0:T(8,128)(2,1)} %bitcast.45), calls=%async_computation.2 | async-start | bytes 1703936 | tf_op jit(solution)/shard_map/all_to_all | solution.py:416
  114.1 11.8 %collective-permute-done.18.q3 = s16[64,6272]{1,0:T(8,128)(2,1)S(1)} collective-permute-done((s16[64,6272]{1,0:T(8,128)(2,1)}, s16[64,6272]{1,0:T(8,128)(2,1)S(1)}, u32[]{:S(2)}, u32[]{:S(2)}) %collective-permute-start.18) | collective-permute-done | bytes 802848 | tf_op jit(solution)/shard_map/ppermute | solution.py:44
  126.8 3.7 %shard_map.62 = s16[256,1664]{1,0:T(8,128)(2,1)} custom-call(f32[64,6144]{1,0:T(8,128)} %get-tuple-element.35.own_ref, s16[64,6272]{1,0:T(8,128)(2,1)S(1)} %collective-permute-done.16.q1, s16[64,6272]{1,0:T(8,128)(2,1)S(1)} %collective-permute-done.17.q2, s16[64,6272]{1,0:T(8,128)(2,1)} %copy-done.5), custom_call_target="tpu_custom_call" | custom-call | flops 3145728 | bytes 4718592 | tf_op jit(solution)/shard_map/pallas_call | solution.py:307
  130.6 4.3 %all-to-all-start.3 = ((s16[16,16,1664]{2,1,0:T(8,128)(2,1)}), s16[16,16,1664]{2,1,0:T(8,128)(2,1)S(1)}, u32[]{:S(2)}, u32[]{:S(2)}) async-start(s16[16,16,1664]{2,1,0:T(8,128)(2,1)} %bitcast.46), calls=%async_computation.3 | async-start | bytes 1703936 | tf_op jit(solution)/shard_map/all_to_all | solution.py:416
  134.9 11.8 %all-to-all-done.3 = s16[16,16,1664]{2,1,0:T(8,128)(2,1)S(1)} async-done(((s16[16,16,1664]{2,1,0:T(8,128)(2,1)}), s16[16,16,1664]{2,1,0:T(8,128)(2,1)S(1)}, u32[]{:S(2)}, u32[]{:S(2)}) %all-to-all-start.3) | async-done | bytes 852000 | tf_op jit(solution)/shard_map/all_to_all | solution.py:416
  (72 shorter events, 22.5 us)
Async XLA Ops:
  0.0 52.7 %collective-permute-start.6 = (bf16[8,8,192,768]{3,2,1,0:T(8,128)(2,1)}, bf16[8,8,192,768]{3,2,1,0:T(8,128)(2,1)}, u32[]{:S(2)}, u32[]{:S(2)}) collective-permute-start(bf16[8,8,192,768]{3,2,1,0:T(8,128)(2,1)} %refs_8_.3), channel_id=1, source_target_pairs={{0,1},{1,0},{2,3},{3,2},{4,5},{5,4},{6,7},{7,6},{8,9},{9,8},{10,11... | collective-permute-start | bytes 56623112 | tf_op jit(solution)/shard_map/ppermute | solution.py:44
  3.2 23.2 %all-to-all-start = ((bf16[16,16,1536]{2,1,0:T(8,128)(2,1)}), bf16[16,16,1536]{2,1,0:T(8,128)(2,1)S(1)}, u32[]{:S(2)}, u32[]{:S(2)}) async-start(bf16[16,16,1536]{2,1,0:T(8,128)(2,1)} %bitcast.50), calls=%async_computation | async-start | bytes 1572864 | tf_op jit(solution)/shard_map/all_to_all | solution.py:387
  26.4 20.9 %all-to-all-start.1 = ((bf16[16,16,1536]{2,1,0:T(8,128)(2,1)}), bf16[16,16,1536]{2,1,0:T(8,128)(2,1)S(1)}, u32[]{:S(2)}, u32[]{:S(2)}) async-start(bf16[16,16,1536]{2,1,0:T(8,128)(2,1)} %bitcast.49), calls=%async_computation.1 | async-start | bytes 1572864 | tf_op jit(solution)/shard_map/all_to_all | solution.py:387
  30.3 29.1 %copy-start.2 = (bf16[128,1536]{1,0:T(8,128)(2,1)}, bf16[128,1536]{1,0:T(8,128)(2,1)S(1)}, u32[]{:S(2)}) copy-start(bf16[128,1536]{1,0:T(8,128)(2,1)S(1)} %convolution_convert_fusion.2) | copy-start | bytes 1179652
  30.3 13.3 %collective-permute-start.4 = (bf16[128,1536]{1,0:T(8,128)(2,1)S(1)}, bf16[128,1536]{1,0:T(8,128)(2,1)S(1)}, u32[]{:S(2)}, u32[]{:S(2)}) collective-permute-start(bf16[128,1536]{1,0:T(8,128)(2,1)S(1)} %convolution_convert_fusion.2), channel_id=1, source_target_pairs={{0,2},{1,3},{2,4},{3,5},{4,6},{5,7},{6,0},{7,1},{8,10},{9,11},{10,... | collective-permute-start | bytes 1179656 | tf_op jit(solution)/shard_map/ppermute | solution.py:44
  32.2 12.1 %collective-permute-start = (bf16[128,1536]{1,0:T(8,128)(2,1)S(1)}, bf16[128,1536]{1,0:T(8,128)(2,1)S(1)}, u32[]{:S(2)}, u32[]{:S(2)}) collective-permute-start(bf16[128,1536]{1,0:T(8,128)(2,1)S(1)} %convolution_convert_fusion.3), channel_id=1, source_target_pairs={{0,6},{1,7},{2,0},{3,1},{4,2},{5,3},{6,4},{7,5},{8,14},{9,15},{10,... | collective-permute-start | bytes 1179656 | tf_op jit(solution)/shard_map/ppermute | solution.py:44
  34.0 18.1 %collective-permute-start.2 = (bf16[128,1536]{1,0:T(8,128)(2,1)S(1)}, bf16[128,1536]{1,0:T(8,128)(2,1)S(1)}, u32[]{:S(2)}, u32[]{:S(2)}) collective-permute-start(bf16[128,1536]{1,0:T(8,128)(2,1)S(1)} %convolution_convert_fusion.3), channel_id=1, source_target_pairs={{0,2},{1,3},{2,4},{3,5},{4,6},{5,7},{6,0},{7,1},{8,10},{9,11},{10,... | collective-permute-start | bytes 1179656 | tf_op jit(solution)/shard_map/ppermute | solution.py:44
  34.3 18.5 %collective-permute-start.3 = (bf16[128,1536]{1,0:T(8,128)(2,1)S(1)}, bf16[128,1536]{1,0:T(8,128)(2,1)S(1)}, u32[]{:S(2)}, u32[]{:S(2)}) collective-permute-start(bf16[128,1536]{1,0:T(8,128)(2,1)S(1)} %convolution_convert_fusion.2), channel_id=1, source_target_pairs={{0,6},{1,7},{2,0},{3,1},{4,2},{5,3},{6,4},{7,5},{8,14},{9,15},{10,... | collective-permute-start | bytes 1179656 | tf_op jit(solution)/shard_map/ppermute | solution.py:44
  43.7 17.0 %collective-permute-start.5 = (bf16[128,1536]{1,0:T(8,128)(2,1)S(1)}, bf16[128,1536]{1,0:T(8,128)(2,1)}, u32[]{:S(2)}, u32[]{:S(2)}) collective-permute-start(bf16[128,1536]{1,0:T(8,128)(2,1)S(1)} %collective-permute-done.4), channel_id=1, source_target_pairs={{0,2},{1,3},{2,4},{3,5},{4,6},{5,7},{6,0},{7,1},{8,10},{9,11},{10,... | collective-permute-start | bytes 1179656 | tf_op jit(solution)/shard_map/ppermute | solution.py:44
  44.3 18.2 %collective-permute-start.1 = (bf16[128,1536]{1,0:T(8,128)(2,1)S(1)}, bf16[128,1536]{1,0:T(8,128)(2,1)}, u32[]{:S(2)}, u32[]{:S(2)}) collective-permute-start(bf16[128,1536]{1,0:T(8,128)(2,1)S(1)} %collective-permute-done), channel_id=1, source_target_pairs={{0,6},{1,7},{2,0},{3,1},{4,2},{5,3},{6,4},{7,5},{8,14},{9,15},{10,... | collective-permute-start | bytes 1179656 | tf_op jit(solution)/shard_map/ppermute | solution.py:44
  52.7 21.5 %collective-permute-start.10 = (bf16[128,1536]{1,0:T(8,128)(2,1)S(1)}, bf16[128,1536]{1,0:T(8,128)(2,1)S(1)}, u32[]{:S(2)}, u32[]{:S(2)}) collective-permute-start(bf16[128,1536]{1,0:T(8,128)(2,1)S(1)} %convolution_convert_fusion.1.after), channel_id=1, source_target_pairs={{0,6},{1,7},{2,0},{3,1},{4,2},{5,3},{6,4},{7,5},{8,14},{9,15},{10,... | collective-permute-start | bytes 1179656 | tf_op jit(solution)/shard_map/ppermute | solution.py:44
  55.7 23.4 %collective-permute-start.13 = (bf16[128,1536]{1,0:T(8,128)(2,1)S(1)}, bf16[128,1536]{1,0:T(8,128)(2,1)S(1)}, u32[]{:S(2)}, u32[]{:S(2)}) collective-permute-start(bf16[128,1536]{1,0:T(8,128)(2,1)S(1)} %convolution_convert_fusion.1.after), channel_id=1, source_target_pairs={{0,2},{1,3},{2,4},{3,5},{4,6},{5,7},{6,0},{7,1},{8,10},{9,11},{10,... | collective-permute-start | bytes 1179656 | tf_op jit(solution)/shard_map/ppermute | solution.py:44
  55.7 19.7 %collective-permute-start.11 = (bf16[128,1536]{1,0:T(8,128)(2,1)S(1)}, bf16[128,1536]{1,0:T(8,128)(2,1)S(1)}, u32[]{:S(2)}, u32[]{:S(2)}) collective-permute-start(bf16[128,1536]{1,0:T(8,128)(2,1)S(1)} %convolution_convert_fusion), channel_id=1, source_target_pairs={{0,2},{1,3},{2,4},{3,5},{4,6},{5,7},{6,0},{7,1},{8,10},{9,11},{10,... | collective-permute-start | bytes 1179656 | tf_op jit(solution)/shard_map/ppermute | solution.py:44
  60.6 20.1 %collective-permute-start.14 = (bf16[128,1536]{1,0:T(8,128)(2,1)S(1)}, bf16[128,1536]{1,0:T(8,128)(2,1)S(1)}, u32[]{:S(2)}, u32[]{:S(2)}) collective-permute-start(bf16[128,1536]{1,0:T(8,128)(2,1)S(1)} %convolution_convert_fusion), channel_id=1, source_target_pairs={{0,6},{1,7},{2,0},{3,1},{4,2},{5,3},{6,4},{7,5},{8,14},{9,15},{10,... | collective-permute-start | bytes 1179656 | tf_op jit(solution)/shard_map/ppermute | solution.py:44
  75.5 10.4 %collective-permute-start.12 = (bf16[128,1536]{1,0:T(8,128)(2,1)S(1)}, bf16[128,1536]{1,0:T(8,128)(2,1)S(1)}, u32[]{:S(2)}, u32[]{:S(2)}) collective-permute-start(bf16[128,1536]{1,0:T(8,128)(2,1)S(1)} %collective-permute-done.10), channel_id=1, source_target_pairs={{0,6},{1,7},{2,0},{3,1},{4,2},{5,3},{6,4},{7,5},{8,14},{9,15},{10,... | collective-permute-start | bytes 1179656 | tf_op jit(solution)/shard_map/ppermute | solution.py:44
  77.0 10.1 %collective-permute-start.15 = (bf16[128,1536]{1,0:T(8,128)(2,1)S(1)}, bf16[128,1536]{1,0:T(8,128)(2,1)S(1)}, u32[]{:S(2)}, u32[]{:S(2)}) collective-permute-start(bf16[128,1536]{1,0:T(8,128)(2,1)S(1)} %collective-permute-done.11), channel_id=1, source_target_pairs={{0,2},{1,3},{2,4},{3,5},{4,6},{5,7},{6,0},{7,1},{8,10},{9,11},{10,... | collective-permute-start | bytes 1179656 | tf_op jit(solution)/shard_map/ppermute | solution.py:44
  77.5 23.7 %collective-permute-start.7 = (s16[64,6272]{1,0:T(8,128)(2,1)}, s16[64,6272]{1,0:T(8,128)(2,1)S(1)}, u32[]{:S(2)}, u32[]{:S(2)}) collective-permute-start(s16[64,6272]{1,0:T(8,128)(2,1)} %get-tuple-element.27.after), channel_id=1, source_target_pairs={{0,8},{1,33},{2,10},{3,35},{4,12},{5,37},{6,14},{7,39},{8,16},{9,4... | collective-permute-start | bytes 2408456 | tf_op jit(solution)/shard_map/ppermute | solution.py:44
  79.1 23.9 %collective-permute-start.8 = (s16[64,6272]{1,0:T(8,128)(2,1)}, s16[64,6272]{1,0:T(8,128)(2,1)S(1)}, u32[]{:S(2)}, u32[]{:S(2)}) collective-permute-start(s16[64,6272]{1,0:T(8,128)(2,1)} %get-tuple-element.28), channel_id=1, source_target_pairs={{0,24},{1,97},{2,26},{3,99},{4,28},{5,101},{6,30},{7,103},{8,0},{9... | collective-permute-start | bytes 2408456 | tf_op jit(solution)/shard_map/ppermute | solution.py:44
  80.7 22.3 %collective-permute-start.9 = (s16[64,6272]{1,0:T(8,128)(2,1)}, s16[64,6272]{1,0:T(8,128)(2,1)S(1)}, u32[]{:S(2)}, u32[]{:S(2)}) collective-permute-start(s16[64,6272]{1,0:T(8,128)(2,1)} %get-tuple-element.29), channel_id=1, source_target_pairs={{0,16},{1,65},{2,18},{3,67},{4,20},{5,69},{6,22},{7,71},{8,24},{9,... | collective-permute-start | bytes 2408456 | tf_op jit(solution)/shard_map/ppermute | solution.py:44
  97.9 15.3 %collective-permute-start.16 = (s16[64,6272]{1,0:T(8,128)(2,1)}, s16[64,6272]{1,0:T(8,128)(2,1)S(1)}, u32[]{:S(2)}, u32[]{:S(2)}) collective-permute-start(s16[64,6272]{1,0:T(8,128)(2,1)} %get-tuple-element.40), channel_id=1, source_target_pairs={{0,8},{1,33},{2,10},{3,35},{4,12},{5,37},{6,14},{7,39},{8,16},{9,4... | collective-permute-start | bytes 2408456 | tf_op jit(solution)/shard_map/ppermute | solution.py:44
  99.5 14.7 %collective-permute-start.17 = (s16[64,6272]{1,0:T(8,128)(2,1)}, s16[64,6272]{1,0:T(8,128)(2,1)S(1)}, u32[]{:S(2)}, u32[]{:S(2)}) collective-permute-start(s16[64,6272]{1,0:T(8,128)(2,1)} %get-tuple-element.41), channel_id=1, source_target_pairs={{0,24},{1,97},{2,26},{3,99},{4,28},{5,101},{6,30},{7,103},{8,0},{9... | collective-permute-start | bytes 2408456 | tf_op jit(solution)/shard_map/ppermute | solution.py:44
  101.2 24.7 %collective-permute-start.18 = (s16[64,6272]{1,0:T(8,128)(2,1)}, s16[64,6272]{1,0:T(8,128)(2,1)S(1)}, u32[]{:S(2)}, u32[]{:S(2)}) collective-permute-start(s16[64,6272]{1,0:T(8,128)(2,1)} %get-tuple-element.42), channel_id=1, source_target_pairs={{0,16},{1,65},{2,18},{3,67},{4,20},{5,69},{6,22},{7,71},{8,24},{9,... | collective-permute-start | bytes 2408456 | tf_op jit(solution)/shard_map/ppermute | solution.py:44
  107.6 22.9 %all-to-all-start.2 = ((s16[16,16,1664]{2,1,0:T(8,128)(2,1)}), s16[16,16,1664]{2,1,0:T(8,128)(2,1)S(1)}, u32[]{:S(2)}, u32[]{:S(2)}) async-start(s16[16,16,1664]{2,1,0:T(8,128)(2,1)} %bitcast.45), calls=%async_computation.2 | async-start | bytes 1703936 | tf_op jit(solution)/shard_map/all_to_all | solution.py:416
  130.6 16.2 %all-to-all-start.3 = ((s16[16,16,1664]{2,1,0:T(8,128)(2,1)}), s16[16,16,1664]{2,1,0:T(8,128)(2,1)S(1)}, u32[]{:S(2)}, u32[]{:S(2)}) async-start(s16[16,16,1664]{2,1,0:T(8,128)(2,1)} %bitcast.46), calls=%async_computation.3 | async-start | bytes 1703936 | tf_op jit(solution)/shard_map/all_to_all | solution.py:416
  (12 other events, 139.1 us)

commit v5 on v4

--- a/solution.py
+++ b/solution.py
@@ -8,7 +8,7 @@
 from jax.sharding import PartitionSpec as P
 
 SPLIT = (4, 4)
-TOP = 32766.0
+TOP = 32700.0
 FINE = 256.0
 AXES = ("slab", "pair")
 MIB = 2**20
@@ -67,7 +67,7 @@
 
 
 def code_of(part):
-    peak = jnp.maximum(jnp.max(jnp.abs(part), axis=1, keepdims=True), 2.0**-100)
+    peak = jnp.maximum(jnp.max(jnp.abs(part), axis=1, keepdims=True), 2.0**-110)
     code = jnp.ceil(jnp.log2(peak) * FINE)
     return code, jnp.round(part * (jnp.exp2(code * (-1.0 / FINE)) * TOP))
 
@@ -317,7 +317,7 @@
         ],
         compiler_params=params(LIMIT),
         cost_estimate=cost(8 * own.size, 12 * own.size),
-    )(own, *parts)
+    )(own, *in_vmem(parts))
 
 
 def final_kernel(allow, *refs):

time: 149 us -> 148 us (level)
  local copies, waits for them, and re-layouts: 2.83 us -> 0.35 us
  waiting for transfers between devices: 51.5 us -> 53 us
    unnamed x26 -> x20, local copies, waits for them, and re-layouts: 1.84 us -> 0.05 us
    ppermute x19, waiting for transfers between devices: 28 us -> 29.5 us  [send(): return lax.ppermute(value, AXES, pairs)]
  transfers between devices with their start and end apart: 23 -> 23, of which waited for: 11 -> 12; matrix products, arithmetic and copies ran while one was open for 2% -> 1% of each run, Pallas kernels for 29% -> 29%
where the time goes in v5:
time: 148 us; the launch traced here: 147 us
  waiting for transfers between devices  53 us (36%)
  starting transfers between devices  47.8 us (32%)
  Pallas kernels  44.1 us (30%)
    ppermute x19, waiting for transfers between devices, send(): return lax.ppermute(value, AXES, pairs)  29.5 us
    ppermute x19, starting transfers between devices, send(): return lax.ppermute(value, AXES, pairs)  27.5 us
    pallas_call x2, Pallas kernels, matmul(): pl.pallas_call(functools.partial(matmul_kernel, m, start), in_specs=[SMEM...  22.4 us
    all_to_all x2, waiting for transfers between devices, shards(): lax.all_to_all(coded, AXES, split_axis=0, concat_axis=0, tiled=True, axis...  11.8 us
    all_to_all x2, starting transfers between devices, shards(): lax.all_to_all(piece, 'slab', split_axis=0, concat_axis=0, tiled=True)  11.7 us
    all_to_all x2, waiting for transfers between devices, shards(): lax.all_to_all(piece, 'slab', split_axis=0, concat_axis=0, tiled=True)  11.7 us
    all_to_all x2, starting transfers between devices, shards(): lax.all_to_all(coded, AXES, split_axis=0, concat_axis=0, tiled=True, axis...  8.54 us
    pallas_call x2, Pallas kernels, sum_coded(): pl.pallas_call(functools.partial(sum_kernel, number), in_specs=[HBM] * 4,...  7.52 us
  transfers between devices with their start and end apart: 23, of which 12 were waited for; matrix products, arithmetic and copies ran while one was open for 1% of the time, Pallas kernels for 29%

profile of v5, /device:TPU:0, one launch (start us, length us, event | category | flops | bytes accessed | tf_op | source)
XLA Modules:
  0.0 147.0 jit_solution(452367951681042192)
XLA Ops:
  0.0 3.2 %shard_map.55 = bf16[256,1536]{1,0:T(8,128)(2,1)} custom-call(s32[8]{0:T(128)} %counts.11, s32[1,128]{1,0:T(1,128)} %bitcast.55, bf16[4,8,192,128]{3,2,1,0:T(8,128)(2,1)} %bitcast.57), custom_call_target="tpu_custom_call" | custom-call | flops 2000000000 | bytes 4000000 | tf_op jit(solution)/shard_map/pallas_call | solution.py:112
  3.2 8.1 %all-to-all-start = ((bf16[16,16,1536]{2,1,0:T(8,128)(2,1)}), bf16[16,16,1536]{2,1,0:T(8,128)(2,1)S(1)}, u32[]{:S(2)}, u32[]{:S(2)}) async-start(bf16[16,16,1536]{2,1,0:T(8,128)(2,1)} %bitcast.50), calls=%async_computation | async-start | bytes 1572864 | tf_op jit(solution)/shard_map/all_to_all | solution.py:387
  11.4 3.2 %shard_map.56 = bf16[256,1536]{1,0:T(8,128)(2,1)} custom-call(s32[8]{0:T(128)} %counts.11, s32[1,128]{1,0:T(1,128)} %bitcast.56, bf16[4,8,192,128]{3,2,1,0:T(8,128)(2,1)} %bitcast.58), custom_call_target="tpu_custom_call" | custom-call | flops 2000000000 | bytes 4000000 | tf_op jit(solution)/shard_map/pallas_call | solution.py:112
  14.7 11.7 %all-to-all-done = bf16[16,16,1536]{2,1,0:T(8,128)(2,1)S(1)} async-done(((bf16[16,16,1536]{2,1,0:T(8,128)(2,1)}), bf16[16,16,1536]{2,1,0:T(8,128)(2,1)S(1)}, u32[]{:S(2)}, u32[]{:S(2)}) %all-to-all-start) | async-done | bytes 786464 | tf_op jit(solution)/shard_map/all_to_all | solution.py:387
  26.4 3.6 %all-to-all-start.1 = ((bf16[16,16,1536]{2,1,0:T(8,128)(2,1)}), bf16[16,16,1536]{2,1,0:T(8,128)(2,1)S(1)}, u32[]{:S(2)}, u32[]{:S(2)}) async-start(bf16[16,16,1536]{2,1,0:T(8,128)(2,1)} %bitcast.49), calls=%async_computation.1 | async-start | bytes 1572864 | tf_op jit(solution)/shard_map/all_to_all | solution.py:387
  32.2 1.8 %collective-permute-start = (bf16[128,1536]{1,0:T(8,128)(2,1)S(1)}, bf16[128,1536]{1,0:T(8,128)(2,1)S(1)}, u32[]{:S(2)}, u32[]{:S(2)}) collective-permute-start(bf16[128,1536]{1,0:T(8,128)(2,1)S(1)} %convolution_convert_fusion.3), channel_id=1, source_target_pairs={{0,6},{1,7},{2,0},{3,1},{4,2},{5,3},{6,4},{7,5},{8,14},{9,15},{10,... | collective-permute-start | bytes 1179656 | tf_op jit(solution)/shard_map/ppermute | solution.py:44
  34.3 3.0 %collective-permute-start.3 = (bf16[128,1536]{1,0:T(8,128)(2,1)S(1)}, bf16[128,1536]{1,0:T(8,128)(2,1)S(1)}, u32[]{:S(2)}, u32[]{:S(2)}) collective-permute-start(bf16[128,1536]{1,0:T(8,128)(2,1)S(1)} %convolution_convert_fusion.2), channel_id=1, source_target_pairs={{0,6},{1,7},{2,0},{3,1},{4,2},{5,3},{6,4},{7,5},{8,14},{9,15},{10,... | collective-permute-start | bytes 1179656 | tf_op jit(solution)/shard_map/ppermute | solution.py:44
  37.2 6.4 %collective-permute-done.4 = bf16[128,1536]{1,0:T(8,128)(2,1)S(1)} collective-permute-done((bf16[128,1536]{1,0:T(8,128)(2,1)S(1)}, bf16[128,1536]{1,0:T(8,128)(2,1)S(1)}, u32[]{:S(2)}, u32[]{:S(2)}) %collective-permute-start.4) | collective-permute-done | bytes 393248 | tf_op jit(solution)/shard_map/ppermute | solution.py:44
  44.3 3.0 %collective-permute-start.1 = (bf16[128,1536]{1,0:T(8,128)(2,1)S(1)}, bf16[128,1536]{1,0:T(8,128)(2,1)}, u32[]{:S(2)}, u32[]{:S(2)}) collective-permute-start(bf16[128,1536]{1,0:T(8,128)(2,1)S(1)} %collective-permute-done), channel_id=1, source_target_pairs={{0,6},{1,7},{2,0},{3,1},{4,2},{5,3},{6,4},{7,5},{8,14},{9,15},{10,... | collective-permute-start | bytes 1179656 | tf_op jit(solution)/shard_map/ppermute | solution.py:44
  47.9 4.2 %collective-permute-done.2 = bf16[128,1536]{1,0:T(8,128)(2,1)S(1)} collective-permute-done((bf16[128,1536]{1,0:T(8,128)(2,1)S(1)}, bf16[128,1536]{1,0:T(8,128)(2,1)S(1)}, u32[]{:S(2)}, u32[]{:S(2)}) %collective-permute-start.2) | collective-permute-done | bytes 393248 | tf_op jit(solution)/shard_map/ppermute | solution.py:44
  52.7 3.0 %collective-permute-start.10 = (bf16[128,1536]{1,0:T(8,128)(2,1)S(1)}, bf16[128,1536]{1,0:T(8,128)(2,1)S(1)}, u32[]{:S(2)}, u32[]{:S(2)}) collective-permute-start(bf16[128,1536]{1,0:T(8,128)(2,1)S(1)} %convolution_convert_fusion.1.after), channel_id=1, source_target_pairs={{0,6},{1,7},{2,0},{3,1},{4,2},{5,3},{6,4},{7,5},{8,14},{9,15},{10,... | collective-permute-start | bytes 1179656 | tf_op jit(solution)/shard_map/ppermute | solution.py:44
  56.2 3.2 %shard_map.57.refs_10_ = bf16[2,1536,768]{2,1,0:T(8,128)(2,1)S(1)} custom-call(s32[8]{0:T(128)} %counts.11, s32[128]{0:T(128)} %c_orbitals.7, bf16[8,8,192,768]{3,2,1,0:T(8,128)(2,1)} %refs_8_.3, bf16[8,8,192,768]{3,2,1,0:T(8,128)(2,1)} %collective-permute-done.6.v_other.refs_9_, bf16[128,1536]{1,0:T(8,128)(2,1)} %copy-done), custom_call_target="tpu_custom_call" | custom-call | bytes 9437184 | tf_op jit(solution)/shard_map/pallas_call | solution.py:154
  60.6 1.8 %collective-permute-start.14 = (bf16[128,1536]{1,0:T(8,128)(2,1)S(1)}, bf16[128,1536]{1,0:T(8,128)(2,1)S(1)}, u32[]{:S(2)}, u32[]{:S(2)}) collective-permute-start(bf16[128,1536]{1,0:T(8,128)(2,1)S(1)} %convolution_convert_fusion), channel_id=1, source_target_pairs={{0,6},{1,7},{2,0},{3,1},{4,2},{5,3},{6,4},{7,5},{8,14},{9,15},{10,... | collective-permute-start | bytes 1179656 | tf_op jit(solution)/shard_map/ppermute | solution.py:44
  62.5 11.8 %shard_map.58 = (f32[64,6144]{1,0:T(8,128)}, s16[64,6272]{1,0:T(8,128)(2,1)}, s16[64,6272]{1,0:T(8,128)(2,1)}, s16[64,6272]{1,0:T(8,128)(2,1)}) custom-call(s32[8]{0:T(128)} %counts.11, s32[128]{0:T(128)} %c_orbitals.7, bf16[2,64,1536]{2,1,0:T(8,128)(2,1)} %bitcast.48, bf16[2,64,1536]{2,1,0:T(8,128)(2,1)} %bitcast.52, bf16[2,64,1536]{2,1,0:T(8,128)(2,1)} %bitcast.6.refs_2_, ...), custom_call_target="tpu_custom_call" | custom-call | flops 4831838208 | bytes 18874368 | tf_op jit(solution)/shard_map/pallas_call | solution.py:248
  80.7 1.9 %collective-permute-start.9 = (s16[64,6272]{1,0:T(8,128)(2,1)}, s16[64,6272]{1,0:T(8,128)(2,1)}, u32[]{:S(2)}, u32[]{:S(2)}) collective-permute-start(s16[64,6272]{1,0:T(8,128)(2,1)} %get-tuple-element.29), channel_id=1, source_target_pairs={{0,16},{1,65},{2,18},{3,67},{4,20},{5,69},{6,22},{7,71},{8,24},{9,... | collective-permute-start | bytes 2408456 | tf_op jit(solution)/shard_map/ppermute | solution.py:44
  82.7 3.1 %shard_map.59.refs_10_ = bf16[2,1536,768]{2,1,0:T(8,128)(2,1)S(1)} custom-call(s32[8]{0:T(128)} %counts.11, s32[128]{0:T(128)} %c_orbitals.7, bf16[8,8,192,768]{3,2,1,0:T(8,128)(2,1)} %refs_8_.3, bf16[8,8,192,768]{3,2,1,0:T(8,128)(2,1)} %collective-permute-done.6.v_other.refs_9_, s16[64,6272]{1,0:T(8,128)(2,1)} %get-tuple-element.27.after), custom_call_target="tpu_custom_call" | custom-call | bytes 9437184 | tf_op jit(solution)/shard_map/pallas_call | solution.py:154
  87.1 10.7 %shard_map.60 = (f32[64,6144]{1,0:T(8,128)}, s16[64,6272]{1,0:T(8,128)(2,1)}, s16[64,6272]{1,0:T(8,128)(2,1)}, s16[64,6272]{1,0:T(8,128)(2,1)}) custom-call(s32[8]{0:T(128)} %counts.11, s32[128]{0:T(128)} %c_orbitals.7, bf16[2,64,1536]{2,1,0:T(8,128)(2,1)S(1)} %bitcast.31, bf16[2,64,1536]{2,1,0:T(8,128)(2,1)S(1)} %bitcast.35, ...), custom_call_target="tpu_custom_call" | custom-call | flops 4831838208 | bytes 18874368 | tf_op jit(solution)/shard_map/pallas_call | solution.py:248
  101.1 1.8 %collective-permute-start.18 = (s16[64,6272]{1,0:T(8,128)(2,1)}, s16[64,6272]{1,0:T(8,128)(2,1)}, u32[]{:S(2)}, u32[]{:S(2)}) collective-permute-start(s16[64,6272]{1,0:T(8,128)(2,1)} %get-tuple-element.42), channel_id=1, source_target_pairs={{0,16},{1,65},{2,18},{3,67},{4,20},{5,69},{6,22},{7,71},{8,24},{9,... | collective-permute-start | bytes 2408456 | tf_op jit(solution)/shard_map/ppermute | solution.py:44
  102.9 3.7 %shard_map.61 = s16[256,1664]{1,0:T(8,128)(2,1)} custom-call(f32[64,6144]{1,0:T(8,128)} %get-tuple-element.36.own_ref, s16[64,6272]{1,0:T(8,128)(2,1)S(1)} %collective-permute-done.7.q1, s16[64,6272]{1,0:T(8,128)(2,1)S(1)} %collective-permute-done.8.q2, s16[64,6272]{1,0:T(8,128)(2,1)} %collective-permute-done.9.q3), custom_call_target="tpu_custom_call" | custom-call | flops 3145728 | bytes 4718592 | tf_op jit(solution)/shard_map/pallas_call | solution.py:307
  106.7 4.5 %all-to-all-start.2 = ((s16[16,16,1664]{2,1,0:T(8,128)(2,1)}), s16[16,16,1664]{2,1,0:T(8,128)(2,1)S(1)}, u32[]{:S(2)}, u32[]{:S(2)}) async-start(s16[16,16,1664]{2,1,0:T(8,128)(2,1)} %bitcast.45), calls=%async_computation.2 | async-start | bytes 1703936 | tf_op jit(solution)/shard_map/all_to_all | solution.py:416
  112.2 12.1 %collective-permute-done.17.q2 = s16[64,6272]{1,0:T(8,128)(2,1)S(1)} collective-permute-done((s16[64,6272]{1,0:T(8,128)(2,1)}, s16[64,6272]{1,0:T(8,128)(2,1)S(1)}, u32[]{:S(2)}, u32[]{:S(2)}) %collective-permute-start.17) | collective-permute-done | bytes 802848 | tf_op jit(solution)/shard_map/ppermute | solution.py:44
  125.9 3.8 %shard_map.62 = s16[256,1664]{1,0:T(8,128)(2,1)} custom-call(f32[64,6144]{1,0:T(8,128)} %get-tuple-element.35.own_ref, s16[64,6272]{1,0:T(8,128)(2,1)S(1)} %collective-permute-done.16.q1, s16[64,6272]{1,0:T(8,128)(2,1)S(1)} %collective-permute-done.17.q2, s16[64,6272]{1,0:T(8,128)(2,1)} %collective-permute-done.18.q3), custom_call_target="tpu_custom_call" | custom-call | flops 3145728 | bytes 4718592 | tf_op jit(solution)/shard_map/pallas_call | solution.py:307
  129.7 4.0 %all-to-all-start.3 = ((s16[16,16,1664]{2,1,0:T(8,128)(2,1)}), s16[16,16,1664]{2,1,0:T(8,128)(2,1)S(1)}, u32[]{:S(2)}, u32[]{:S(2)}) async-start(s16[16,16,1664]{2,1,0:T(8,128)(2,1)} %bitcast.46), calls=%async_computation.3 | async-start | bytes 1703936 | tf_op jit(solution)/shard_map/all_to_all | solution.py:416
  133.8 11.8 %all-to-all-done.3 = s16[16,16,1664]{2,1,0:T(8,128)(2,1)S(1)} async-done(((s16[16,16,1664]{2,1,0:T(8,128)(2,1)}), s16[16,16,1664]{2,1,0:T(8,128)(2,1)S(1)}, u32[]{:S(2)}, u32[]{:S(2)}) %all-to-all-start.3) | async-done | bytes 852000 | tf_op jit(solution)/shard_map/all_to_all | solution.py:416
  (66 shorter events, 21.2 us)
Async XLA Ops:
  0.0 52.7 %collective-permute-start.6 = (bf16[8,8,192,768]{3,2,1,0:T(8,128)(2,1)}, bf16[8,8,192,768]{3,2,1,0:T(8,128)(2,1)}, u32[]{:S(2)}, u32[]{:S(2)}) collective-permute-start(bf16[8,8,192,768]{3,2,1,0:T(8,128)(2,1)} %refs_8_.3), channel_id=1, source_target_pairs={{0,1},{1,0},{2,3},{3,2},{4,5},{5,4},{6,7},{7,6},{8,9},{9,8},{10,11... | collective-permute-start | bytes 56623112 | tf_op jit(solution)/shard_map/ppermute | solution.py:44
  3.2 23.2 %all-to-all-start = ((bf16[16,16,1536]{2,1,0:T(8,128)(2,1)}), bf16[16,16,1536]{2,1,0:T(8,128)(2,1)S(1)}, u32[]{:S(2)}, u32[]{:S(2)}) async-start(bf16[16,16,1536]{2,1,0:T(8,128)(2,1)} %bitcast.50), calls=%async_computation | async-start | bytes 1572864 | tf_op jit(solution)/shard_map/all_to_all | solution.py:387
  26.4 20.9 %all-to-all-start.1 = ((bf16[16,16,1536]{2,1,0:T(8,128)(2,1)}), bf16[16,16,1536]{2,1,0:T(8,128)(2,1)S(1)}, u32[]{:S(2)}, u32[]{:S(2)}) async-start(bf16[16,16,1536]{2,1,0:T(8,128)(2,1)} %bitcast.49), calls=%async_computation.1 | async-start | bytes 1572864 | tf_op jit(solution)/shard_map/all_to_all | solution.py:387
  30.3 29.1 %copy-start.2 = (bf16[128,1536]{1,0:T(8,128)(2,1)}, bf16[128,1536]{1,0:T(8,128)(2,1)S(1)}, u32[]{:S(2)}) copy-start(bf16[128,1536]{1,0:T(8,128)(2,1)S(1)} %convolution_convert_fusion.2) | copy-start | bytes 1179652
  30.3 13.3 %collective-permute-start.4 = (bf16[128,1536]{1,0:T(8,128)(2,1)S(1)}, bf16[128,1536]{1,0:T(8,128)(2,1)S(1)}, u32[]{:S(2)}, u32[]{:S(2)}) collective-permute-start(bf16[128,1536]{1,0:T(8,128)(2,1)S(1)} %convolution_convert_fusion.2), channel_id=1, source_target_pairs={{0,2},{1,3},{2,4},{3,5},{4,6},{5,7},{6,0},{7,1},{8,10},{9,11},{10,... | collective-permute-start | bytes 1179656 | tf_op jit(solution)/shard_map/ppermute | solution.py:44
  32.2 12.1 %collective-permute-start = (bf16[128,1536]{1,0:T(8,128)(2,1)S(1)}, bf16[128,1536]{1,0:T(8,128)(2,1)S(1)}, u32[]{:S(2)}, u32[]{:S(2)}) collective-permute-start(bf16[128,1536]{1,0:T(8,128)(2,1)S(1)} %convolution_convert_fusion.3), channel_id=1, source_target_pairs={{0,6},{1,7},{2,0},{3,1},{4,2},{5,3},{6,4},{7,5},{8,14},{9,15},{10,... | collective-permute-start | bytes 1179656 | tf_op jit(solution)/shard_map/ppermute | solution.py:44
  34.0 18.1 %collective-permute-start.2 = (bf16[128,1536]{1,0:T(8,128)(2,1)S(1)}, bf16[128,1536]{1,0:T(8,128)(2,1)S(1)}, u32[]{:S(2)}, u32[]{:S(2)}) collective-permute-start(bf16[128,1536]{1,0:T(8,128)(2,1)S(1)} %convolution_convert_fusion.3), channel_id=1, source_target_pairs={{0,2},{1,3},{2,4},{3,5},{4,6},{5,7},{6,0},{7,1},{8,10},{9,11},{10,... | collective-permute-start | bytes 1179656 | tf_op jit(solution)/shard_map/ppermute | solution.py:44
  34.3 18.5 %collective-permute-start.3 = (bf16[128,1536]{1,0:T(8,128)(2,1)S(1)}, bf16[128,1536]{1,0:T(8,128)(2,1)S(1)}, u32[]{:S(2)}, u32[]{:S(2)}) collective-permute-start(bf16[128,1536]{1,0:T(8,128)(2,1)S(1)} %convolution_convert_fusion.2), channel_id=1, source_target_pairs={{0,6},{1,7},{2,0},{3,1},{4,2},{5,3},{6,4},{7,5},{8,14},{9,15},{10,... | collective-permute-start | bytes 1179656 | tf_op jit(solution)/shard_map/ppermute | solution.py:44
  43.7 17.0 %collective-permute-start.5 = (bf16[128,1536]{1,0:T(8,128)(2,1)S(1)}, bf16[128,1536]{1,0:T(8,128)(2,1)}, u32[]{:S(2)}, u32[]{:S(2)}) collective-permute-start(bf16[128,1536]{1,0:T(8,128)(2,1)S(1)} %collective-permute-done.4), channel_id=1, source_target_pairs={{0,2},{1,3},{2,4},{3,5},{4,6},{5,7},{6,0},{7,1},{8,10},{9,11},{10,... | collective-permute-start | bytes 1179656 | tf_op jit(solution)/shard_map/ppermute | solution.py:44
  44.3 18.2 %collective-permute-start.1 = (bf16[128,1536]{1,0:T(8,128)(2,1)S(1)}, bf16[128,1536]{1,0:T(8,128)(2,1)}, u32[]{:S(2)}, u32[]{:S(2)}) collective-permute-start(bf16[128,1536]{1,0:T(8,128)(2,1)S(1)} %collective-permute-done), channel_id=1, source_target_pairs={{0,6},{1,7},{2,0},{3,1},{4,2},{5,3},{6,4},{7,5},{8,14},{9,15},{10,... | collective-permute-start | bytes 1179656 | tf_op jit(solution)/shard_map/ppermute | solution.py:44
  52.7 21.5 %collective-permute-start.10 = (bf16[128,1536]{1,0:T(8,128)(2,1)S(1)}, bf16[128,1536]{1,0:T(8,128)(2,1)S(1)}, u32[]{:S(2)}, u32[]{:S(2)}) collective-permute-start(bf16[128,1536]{1,0:T(8,128)(2,1)S(1)} %convolution_convert_fusion.1.after), channel_id=1, source_target_pairs={{0,6},{1,7},{2,0},{3,1},{4,2},{5,3},{6,4},{7,5},{8,14},{9,15},{10,... | collective-permute-start | bytes 1179656 | tf_op jit(solution)/shard_map/ppermute | solution.py:44
  55.7 23.4 %collective-permute-start.13 = (bf16[128,1536]{1,0:T(8,128)(2,1)S(1)}, bf16[128,1536]{1,0:T(8,128)(2,1)S(1)}, u32[]{:S(2)}, u32[]{:S(2)}) collective-permute-start(bf16[128,1536]{1,0:T(8,128)(2,1)S(1)} %convolution_convert_fusion.1.after), channel_id=1, source_target_pairs={{0,2},{1,3},{2,4},{3,5},{4,6},{5,7},{6,0},{7,1},{8,10},{9,11},{10,... | collective-permute-start | bytes 1179656 | tf_op jit(solution)/shard_map/ppermute | solution.py:44
  55.7 19.7 %collective-permute-start.11 = (bf16[128,1536]{1,0:T(8,128)(2,1)S(1)}, bf16[128,1536]{1,0:T(8,128)(2,1)S(1)}, u32[]{:S(2)}, u32[]{:S(2)}) collective-permute-start(bf16[128,1536]{1,0:T(8,128)(2,1)S(1)} %convolution_convert_fusion), channel_id=1, source_target_pairs={{0,2},{1,3},{2,4},{3,5},{4,6},{5,7},{6,0},{7,1},{8,10},{9,11},{10,... | collective-permute-start | bytes 1179656 | tf_op jit(solution)/shard_map/ppermute | solution.py:44
  60.6 20.1 %collective-permute-start.14 = (bf16[128,1536]{1,0:T(8,128)(2,1)S(1)}, bf16[128,1536]{1,0:T(8,128)(2,1)S(1)}, u32[]{:S(2)}, u32[]{:S(2)}) collective-permute-start(bf16[128,1536]{1,0:T(8,128)(2,1)S(1)} %convolution_convert_fusion), channel_id=1, source_target_pairs={{0,6},{1,7},{2,0},{3,1},{4,2},{5,3},{6,4},{7,5},{8,14},{9,15},{10,... | collective-permute-start | bytes 1179656 | tf_op jit(solution)/shard_map/ppermute | solution.py:44
  75.5 10.4 %collective-permute-start.12 = (bf16[128,1536]{1,0:T(8,128)(2,1)S(1)}, bf16[128,1536]{1,0:T(8,128)(2,1)S(1)}, u32[]{:S(2)}, u32[]{:S(2)}) collective-permute-start(bf16[128,1536]{1,0:T(8,128)(2,1)S(1)} %collective-permute-done.10), channel_id=1, source_target_pairs={{0,6},{1,7},{2,0},{3,1},{4,2},{5,3},{6,4},{7,5},{8,14},{9,15},{10,... | collective-permute-start | bytes 1179656 | tf_op jit(solution)/shard_map/ppermute | solution.py:44
  77.0 10.1 %collective-permute-start.15 = (bf16[128,1536]{1,0:T(8,128)(2,1)S(1)}, bf16[128,1536]{1,0:T(8,128)(2,1)S(1)}, u32[]{:S(2)}, u32[]{:S(2)}) collective-permute-start(bf16[128,1536]{1,0:T(8,128)(2,1)S(1)} %collective-permute-done.11), channel_id=1, source_target_pairs={{0,2},{1,3},{2,4},{3,5},{4,6},{5,7},{6,0},{7,1},{8,10},{9,11},{10,... | collective-permute-start | bytes 1179656 | tf_op jit(solution)/shard_map/ppermute | solution.py:44
  77.5 23.7 %collective-permute-start.7 = (s16[64,6272]{1,0:T(8,128)(2,1)}, s16[64,6272]{1,0:T(8,128)(2,1)S(1)}, u32[]{:S(2)}, u32[]{:S(2)}) collective-permute-start(s16[64,6272]{1,0:T(8,128)(2,1)} %get-tuple-element.27.after), channel_id=1, source_target_pairs={{0,8},{1,33},{2,10},{3,35},{4,12},{5,37},{6,14},{7,39},{8,16},{9,4... | collective-permute-start | bytes 2408456 | tf_op jit(solution)/shard_map/ppermute | solution.py:44
  79.1 23.8 %collective-permute-start.8 = (s16[64,6272]{1,0:T(8,128)(2,1)}, s16[64,6272]{1,0:T(8,128)(2,1)S(1)}, u32[]{:S(2)}, u32[]{:S(2)}) collective-permute-start(s16[64,6272]{1,0:T(8,128)(2,1)} %get-tuple-element.28), channel_id=1, source_target_pairs={{0,24},{1,97},{2,26},{3,99},{4,28},{5,101},{6,30},{7,103},{8,0},{9... | collective-permute-start | bytes 2408456 | tf_op jit(solution)/shard_map/ppermute | solution.py:44
  80.7 22.2 %collective-permute-start.9 = (s16[64,6272]{1,0:T(8,128)(2,1)}, s16[64,6272]{1,0:T(8,128)(2,1)}, u32[]{:S(2)}, u32[]{:S(2)}) collective-permute-start(s16[64,6272]{1,0:T(8,128)(2,1)} %get-tuple-element.29), channel_id=1, source_target_pairs={{0,16},{1,65},{2,18},{3,67},{4,20},{5,69},{6,22},{7,71},{8,24},{9,... | collective-permute-start | bytes 2408456 | tf_op jit(solution)/shard_map/ppermute | solution.py:44
  97.8 14.4 %collective-permute-start.16 = (s16[64,6272]{1,0:T(8,128)(2,1)}, s16[64,6272]{1,0:T(8,128)(2,1)S(1)}, u32[]{:S(2)}, u32[]{:S(2)}) collective-permute-start(s16[64,6272]{1,0:T(8,128)(2,1)} %get-tuple-element.40), channel_id=1, source_target_pairs={{0,8},{1,33},{2,10},{3,35},{4,12},{5,37},{6,14},{7,39},{8,16},{9,4... | collective-permute-start | bytes 2408456 | tf_op jit(solution)/shard_map/ppermute | solution.py:44
  99.4 25.0 %collective-permute-start.17 = (s16[64,6272]{1,0:T(8,128)(2,1)}, s16[64,6272]{1,0:T(8,128)(2,1)S(1)}, u32[]{:S(2)}, u32[]{:S(2)}) collective-permute-start(s16[64,6272]{1,0:T(8,128)(2,1)} %get-tuple-element.41), channel_id=1, source_target_pairs={{0,24},{1,97},{2,26},{3,99},{4,28},{5,101},{6,30},{7,103},{8,0},{9... | collective-permute-start | bytes 2408456 | tf_op jit(solution)/shard_map/ppermute | solution.py:44
  101.1 24.8 %collective-permute-start.18 = (s16[64,6272]{1,0:T(8,128)(2,1)}, s16[64,6272]{1,0:T(8,128)(2,1)}, u32[]{:S(2)}, u32[]{:S(2)}) collective-permute-start(s16[64,6272]{1,0:T(8,128)(2,1)} %get-tuple-element.42), channel_id=1, source_target_pairs={{0,16},{1,65},{2,18},{3,67},{4,20},{5,69},{6,22},{7,71},{8,24},{9,... | collective-permute-start | bytes 2408456 | tf_op jit(solution)/shard_map/ppermute | solution.py:44
  106.7 23.1 %all-to-all-start.2 = ((s16[16,16,1664]{2,1,0:T(8,128)(2,1)}), s16[16,16,1664]{2,1,0:T(8,128)(2,1)S(1)}, u32[]{:S(2)}, u32[]{:S(2)}) async-start(s16[16,16,1664]{2,1,0:T(8,128)(2,1)} %bitcast.45), calls=%async_computation.2 | async-start | bytes 1703936 | tf_op jit(solution)/shard_map/all_to_all | solution.py:416
  129.7 15.9 %all-to-all-start.3 = ((s16[16,16,1664]{2,1,0:T(8,128)(2,1)}), s16[16,16,1664]{2,1,0:T(8,128)(2,1)S(1)}, u32[]{:S(2)}, u32[]{:S(2)}) async-start(s16[16,16,1664]{2,1,0:T(8,128)(2,1)} %bitcast.46), calls=%async_computation.3 | async-start | bytes 1703936 | tf_op jit(solution)/shard_map/all_to_all | solution.py:416
  (9 other events, 114.2 us)

commit v6 on v5

--- a/solution.py
+++ b/solution.py
@@ -308,7 +308,7 @@
         functools.partial(sum_kernel, number),
         in_specs=[HBM] * 4,
         out_specs=VMEM,
-        out_shape=jax.ShapeDtypeStruct((number * rows, width), jnp.int16),
+        out_shape=pltpu.VMEM((number * rows, width), jnp.int16),
         scratch_shapes=[
             pltpu.VMEM(own.shape, jnp.float32),
             pltpu.VMEM((3,) + parts[0].shape, jnp.int16),
@@ -396,7 +396,7 @@
             low, high, other, *_ = lax.optimization_barrier((low, high, other, *before))
         low1, high3 = send(low, X_DOWN), send(high, X_UP)
         high1, low3 = send(high, X_DOWN), send(low, X_UP)
-        before = (high1, low3)
+        before = (low1, high3)
         if products:
             low1, high3, _ = lax.optimization_barrier((low1, high3, products[-1][0]))
         low2, high2 = send(low1, X_DOWN), send(high3, X_UP)

time: 148 us -> 148 us (level)
  transfers between devices with their start and end apart: 23 -> 23, of which waited for: 12 -> 11; matrix products, arithmetic and copies ran while one was open for 1% -> 1% of each run, Pallas kernels for 29% -> 29%
where the time goes in v6:
time: 148 us; the launch traced here: 147 us
  waiting for transfers between devices  54.2 us (37%)
  starting transfers between devices  46.5 us (31%)
  Pallas kernels  44.1 us (30%)
    ppermute x19, waiting for transfers between devices, send(): return lax.ppermute(value, AXES, pairs)  30.7 us
    ppermute x19, starting transfers between devices, send(): return lax.ppermute(value, AXES, pairs)  26.2 us
    pallas_call x2, Pallas kernels, matmul(): pl.pallas_call(functools.partial(matmul_kernel, m, start), in_specs=[SMEM...  22.5 us
    all_to_all x2, waiting for transfers between devices, shards(): lax.all_to_all(coded, AXES, split_axis=0, concat_axis=0, tiled=True, axis...  11.8 us
    all_to_all x2, starting transfers between devices, shards(): lax.all_to_all(piece, 'slab', split_axis=0, concat_axis=0, tiled=True)  11.7 us
    all_to_all x2, waiting for transfers between devices, shards(): lax.all_to_all(piece, 'slab', split_axis=0, concat_axis=0, tiled=True)  11.7 us
    all_to_all x2, starting transfers between devices, shards(): lax.all_to_all(coded, AXES, split_axis=0, concat_axis=0, tiled=True, axis...  8.54 us
    pallas_call x2, Pallas kernels, sum_coded(): pl.pallas_call(functools.partial(sum_kernel, number), in_specs=[HBM] * 4,...  7.52 us
  transfers between devices with their start and end apart: 23, of which 11 were waited for; matrix products, arithmetic and copies ran while one was open for 1% of the time, Pallas kernels for 29%

profile of v6, /device:TPU:0, one launch (start us, length us, event | category | flops | bytes accessed | tf_op | source)
XLA Modules:
  0.0 147.0 jit_solution(600059298640658661)
XLA Ops:
  0.0 3.2 %shard_map.55 = bf16[256,1536]{1,0:T(8,128)(2,1)} custom-call(s32[8]{0:T(128)} %counts.11, s32[1,128]{1,0:T(1,128)} %bitcast.53, bf16[4,8,192,128]{3,2,1,0:T(8,128)(2,1)} %bitcast.55), custom_call_target="tpu_custom_call" | custom-call | flops 2000000000 | bytes 4000000 | tf_op jit(solution)/shard_map/pallas_call | solution.py:112
  3.2 8.1 %all-to-all-start = ((bf16[16,16,1536]{2,1,0:T(8,128)(2,1)}), bf16[16,16,1536]{2,1,0:T(8,128)(2,1)S(1)}, u32[]{:S(2)}, u32[]{:S(2)}) async-start(bf16[16,16,1536]{2,1,0:T(8,128)(2,1)} %bitcast.48), calls=%async_computation | async-start | bytes 1572864 | tf_op jit(solution)/shard_map/all_to_all | solution.py:387
  11.4 3.2 %shard_map.56 = bf16[256,1536]{1,0:T(8,128)(2,1)} custom-call(s32[8]{0:T(128)} %counts.11, s32[1,128]{1,0:T(1,128)} %bitcast.54, bf16[4,8,192,128]{3,2,1,0:T(8,128)(2,1)} %bitcast.56), custom_call_target="tpu_custom_call" | custom-call | flops 2000000000 | bytes 4000000 | tf_op jit(solution)/shard_map/pallas_call | solution.py:112
  14.7 11.7 %all-to-all-done = bf16[16,16,1536]{2,1,0:T(8,128)(2,1)S(1)} async-done(((bf16[16,16,1536]{2,1,0:T(8,128)(2,1)}), bf16[16,16,1536]{2,1,0:T(8,128)(2,1)S(1)}, u32[]{:S(2)}, u32[]{:S(2)}) %all-to-all-start) | async-done | bytes 786464 | tf_op jit(solution)/shard_map/all_to_all | solution.py:387
  26.4 3.6 %all-to-all-start.1 = ((bf16[16,16,1536]{2,1,0:T(8,128)(2,1)}), bf16[16,16,1536]{2,1,0:T(8,128)(2,1)S(1)}, u32[]{:S(2)}, u32[]{:S(2)}) async-start(bf16[16,16,1536]{2,1,0:T(8,128)(2,1)} %bitcast.47), calls=%async_computation.1 | async-start | bytes 1572864 | tf_op jit(solution)/shard_map/all_to_all | solution.py:387
  32.2 1.8 %collective-permute-start = (bf16[128,1536]{1,0:T(8,128)(2,1)S(1)}, bf16[128,1536]{1,0:T(8,128)(2,1)S(1)}, u32[]{:S(2)}, u32[]{:S(2)}) collective-permute-start(bf16[128,1536]{1,0:T(8,128)(2,1)S(1)} %convolution_convert_fusion.3), channel_id=1, source_target_pairs={{0,6},{1,7},{2,0},{3,1},{4,2},{5,3},{6,4},{7,5},{8,14},{9,15},{10,... | collective-permute-start | bytes 1179656 | tf_op jit(solution)/shard_map/ppermute | solution.py:44
  34.3 3.0 %collective-permute-start.3 = (bf16[128,1536]{1,0:T(8,128)(2,1)S(1)}, bf16[128,1536]{1,0:T(8,128)(2,1)S(1)}, u32[]{:S(2)}, u32[]{:S(2)}) collective-permute-start(bf16[128,1536]{1,0:T(8,128)(2,1)S(1)} %convolution_convert_fusion.2), channel_id=1, source_target_pairs={{0,6},{1,7},{2,0},{3,1},{4,2},{5,3},{6,4},{7,5},{8,14},{9,15},{10,... | collective-permute-start | bytes 1179656 | tf_op jit(solution)/shard_map/ppermute | solution.py:44
  37.2 6.4 %collective-permute-done.4 = bf16[128,1536]{1,0:T(8,128)(2,1)S(1)} collective-permute-done((bf16[128,1536]{1,0:T(8,128)(2,1)S(1)}, bf16[128,1536]{1,0:T(8,128)(2,1)S(1)}, u32[]{:S(2)}, u32[]{:S(2)}) %collective-permute-start.4) | collective-permute-done | bytes 393248 | tf_op jit(solution)/shard_map/ppermute | solution.py:44
  44.3 3.0 %collective-permute-start.1 = (bf16[128,1536]{1,0:T(8,128)(2,1)S(1)}, bf16[128,1536]{1,0:T(8,128)(2,1)}, u32[]{:S(2)}, u32[]{:S(2)}) collective-permute-start(bf16[128,1536]{1,0:T(8,128)(2,1)S(1)} %collective-permute-done), channel_id=1, source_target_pairs={{0,6},{1,7},{2,0},{3,1},{4,2},{5,3},{6,4},{7,5},{8,14},{9,15},{10,... | collective-permute-start | bytes 1179656 | tf_op jit(solution)/shard_map/ppermute | solution.py:44
  48.3 3.1 %shard_map.57.refs_10_ = bf16[2,1536,768]{2,1,0:T(8,128)(2,1)S(1)} custom-call(s32[8]{0:T(128)} %counts.11, s32[128]{0:T(128)} %c_orbitals.7, bf16[8,8,192,768]{3,2,1,0:T(8,128)(2,1)} %refs_8_.3, bf16[8,8,192,768]{3,2,1,0:T(8,128)(2,1)} %collective-permute-done.6.v_other.refs_9_, bf16[128,1536]{1,0:T(8,128)(2,1)} %copy-done), custom_call_target="tpu_custom_call" | custom-call | bytes 9437184 | tf_op jit(solution)/shard_map/pallas_call | solution.py:154
  54.2 6.4 %collective-permute-done.5 = bf16[128,1536]{1,0:T(8,128)(2,1)} collective-permute-done((bf16[128,1536]{1,0:T(8,128)(2,1)S(1)}, bf16[128,1536]{1,0:T(8,128)(2,1)}, u32[]{:S(2)}, u32[]{:S(2)}) %collective-permute-start.5) | collective-permute-done | bytes 393248 | tf_op jit(solution)/shard_map/ppermute | solution.py:44
  62.2 11.8 %shard_map.58 = (f32[64,6144]{1,0:T(8,128)}, s16[64,6272]{1,0:T(8,128)(2,1)}, s16[64,6272]{1,0:T(8,128)(2,1)}, s16[64,6272]{1,0:T(8,128)(2,1)}) custom-call(s32[8]{0:T(128)} %counts.11, s32[128]{0:T(128)} %c_orbitals.7, bf16[2,64,1536]{2,1,0:T(8,128)(2,1)} %bitcast.46, bf16[2,64,1536]{2,1,0:T(8,128)(2,1)} %bitcast.50, bf16[2,64,1536]{2,1,0:T(8,128)(2,1)} %bitcast.6.refs_2_, ...), custom_call_target="tpu_custom_call" | custom-call | flops 4831838208 | bytes 18874368 | tf_op jit(solution)/shard_map/pallas_call | solution.py:248
  77.5 1.6 %collective-permute-start.7 = (s16[64,6272]{1,0:T(8,128)(2,1)}, s16[64,6272]{1,0:T(8,128)(2,1)S(1)}, u32[]{:S(2)}, u32[]{:S(2)}) collective-permute-start(s16[64,6272]{1,0:T(8,128)(2,1)} %get-tuple-element.27.after), channel_id=1, source_target_pairs={{0,8},{1,33},{2,10},{3,35},{4,12},{5,37},{6,14},{7,39},{8,16},{9,4... | collective-permute-start | bytes 2408456 | tf_op jit(solution)/shard_map/ppermute | solution.py:44
  80.7 1.9 %collective-permute-start.9 = (s16[64,6272]{1,0:T(8,128)(2,1)}, s16[64,6272]{1,0:T(8,128)(2,1)}, u32[]{:S(2)}, u32[]{:S(2)}) collective-permute-start(s16[64,6272]{1,0:T(8,128)(2,1)} %get-tuple-element.29), channel_id=1, source_target_pairs={{0,16},{1,65},{2,18},{3,67},{4,20},{5,69},{6,22},{7,71},{8,24},{9,... | collective-permute-start | bytes 2408456 | tf_op jit(solution)/shard_map/ppermute | solution.py:44
  82.7 3.1 %shard_map.59.refs_10_ = bf16[2,1536,768]{2,1,0:T(8,128)(2,1)S(1)} custom-call(s32[8]{0:T(128)} %counts.11, s32[128]{0:T(128)} %c_orbitals.7, bf16[8,8,192,768]{3,2,1,0:T(8,128)(2,1)} %refs_8_.3, bf16[8,8,192,768]{3,2,1,0:T(8,128)(2,1)} %collective-permute-done.6.v_other.refs_9_, s16[64,6272]{1,0:T(8,128)(2,1)} %get-tuple-element.27.after), custom_call_target="tpu_custom_call" | custom-call | bytes 9437184 | tf_op jit(solution)/shard_map/pallas_call | solution.py:154
  87.1 10.7 %shard_map.60 = (f32[64,6144]{1,0:T(8,128)}, s16[64,6272]{1,0:T(8,128)(2,1)}, s16[64,6272]{1,0:T(8,128)(2,1)}, s16[64,6272]{1,0:T(8,128)(2,1)}) custom-call(s32[8]{0:T(128)} %counts.11, s32[128]{0:T(128)} %c_orbitals.7, bf16[2,64,1536]{2,1,0:T(8,128)(2,1)S(1)} %bitcast.31, bf16[2,64,1536]{2,1,0:T(8,128)(2,1)S(1)} %bitcast.35, ...), custom_call_target="tpu_custom_call" | custom-call | flops 4831838208 | bytes 18874368 | tf_op jit(solution)/shard_map/pallas_call | solution.py:248
  99.4 1.8 %collective-permute-start.17 = (s16[64,6272]{1,0:T(8,128)(2,1)}, s16[64,6272]{1,0:T(8,128)(2,1)S(1)}, u32[]{:S(2)}, u32[]{:S(2)}) collective-permute-start(s16[64,6272]{1,0:T(8,128)(2,1)} %get-tuple-element.41), channel_id=1, source_target_pairs={{0,24},{1,97},{2,26},{3,99},{4,28},{5,101},{6,30},{7,103},{8,0},{9... | collective-permute-start | bytes 2408456 | tf_op jit(solution)/shard_map/ppermute | solution.py:44
  101.1 1.8 %collective-permute-start.18 = (s16[64,6272]{1,0:T(8,128)(2,1)}, s16[64,6272]{1,0:T(8,128)(2,1)}, u32[]{:S(2)}, u32[]{:S(2)}) collective-permute-start(s16[64,6272]{1,0:T(8,128)(2,1)} %get-tuple-element.42), channel_id=1, source_target_pairs={{0,16},{1,65},{2,18},{3,67},{4,20},{5,69},{6,22},{7,71},{8,24},{9,... | collective-permute-start | bytes 2408456 | tf_op jit(solution)/shard_map/ppermute | solution.py:44
  102.9 3.7 %shard_map.61 = s16[256,1664]{1,0:T(8,128)(2,1)} custom-call(f32[64,6144]{1,0:T(8,128)} %get-tuple-element.36.own_ref, s16[64,6272]{1,0:T(8,128)(2,1)S(1)} %collective-permute-done.7.q1, s16[64,6272]{1,0:T(8,128)(2,1)S(1)} %collective-permute-done.8.q2, s16[64,6272]{1,0:T(8,128)(2,1)} %collective-permute-done.9.q3), custom_call_target="tpu_custom_call" | custom-call | flops 3145728 | bytes 4718592 | tf_op jit(solution)/shard_map/pallas_call | solution.py:307
  106.7 4.5 %all-to-all-start.2 = ((s16[16,16,1664]{2,1,0:T(8,128)(2,1)}), s16[16,16,1664]{2,1,0:T(8,128)(2,1)S(1)}, u32[]{:S(2)}, u32[]{:S(2)}) async-start(s16[16,16,1664]{2,1,0:T(8,128)(2,1)} %bitcast.22), calls=%async_computation.2 | async-start | bytes 1703936 | tf_op jit(solution)/shard_map/all_to_all | solution.py:416
  112.3 12.1 %collective-permute-done.17.q2 = s16[64,6272]{1,0:T(8,128)(2,1)S(1)} collective-permute-done((s16[64,6272]{1,0:T(8,128)(2,1)}, s16[64,6272]{1,0:T(8,128)(2,1)S(1)}, u32[]{:S(2)}, u32[]{:S(2)}) %collective-permute-start.17) | collective-permute-done | bytes 802848 | tf_op jit(solution)/shard_map/ppermute | solution.py:44
  125.9 3.8 %shard_map.62 = s16[256,1664]{1,0:T(8,128)(2,1)} custom-call(f32[64,6144]{1,0:T(8,128)} %get-tuple-element.35.own_ref, s16[64,6272]{1,0:T(8,128)(2,1)S(1)} %collective-permute-done.16.q1, s16[64,6272]{1,0:T(8,128)(2,1)S(1)} %collective-permute-done.17.q2, s16[64,6272]{1,0:T(8,128)(2,1)} %collective-permute-done.18.q3), custom_call_target="tpu_custom_call" | custom-call | flops 3145728 | bytes 4718592 | tf_op jit(solution)/shard_map/pallas_call | solution.py:307
  129.7 4.0 %all-to-all-start.3 = ((s16[16,16,1664]{2,1,0:T(8,128)(2,1)}), s16[16,16,1664]{2,1,0:T(8,128)(2,1)S(1)}, u32[]{:S(2)}, u32[]{:S(2)}) async-start(s16[16,16,1664]{2,1,0:T(8,128)(2,1)} %bitcast.24), calls=%async_computation.3 | async-start | bytes 1703936 | tf_op jit(solution)/shard_map/all_to_all | solution.py:416
  133.8 11.8 %all-to-all-done.3 = s16[16,16,1664]{2,1,0:T(8,128)(2,1)S(1)} async-done(((s16[16,16,1664]{2,1,0:T(8,128)(2,1)}), s16[16,16,1664]{2,1,0:T(8,128)(2,1)S(1)}, u32[]{:S(2)}, u32[]{:S(2)}) %all-to-all-start.3) | async-done | bytes 852000 | tf_op jit(solution)/shard_map/all_to_all | solution.py:416
  (66 shorter events, 20.4 us)
Async XLA Ops:
  0.0 47.9 %collective-permute-start.6 = (bf16[8,8,192,768]{3,2,1,0:T(8,128)(2,1)}, bf16[8,8,192,768]{3,2,1,0:T(8,128)(2,1)}, u32[]{:S(2)}, u32[]{:S(2)}) collective-permute-start(bf16[8,8,192,768]{3,2,1,0:T(8,128)(2,1)} %refs_8_.3), channel_id=1, source_target_pairs={{0,1},{1,0},{2,3},{3,2},{4,5},{5,4},{6,7},{7,6},{8,9},{9,8},{10,11... | collective-permute-start | bytes 56623112 | tf_op jit(solution)/shard_map/ppermute | solution.py:44
  3.2 23.2 %all-to-all-start = ((bf16[16,16,1536]{2,1,0:T(8,128)(2,1)}), bf16[16,16,1536]{2,1,0:T(8,128)(2,1)S(1)}, u32[]{:S(2)}, u32[]{:S(2)}) async-start(bf16[16,16,1536]{2,1,0:T(8,128)(2,1)} %bitcast.48), calls=%async_computation | async-start | bytes 1572864 | tf_op jit(solution)/shard_map/all_to_all | solution.py:387
  26.4 20.9 %all-to-all-start.1 = ((bf16[16,16,1536]{2,1,0:T(8,128)(2,1)}), bf16[16,16,1536]{2,1,0:T(8,128)(2,1)S(1)}, u32[]{:S(2)}, u32[]{:S(2)}) async-start(bf16[16,16,1536]{2,1,0:T(8,128)(2,1)} %bitcast.47), calls=%async_computation.1 | async-start | bytes 1572864 | tf_op jit(solution)/shard_map/all_to_all | solution.py:387
  30.3 21.2 %copy-start.2 = (bf16[128,1536]{1,0:T(8,128)(2,1)}, bf16[128,1536]{1,0:T(8,128)(2,1)S(1)}, u32[]{:S(2)}) copy-start(bf16[128,1536]{1,0:T(8,128)(2,1)S(1)} %convolution_convert_fusion.2) | copy-start | bytes 1179652
  30.3 13.3 %collective-permute-start.4 = (bf16[128,1536]{1,0:T(8,128)(2,1)S(1)}, bf16[128,1536]{1,0:T(8,128)(2,1)S(1)}, u32[]{:S(2)}, u32[]{:S(2)}) collective-permute-start(bf16[128,1536]{1,0:T(8,128)(2,1)S(1)} %convolution_convert_fusion.2), channel_id=1, source_target_pairs={{0,2},{1,3},{2,4},{3,5},{4,6},{5,7},{6,0},{7,1},{8,10},{9,11},{10,... | collective-permute-start | bytes 1179656 | tf_op jit(solution)/shard_map/ppermute | solution.py:44
  32.2 12.1 %collective-permute-start = (bf16[128,1536]{1,0:T(8,128)(2,1)S(1)}, bf16[128,1536]{1,0:T(8,128)(2,1)S(1)}, u32[]{:S(2)}, u32[]{:S(2)}) collective-permute-start(bf16[128,1536]{1,0:T(8,128)(2,1)S(1)} %convolution_convert_fusion.3), channel_id=1, source_target_pairs={{0,6},{1,7},{2,0},{3,1},{4,2},{5,3},{6,4},{7,5},{8,14},{9,15},{10,... | collective-permute-start | bytes 1179656 | tf_op jit(solution)/shard_map/ppermute | solution.py:44
  34.0 18.1 %collective-permute-start.2 = (bf16[128,1536]{1,0:T(8,128)(2,1)S(1)}, bf16[128,1536]{1,0:T(8,128)(2,1)S(1)}, u32[]{:S(2)}, u32[]{:S(2)}) collective-permute-start(bf16[128,1536]{1,0:T(8,128)(2,1)S(1)} %convolution_convert_fusion.3), channel_id=1, source_target_pairs={{0,2},{1,3},{2,4},{3,5},{4,6},{5,7},{6,0},{7,1},{8,10},{9,11},{10,... | collective-permute-start | bytes 1179656 | tf_op jit(solution)/shard_map/ppermute | solution.py:44
  34.3 19.0 %collective-permute-start.3 = (bf16[128,1536]{1,0:T(8,128)(2,1)S(1)}, bf16[128,1536]{1,0:T(8,128)(2,1)S(1)}, u32[]{:S(2)}, u32[]{:S(2)}) collective-permute-start(bf16[128,1536]{1,0:T(8,128)(2,1)S(1)} %convolution_convert_fusion.2), channel_id=1, source_target_pairs={{0,6},{1,7},{2,0},{3,1},{4,2},{5,3},{6,4},{7,5},{8,14},{9,15},{10,... | collective-permute-start | bytes 1179656 | tf_op jit(solution)/shard_map/ppermute | solution.py:44
  43.7 17.0 %collective-permute-start.5 = (bf16[128,1536]{1,0:T(8,128)(2,1)S(1)}, bf16[128,1536]{1,0:T(8,128)(2,1)}, u32[]{:S(2)}, u32[]{:S(2)}) collective-permute-start(bf16[128,1536]{1,0:T(8,128)(2,1)S(1)} %collective-permute-done.4), channel_id=1, source_target_pairs={{0,2},{1,3},{2,4},{3,5},{4,6},{5,7},{6,0},{7,1},{8,10},{9,11},{10,... | collective-permute-start | bytes 1179656 | tf_op jit(solution)/shard_map/ppermute | solution.py:44
  44.3 17.9 %collective-permute-start.1 = (bf16[128,1536]{1,0:T(8,128)(2,1)S(1)}, bf16[128,1536]{1,0:T(8,128)(2,1)}, u32[]{:S(2)}, u32[]{:S(2)}) collective-permute-start(bf16[128,1536]{1,0:T(8,128)(2,1)S(1)} %collective-permute-done), channel_id=1, source_target_pairs={{0,6},{1,7},{2,0},{3,1},{4,2},{5,3},{6,4},{7,5},{8,14},{9,15},{10,... | collective-permute-start | bytes 1179656 | tf_op jit(solution)/shard_map/ppermute | solution.py:44
  47.9 26.1 %collective-permute-start.10 = (bf16[128,1536]{1,0:T(8,128)(2,1)S(1)}, bf16[128,1536]{1,0:T(8,128)(2,1)S(1)}, u32[]{:S(2)}, u32[]{:S(2)}) collective-permute-start(bf16[128,1536]{1,0:T(8,128)(2,1)S(1)} %convolution_convert_fusion.1.after), channel_id=1, source_target_pairs={{0,6},{1,7},{2,0},{3,1},{4,2},{5,3},{6,4},{7,5},{8,14},{9,15},{10,... | collective-permute-start | bytes 1179656 | tf_op jit(solution)/shard_map/ppermute | solution.py:44
  52.1 27.0 %collective-permute-start.13 = (bf16[128,1536]{1,0:T(8,128)(2,1)}, bf16[128,1536]{1,0:T(8,128)(2,1)S(1)}, u32[]{:S(2)}, u32[]{:S(2)}) collective-permute-start(bf16[128,1536]{1,0:T(8,128)(2,1)} %copy-done), channel_id=1, source_target_pairs={{0,2},{1,3},{2,4},{3,5},{4,6},{5,7},{6,0},{7,1},{8,10},{9,11},{10,... | collective-permute-start | bytes 1179656 | tf_op jit(solution)/shard_map/ppermute | solution.py:44
  53.3 22.2 %collective-permute-start.11 = (bf16[128,1536]{1,0:T(8,128)(2,1)S(1)}, bf16[128,1536]{1,0:T(8,128)(2,1)S(1)}, u32[]{:S(2)}, u32[]{:S(2)}) collective-permute-start(bf16[128,1536]{1,0:T(8,128)(2,1)S(1)} %convolution_convert_fusion), channel_id=1, source_target_pairs={{0,2},{1,3},{2,4},{3,5},{4,6},{5,7},{6,0},{7,1},{8,10},{9,11},{10,... | collective-permute-start | bytes 1179656 | tf_op jit(solution)/shard_map/ppermute | solution.py:44
  60.6 20.1 %collective-permute-start.14 = (bf16[128,1536]{1,0:T(8,128)(2,1)S(1)}, bf16[128,1536]{1,0:T(8,128)(2,1)S(1)}, u32[]{:S(2)}, u32[]{:S(2)}) collective-permute-start(bf16[128,1536]{1,0:T(8,128)(2,1)S(1)} %convolution_convert_fusion), channel_id=1, source_target_pairs={{0,6},{1,7},{2,0},{3,1},{4,2},{5,3},{6,4},{7,5},{8,14},{9,15},{10,... | collective-permute-start | bytes 1179656 | tf_op jit(solution)/shard_map/ppermute | solution.py:44
  75.5 10.4 %collective-permute-start.12 = (bf16[128,1536]{1,0:T(8,128)(2,1)S(1)}, bf16[128,1536]{1,0:T(8,128)(2,1)S(1)}, u32[]{:S(2)}, u32[]{:S(2)}) collective-permute-start(bf16[128,1536]{1,0:T(8,128)(2,1)S(1)} %collective-permute-done.10), channel_id=1, source_target_pairs={{0,6},{1,7},{2,0},{3,1},{4,2},{5,3},{6,4},{7,5},{8,14},{9,15},{10,... | collective-permute-start | bytes 1179656 | tf_op jit(solution)/shard_map/ppermute | solution.py:44
  77.0 10.1 %collective-permute-start.15 = (bf16[128,1536]{1,0:T(8,128)(2,1)S(1)}, bf16[128,1536]{1,0:T(8,128)(2,1)S(1)}, u32[]{:S(2)}, u32[]{:S(2)}) collective-permute-start(bf16[128,1536]{1,0:T(8,128)(2,1)S(1)} %collective-permute-done.11), channel_id=1, source_target_pairs={{0,2},{1,3},{2,4},{3,5},{4,6},{5,7},{6,0},{7,1},{8,10},{9,11},{10,... | collective-permute-start | bytes 1179656 | tf_op jit(solution)/shard_map/ppermute | solution.py:44
  77.5 23.7 %collective-permute-start.7 = (s16[64,6272]{1,0:T(8,128)(2,1)}, s16[64,6272]{1,0:T(8,128)(2,1)S(1)}, u32[]{:S(2)}, u32[]{:S(2)}) collective-permute-start(s16[64,6272]{1,0:T(8,128)(2,1)} %get-tuple-element.27.after), channel_id=1, source_target_pairs={{0,8},{1,33},{2,10},{3,35},{4,12},{5,37},{6,14},{7,39},{8,16},{9,4... | collective-permute-start | bytes 2408456 | tf_op jit(solution)/shard_map/ppermute | solution.py:44
  79.1 23.8 %collective-permute-start.8 = (s16[64,6272]{1,0:T(8,128)(2,1)}, s16[64,6272]{1,0:T(8,128)(2,1)S(1)}, u32[]{:S(2)}, u32[]{:S(2)}) collective-permute-start(s16[64,6272]{1,0:T(8,128)(2,1)} %get-tuple-element.28), channel_id=1, source_target_pairs={{0,24},{1,97},{2,26},{3,99},{4,28},{5,101},{6,30},{7,103},{8,0},{9... | collective-permute-start | bytes 2408456 | tf_op jit(solution)/shard_map/ppermute | solution.py:44
  80.7 22.2 %collective-permute-start.9 = (s16[64,6272]{1,0:T(8,128)(2,1)}, s16[64,6272]{1,0:T(8,128)(2,1)}, u32[]{:S(2)}, u32[]{:S(2)}) collective-permute-start(s16[64,6272]{1,0:T(8,128)(2,1)} %get-tuple-element.29), channel_id=1, source_target_pairs={{0,16},{1,65},{2,18},{3,67},{4,20},{5,69},{6,22},{7,71},{8,24},{9,... | collective-permute-start | bytes 2408456 | tf_op jit(solution)/shard_map/ppermute | solution.py:44
  97.8 14.4 %collective-permute-start.16 = (s16[64,6272]{1,0:T(8,128)(2,1)}, s16[64,6272]{1,0:T(8,128)(2,1)S(1)}, u32[]{:S(2)}, u32[]{:S(2)}) collective-permute-start(s16[64,6272]{1,0:T(8,128)(2,1)} %get-tuple-element.40), channel_id=1, source_target_pairs={{0,8},{1,33},{2,10},{3,35},{4,12},{5,37},{6,14},{7,39},{8,16},{9,4... | collective-permute-start | bytes 2408456 | tf_op jit(solution)/shard_map/ppermute | solution.py:44
  99.4 25.0 %collective-permute-start.17 = (s16[64,6272]{1,0:T(8,128)(2,1)}, s16[64,6272]{1,0:T(8,128)(2,1)S(1)}, u32[]{:S(2)}, u32[]{:S(2)}) collective-permute-start(s16[64,6272]{1,0:T(8,128)(2,1)} %get-tuple-element.41), channel_id=1, source_target_pairs={{0,24},{1,97},{2,26},{3,99},{4,28},{5,101},{6,30},{7,103},{8,0},{9... | collective-permute-start | bytes 2408456 | tf_op jit(solution)/shard_map/ppermute | solution.py:44
  101.1 24.8 %collective-permute-start.18 = (s16[64,6272]{1,0:T(8,128)(2,1)}, s16[64,6272]{1,0:T(8,128)(2,1)}, u32[]{:S(2)}, u32[]{:S(2)}) collective-permute-start(s16[64,6272]{1,0:T(8,128)(2,1)} %get-tuple-element.42), channel_id=1, source_target_pairs={{0,16},{1,65},{2,18},{3,67},{4,20},{5,69},{6,22},{7,71},{8,24},{9,... | collective-permute-start | bytes 2408456 | tf_op jit(solution)/shard_map/ppermute | solution.py:44
  106.7 23.1 %all-to-all-start.2 = ((s16[16,16,1664]{2,1,0:T(8,128)(2,1)}), s16[16,16,1664]{2,1,0:T(8,128)(2,1)S(1)}, u32[]{:S(2)}, u32[]{:S(2)}) async-start(s16[16,16,1664]{2,1,0:T(8,128)(2,1)} %bitcast.22), calls=%async_computation.2 | async-start | bytes 1703936 | tf_op jit(solution)/shard_map/all_to_all | solution.py:416
  129.7 15.9 %all-to-all-start.3 = ((s16[16,16,1664]{2,1,0:T(8,128)(2,1)}), s16[16,16,1664]{2,1,0:T(8,128)(2,1)S(1)}, u32[]{:S(2)}, u32[]{:S(2)}) async-start(s16[16,16,1664]{2,1,0:T(8,128)(2,1)} %bitcast.24), calls=%async_computation.3 | async-start | bytes 1703936 | tf_op jit(solution)/shard_map/all_to_all | solution.py:416
  (9 other events, 87.4 us)
